TPU v7x, 32 devices: a whole 2x2x4 slice. The times are simulated.
32 devices in a mesh: space: 16 (over z, y, core), traj: 2 (over x).
Axes of the slice: x: 2, y: 2, z: 4, core: 2. Of those that a mesh axis runs over, the one named last changes fastest.
Arguments:
- field: float32 [2, 39, 128, 256], P('traj', None, 'space'), may hold values from -6 to 6
- solid: int32 [2, 128, 256], P('traj', 'space'), may hold values 0 or 1
- cotangent: float32 [2, 39, 128, 256], P('traj', None, 'space'), may hold values from -6 to 6
- w_in: bfloat16 [20, 512], replicated, may hold values from -1.25 to 1.25
- b_in: float32 [512], replicated, may hold values from -3 to 3
- w_out: bfloat16 [512, 39], replicated, may hold values from -0.25 to 0.25
- b_out: float32 [39], replicated, may hold values from -3 to 3
Outputs:
- d_field: float32 [2, 39, 128, 256], P('traj', None, 'space')
- g_w_in: float32 [20, 512], replicated
- g_b_in: float32 [512], replicated
- g_w_out: float32 [512, 39], replicated
- g_b_out: float32 [39], replicated
All inputs are finite; a program needn't handle non-finite values. No bound on the sum of `solid` on one device may be relied on, other than what follows from the above.
Results may differ from a plain program's by a relative error of at most 0.0089.
Values sent between devices are 32-bit elements; how exact they have to be, the bound alone decides.
No kernel may reach another device: no remote copies, remote signals or barrier semaphores. Data moves between devices by JAX's collectives and lax.ppermute only.
A program may use at most 64 MiB of HBM per device.

v0:
```python
import math

import jax
import jax.numpy as jnp
from jax import lax
from jax.sharding import PartitionSpec as P

STEPS = 3
NX = 16
NY = 16


def padded_2(shard, sides, width):
    for axis, dim in sides:
        size, length = (lax.axis_size(axis), shard.shape[dim])
        up = [(i, (i + 1) % size) for i in range(size)]
        down = [(j, i) for i, j in up]
        last = lax.slice_in_dim(shard, length - width, length, axis=dim)
        first = lax.slice_in_dim(shard, 0, width, axis=dim)
        before = lax.ppermute(last, axis, up)
        after = lax.ppermute(first, axis, down)
        shard = jnp.concatenate([before, shard, after], axis=dim)
    return shard


def velocity_table():
    rows = [(0, 0, 0)]
    for axis_one in range(3):
        for sign in (1, -1):
            entry = [0, 0, 0]
            entry[axis_one] = sign
            rows.append(tuple(entry))
    for along_x in (1, -1):
        for along_y in (1, -1):
            for along_z in (1, -1):
                rows.append((along_x, along_y, along_z))
    for axis_one in range(3):
        for sign in (1, -1):
            entry = [0, 0, 0]
            entry[axis_one] = 2 * sign
            rows.append(tuple(entry))
    for first, second in ((0, 1), (0, 2), (1, 2)):
        for sign_one in (2, -2):
            for sign_two in (2, -2):
                entry = [0, 0, 0]
                entry[first] = sign_one
                entry[second] = sign_two
                rows.append(tuple(entry))
    for axis_one in range(3):
        for sign in (1, -1):
            entry = [0, 0, 0]
            entry[axis_one] = 3 * sign
            rows.append(tuple(entry))
    return rows


def opposite_index(velocity):
    result = []
    for row in velocity:
        flipped = (-row[0], -row[1], -row[2])
        result.append(velocity.index(flipped))
    return result


def hermite_table(velocity):
    sound = 2.0 / 3.0
    ident = [[1.0 if a == b else 0.0 for b in range(3)] for a in range(3)]
    speed = [[float(v) for v in row] for row in velocity]
    rows = [[1.0 for row in speed]]
    for first in range(3):
        rows.append([row[first] for row in speed])
    for first in range(3):
        for second in range(first, 3):
            rows.append([row[first] * row[second] - sound * ident[first][second] for row in speed])
    for first in range(3):
        for second in range(first, 3):
            for third in range(second, 3):
                rows.append(
                    [
                        row[first] * row[second] * row[third]
                        - sound
                        * (
                            row[first] * ident[second][third]
                            + row[second] * ident[first][third]
                            + row[third] * ident[first][second]
                        )
                        for row in speed
                    ]
                )
    normed = []
    for values in rows:
        length = math.sqrt(sum((v * v for v in values)))
        normed.append([v / length for v in values])
    return jnp.asarray(normed, jnp.float32)


def collide_block(block, weights, hermite):
    w_in, b_in, w_out, b_out = weights
    moments = jnp.dot(
        hermite, block, precision=lax.Precision.HIGHEST, preferred_element_type=jnp.float32
    )
    rounded = moments.astype(jnp.bfloat16)
    hidden = jnp.tanh(
        jnp.dot(w_in.T, rounded, preferred_element_type=jnp.float32) + b_in[:, None]
    ).astype(jnp.bfloat16)
    change = jnp.dot(w_out.T, hidden, preferred_element_type=jnp.float32) + b_out[:, None]
    return (block + change, rounded, hidden)


def adjoint_block(block, incoming, weights, hermite):
    w_in, b_in, w_out, b_out = weights
    unused, rounded, hidden = collide_block(block, weights, hermite)
    grad_rounded = incoming.astype(jnp.bfloat16)
    d_hidden = jnp.dot(w_out, grad_rounded, preferred_element_type=jnp.float32)
    hidden_wide = hidden.astype(jnp.float32)
    d_act = (d_hidden * (1.0 - hidden_wide * hidden_wide)).astype(jnp.bfloat16)
    d_moments = jnp.dot(w_in, d_act, preferred_element_type=jnp.float32)
    d_block = incoming + jnp.dot(
        hermite.T, d_moments, precision=lax.Precision.HIGHEST, preferred_element_type=jnp.float32
    )
    grads = (
        jnp.dot(rounded, d_act.T, preferred_element_type=jnp.float32),
        jnp.sum(d_act.astype(jnp.float32), axis=1),
        jnp.dot(hidden, grad_rounded.T, preferred_element_type=jnp.float32),
        jnp.sum(incoming, axis=1),
    )
    return (d_block, grads)


def collide_layers(state, weights, hermite):
    layers = jnp.moveaxis(state, 1, 0)
    result = lax.map(lambda layer: collide_block(layer, weights, hermite)[0], layers)
    return jnp.moveaxis(result, 0, 1)


def adjoint_layers(state, incoming, weights, hermite):
    zeros = tuple((jnp.zeros(w.shape, jnp.float32) for w in weights))

    def advance(totals, pair):
        d_layer, grads = adjoint_block(pair[0], pair[1], weights, hermite)
        return (tuple((a + b for a, b in zip(totals, grads))), d_layer)

    totals, layers = lax.scan(
        advance, zeros, (jnp.moveaxis(state, 1, 0), jnp.moveaxis(incoming, 1, 0))
    )
    return (jnp.moveaxis(layers, 0, 1), totals)


def roll_plane(rows, along_x, along_y):
    depth = rows.shape[0]
    grid = rows.reshape(depth, NX, NY)
    return jnp.roll(grid, (along_x, along_y), (1, 2)).reshape(depth, NX * NY)


def stream_local(state, velocity, sign):
    depth = state.shape[1]
    count = len(velocity)
    moves = [-sign * velocity[index][2] for index in range(count)]
    pieces = []
    padded = padded_2(state, (("space", 1),), 3)
    for index in range(count):
        pieces.append(padded[index, 3 + moves[index] : 3 + moves[index] + depth])
    moved = []
    for index in range(count):
        moved.append(
            roll_plane(pieces[index], sign * velocity[index][0], sign * velocity[index][1])
        )
    return jnp.stack(moved)


def per_device(field, solid, cotangent, w_in, b_in, w_out, b_out):
    velocity = velocity_table()
    opposite = jnp.asarray(opposite_index(velocity), jnp.int32)
    hermite = hermite_table(velocity)
    weights = (w_in, b_in, w_out, b_out)
    local_count, pops, depth, plane = field.shape
    walls = [solid[0].astype(jnp.float32)[None]]
    current = [field[0]]
    states = [[]]
    for step in range(STEPS):
        t = 0
        states[t].append(current[t])
        post = collide_layers(current[t], weights, hermite)
        current[t] = (1.0 - walls[t]) * stream_local(post, velocity, 1) + walls[t] * post[opposite]
    totals = tuple((jnp.zeros(w.shape, jnp.float32) for w in weights))
    backs = [cotangent[0]]
    for step in range(STEPS - 1, -1, -1):
        local_sums = tuple((jnp.zeros(w.shape, jnp.float32) for w in weights))
        t = 0
        incoming = (
            stream_local((1.0 - walls[t]) * backs[t], velocity, -1)
            + (walls[t] * backs[t])[opposite]
        )
        backs[t], grads = adjoint_layers(states[t][step], incoming, weights, hermite)
        local_sums = tuple((b for b in grads))
        totals = tuple((a + b for a, b in zip(totals, local_sums)))
    totals = lax.psum((totals[0], totals[1], totals[2], totals[3]), ("space", "traj"))
    cells = lax.axis_size("traj") * local_count * lax.axis_size("space") * depth * plane * STEPS
    scale = 1.0 / math.sqrt(float(cells))
    return (
        jnp.stack(backs),
        totals[0] * scale,
        totals[1] * scale,
        totals[2] * scale,
        totals[3] * scale,
    )


def solution(mesh):
    return jax.shard_map(
        per_device,
        mesh=mesh,
        in_specs=(
            P("traj", None, "space", None),
            P("traj", "space", None),
            P("traj", None, "space", None),
            P(),
            P(),
            P(),
            P(),
        ),
        out_specs=(P("traj", None, "space", None), P(), P(), P(), P()),
        check_vma=False,
    )
```

profile of v0, /device:TPU:0, one launch (start us, length us, event | category | flops | bytes accessed | tf_op | source)
XLA Modules:
  0.0 367.0 jit_solution(8561936471670774594)
XLA Ops:
  7.2 1.1 copy.78
  8.4 0.6 copy-done
  9.1 20.9 %while.82 = (s32[]{:T(128)}, f32[8,39,256]{2,0,1:T(8,128)S(1)}, f32[8,39,256]{2,1,0:T(8,128)S(1)}, bf16[20,512]{1,0:T(8,128)(2,1)S(1)}, f32[512]{0:T(512)S(1)}, ...) while((s32[]{:T(128)}, f32[8,39,256]{2,0,1:T(8,128)S(1)}, ...), condition=%wide.region_1.2_spmd.clone, body=%wide.region_0.1_spmd.sunk.clone.sunk | while | flops 18149888 | bytes 376077 | solution.py:132
  9.9 1.8 dynamic_update_slice.34
  12.5 1.8 dynamic_update_slice.34
  15.1 1.8 dynamic_update_slice.34
  17.8 1.8 dynamic_update_slice.34
  20.4 1.8 dynamic_update_slice.34
  23.0 1.8 dynamic_update_slice.34
  25.6 1.8 dynamic_update_slice.34
  28.2 1.8 dynamic_update_slice.34
  30.5 5.1 %collective-permute-start.1 = (f32[39,3,256]{2,1,0:T(4,128)S(1)}, f32[39,3,256]{2,1,0:T(4,128)S(1)}, u32[]{:S(2)}, u32[]{:S(2)}) collective-permute-start(f32[39,3,256]{2,1,0:T(4,128)S(1)} %get-tuple-element.912), channel_id=1, source_target_pairs={{2,0},{4,2},{6,4},{8,6},{10,8},{12,10},{14,12},{16,14},{18,16},{20... | collective-permute-start | bytes 359432 | tf_op jit(solution)/shard_map/ppermute | solution.py:21
  35.7 0.7 copy-done.4
  37.5 0.6 copy-done.5
  48.8 20.9 %while.83 = (s32[]{:T(128)}, f32[8,39,256]{2,0,1:T(8,128)S(1)}, f32[8,39,256]{2,1,0:T(8,128)S(1)}, bf16[20,512]{1,0:T(8,128)(2,1)S(1)}, f32[512]{0:T(512)S(1)}, ...) while((s32[]{:T(128)}, f32[8,39,256]{2,0,1:T(8,128)S(1)}, ...), condition=%wide.region_3.4_spmd.clone, body=%wide.region_2.3_spmd.sunk.clone.sunk | while | flops 18149888 | bytes 376077 | solution.py:132
  49.6 1.8 dynamic_update_slice.35
  52.3 1.8 dynamic_update_slice.35
  54.9 1.8 dynamic_update_slice.35
  57.5 1.8 dynamic_update_slice.35
  60.1 1.8 dynamic_update_slice.35
  62.7 1.8 dynamic_update_slice.35
  65.3 1.8 dynamic_update_slice.35
  67.9 1.8 dynamic_update_slice.35
  71.5 3.9 %collective-permute-start.3 = (f32[39,3,256]{2,1,0:T(4,128)S(1)}, f32[39,3,256]{2,1,0:T(4,128)S(1)}, u32[]{:S(2)}, u32[]{:S(2)}) collective-permute-start(f32[39,3,256]{2,1,0:T(4,128)S(1)} %get-tuple-element.893), channel_id=1, source_target_pairs={{2,0},{4,2},{6,4},{8,6},{10,8},{12,10},{14,12},{16,14},{18,16},{20... | collective-permute-start | bytes 359432 | tf_op jit(solution)/shard_map/ppermute | solution.py:21
  76.0 2.3 collective-permute-done.2
  88.1 0.9 copy-done.3
  90.4 4.5 %collective-permute-start.4 = (f32[39,3,256]{2,1,0:T(4,128)S(1)}, f32[39,3,256]{2,1,0:T(4,128)S(1)}, u32[]{:S(2)}, u32[]{:S(2)}) collective-permute-start(f32[39,3,256]{2,1,0:T(4,128)S(1)} %get-tuple-element.875), channel_id=1, source_target_pairs={{2,0},{4,2},{6,4},{8,6},{10,8},{12,10},{14,12},{16,14},{18,16},{20... | collective-permute-start | bytes 359432 | tf_op jit(solution)/shard_map/ppermute | solution.py:21
  95.5 2.2 collective-permute-done.4
  97.7 4.6 %collective-permute-done.5 = f32[39,3,256]{2,1,0:T(4,128)S(1)} collective-permute-done((f32[39,3,256]{2,1,0:T(4,128)S(1)}, f32[39,3,256]{2,1,0:T(4,128)S(1)}, u32[]{:S(2)}, u32[]{:S(2)}) %collective-permute-start.5) | collective-permute-done | bytes 119840 | tf_op jit(solution)/shard_map/ppermute | solution.py:20
  112.1 30.4 %while.84 = (s32[]{:T(128)}, f32[20,512]{1,0:T(8,128)S(1)}, f32[512]{0:T(512)S(1)}, f32[512,39]{0,1:T(8,128)S(1)}, f32[39]{0:T(128)S(1)}, /*index=5*/f32[8,39,25...) while((s32[]{:T(128)}, f32[20,512]{1,0:T(8,128)S(1)}, ...), condition=%wide.region_7.8_spmd.clone.clone, body=%wide.region_4.7_spmd.sunk.clone.clone.sunk | while | flops 42233896 | bytes 2503530 | solution.py:143
  113.7 1.8 dynamic_update_slice.36
  117.5 1.8 dynamic_update_slice.36
  121.3 1.8 dynamic_update_slice.36
  125.1 1.8 dynamic_update_slice.36
  128.9 1.8 dynamic_update_slice.36
  132.7 1.8 dynamic_update_slice.36
  136.5 1.8 dynamic_update_slice.36
  140.3 1.8 dynamic_update_slice.36
  144.9 1.7 collective-permute-done.6
  146.6 4.8 %collective-permute-done.7 = f32[39,3,256]{2,1,0:T(4,128)S(1)} collective-permute-done((f32[39,3,256]{2,1,0:T(4,128)S(1)}, f32[39,3,256]{2,1,0:T(4,128)S(1)}, u32[]{:S(2)}, u32[]{:S(2)}) %collective-permute-start.7) | collective-permute-done | bytes 119840 | tf_op jit(solution)/shard_map/ppermute | solution.py:20
  161.3 30.4 %while.85 = (s32[]{:T(128)}, f32[20,512]{1,0:T(8,128)S(1)}, f32[512]{0:T(512)S(1)}, f32[512,39]{0,1:T(8,128)S(1)}, f32[39]{0:T(128)S(1)}, /*index=5*/f32[8,39,25...) while((s32[]{:T(128)}, f32[20,512]{1,0:T(8,128)S(1)}, ...), condition=%wide.region_11.12_spmd.clone.clone, body=%wide.region_8.11_spmd.sunk.clone.clone.sunk | while | flops 42233896 | bytes 2433854 | solution.py:143
  162.9 1.8 dynamic_update_slice.37
  166.7 1.8 dynamic_update_slice.37
  170.5 1.8 dynamic_update_slice.37
  174.3 1.8 dynamic_update_slice.37
  178.1 1.8 dynamic_update_slice.37
  181.9 1.8 dynamic_update_slice.37
  185.7 1.8 dynamic_update_slice.37
  189.5 1.8 dynamic_update_slice.37
  194.1 1.7 collective-permute-done.8
  195.8 4.6 %collective-permute-done.9 = f32[39,3,256]{2,1,0:T(4,128)S(1)} collective-permute-done((f32[39,3,256]{2,1,0:T(4,128)S(1)}, f32[39,3,256]{2,1,0:T(4,128)S(1)}, u32[]{:S(2)}, u32[]{:S(2)}) %collective-permute-start.9) | collective-permute-done | bytes 119840 | tf_op jit(solution)/shard_map/ppermute | solution.py:20
  210.2 30.4 %while.86 = (s32[]{:T(128)}, f32[20,512]{1,0:T(8,128)S(1)}, f32[512]{0:T(512)S(1)}, f32[512,39]{0,1:T(8,128)S(1)}, f32[39]{0:T(128)S(1)}, /*index=5*/f32[8,39,25...) while((s32[]{:T(128)}, f32[20,512]{1,0:T(8,128)S(1)}, ...), condition=%wide.region_15.16_spmd.clone.clone, body=%wide.region_12.15_spmd.sunk.clone.clone.sunk | while | flops 42233896 | bytes 2433854 | solution.py:143
  211.9 1.8 dynamic_update_slice.38
  215.7 1.8 dynamic_update_slice.38
  219.5 1.8 dynamic_update_slice.38
  223.3 1.8 dynamic_update_slice.38
  227.1 1.8 dynamic_update_slice.38
  230.9 1.8 dynamic_update_slice.38
  234.7 1.8 dynamic_update_slice.38
  238.5 1.8 dynamic_update_slice.38
  240.7 0.7 add_add_fusion
  241.5 37.4 %all-reduce = (f32[20,512]{1,0:T(8,128)S(1)}, f32[512]{0:T(512)S(1)}, f32[39]{0:T(128)S(1)}) all-reduce(f32[20,512]{1,0:T(8,128)S(1)} %add_add_fusion.1, f32[512]{0:T(512)S(1)} %add_add_fusion.2, f32[39]{0:T(128)S(1)} %add_add_fusion.3), channel_id=1, replica_groups=mesh['space'=16,'traj'=2] {'space','traj'}, use_global_device_ids=true, to_apply=%region_16.17 | all-reduce | flops 10791 | bytes 86328 | tf_op jit(solution)/shard_map/psum | solution.py:197
  280.6 78.1 %all-reduce.3.cloned.1.call-done = f32[512,39]{0,1:T(8,128)} async-done(((f32[512,39]{0,1:T(8,128)}), f32[512,39]{0,1:T(8,128)}) %all-reduce.3.cloned.1.call-update) | async-done | bytes 79888 | tf_op jit(solution)/shard_map/psum | solution.py:197
  358.7 1.5 broadcast_multiply_fusion
  (1332 shorter events, 115.6 us)
Async XLA Ops:
  7.2 351.5 %all-reduce.3.cloned.1.call-start = ((), (), s32[]{:S(2)}) async-start(), calls=%async_computation | async-start | bytes 163840 | tf_op jit(solution)/shard_map/psum | solution.py:197
  8.3 0.7 copy-start
  8.3 0.7 copy-start.1
  8.3 0.8 copy-start.6
  8.3 0.8 copy-start.7
  8.3 0.8 copy-start.8
  30.0 8.8 %collective-permute-start = (f32[39,3,256]{2,1,0:T(4,128)S(1)}, f32[39,3,256]{2,1,0:T(4,128)S(1)}, u32[]{:S(2)}, u32[]{:S(2)}) collective-permute-start(f32[39,3,256]{2,1,0:T(4,128)S(1)} %get-tuple-element.913), channel_id=1, source_target_pairs={{0,2},{2,4},{4,6},{6,8},{8,10},{10,12},{12,14},{14,16},{16,18},{18... | collective-permute-start | bytes 359432 | tf_op jit(solution)/shard_map/ppermute | solution.py:20
  30.5 8.5 %collective-permute-start.1 = (f32[39,3,256]{2,1,0:T(4,128)S(1)}, f32[39,3,256]{2,1,0:T(4,128)S(1)}, u32[]{:S(2)}, u32[]{:S(2)}) collective-permute-start(f32[39,3,256]{2,1,0:T(4,128)S(1)} %get-tuple-element.912), channel_id=1, source_target_pairs={{2,0},{4,2},{6,4},{8,6},{10,8},{12,10},{14,12},{16,14},{18,16},{20... | collective-permute-start | bytes 359432 | tf_op jit(solution)/shard_map/ppermute | solution.py:21
  35.7 0.7 copy-start.4
  37.5 0.7 copy-start.5
  70.9 7.5 %collective-permute-start.2 = (f32[39,3,256]{2,1,0:T(4,128)S(1)}, f32[39,3,256]{2,1,0:T(4,128)S(1)}, u32[]{:S(2)}, u32[]{:S(2)}) collective-permute-start(f32[39,3,256]{2,1,0:T(4,128)S(1)} %get-tuple-element.894), channel_id=1, source_target_pairs={{0,2},{2,4},{4,6},{6,8},{8,10},{10,12},{12,14},{14,16},{16,18},{18... | collective-permute-start | bytes 359432 | tf_op jit(solution)/shard_map/ppermute | solution.py:20
  71.5 6.9 %collective-permute-start.3 = (f32[39,3,256]{2,1,0:T(4,128)S(1)}, f32[39,3,256]{2,1,0:T(4,128)S(1)}, u32[]{:S(2)}, u32[]{:S(2)}) collective-permute-start(f32[39,3,256]{2,1,0:T(4,128)S(1)} %get-tuple-element.893), channel_id=1, source_target_pairs={{2,0},{4,2},{6,4},{8,6},{10,8},{12,10},{14,12},{16,14},{18,16},{20... | collective-permute-start | bytes 359432 | tf_op jit(solution)/shard_map/ppermute | solution.py:21
  88.1 1.0 copy-start.3
  90.4 7.2 %collective-permute-start.4 = (f32[39,3,256]{2,1,0:T(4,128)S(1)}, f32[39,3,256]{2,1,0:T(4,128)S(1)}, u32[]{:S(2)}, u32[]{:S(2)}) collective-permute-start(f32[39,3,256]{2,1,0:T(4,128)S(1)} %get-tuple-element.875), channel_id=1, source_target_pairs={{2,0},{4,2},{6,4},{8,6},{10,8},{12,10},{14,12},{16,14},{18,16},{20... | collective-permute-start | bytes 359432 | tf_op jit(solution)/shard_map/ppermute | solution.py:21
  94.9 7.4 %collective-permute-start.5 = (f32[39,3,256]{2,1,0:T(4,128)S(1)}, f32[39,3,256]{2,1,0:T(4,128)S(1)}, u32[]{:S(2)}, u32[]{:S(2)}) collective-permute-start(f32[39,3,256]{2,1,0:T(4,128)S(1)} %get-tuple-element.874), channel_id=1, source_target_pairs={{0,2},{2,4},{4,6},{6,8},{8,10},{10,12},{12,14},{14,16},{16,18},{18... | collective-permute-start | bytes 359432 | tf_op jit(solution)/shard_map/ppermute | solution.py:20
  143.7 2.9 collective-permute-start.6
  143.8 7.6 %collective-permute-start.7 = (f32[39,3,256]{2,1,0:T(4,128)S(1)}, f32[39,3,256]{2,1,0:T(4,128)S(1)}, u32[]{:S(2)}, u32[]{:S(2)}) collective-permute-start(f32[39,3,256]{2,1,0:T(4,128)S(1)} %get-tuple-element.853), channel_id=1, source_target_pairs={{0,2},{2,4},{4,6},{6,8},{8,10},{10,12},{12,14},{14,16},{16,18},{18... | collective-permute-start | bytes 359432 | tf_op jit(solution)/shard_map/ppermute | solution.py:20
  192.9 2.9 collective-permute-start.8
  193.0 7.4 %collective-permute-start.9 = (f32[39,3,256]{2,1,0:T(4,128)S(1)}, f32[39,3,256]{2,1,0:T(4,128)S(1)}, u32[]{:S(2)}, u32[]{:S(2)}) collective-permute-start(f32[39,3,256]{2,1,0:T(4,128)S(1)} %get-tuple-element.832), channel_id=1, source_target_pairs={{0,2},{2,4},{4,6},{6,8},{8,10},{10,12},{12,14},{14,16},{16,18},{18... | collective-permute-start | bytes 359432 | tf_op jit(solution)/shard_map/ppermute | solution.py:20
  240.6 0.8 copy-start.2
Sparse Core Ops, SparseCore 0:
  241.5 117.1 all-reduce.2
where the time goes:
time: 369 us; the launch traced here: 367 us
  local copies, waits for them, and re-layouts  112 us (30%)
  waiting for transfers between devices  100 us (27%)
  matrix products  47.5 us (13%)
  blocking collectives  37.4 us (10%)
  other arithmetic  31.2 us (8%)
  between operations  20.6 us (6%)
  starting transfers between devices  15.7 us (4%)
    psum x1, waiting for transfers between devices, per_device(): lax.psum((totals[0], totals[1], totals[2], totals[3]), ('space', 'traj'))  78.1 us
    dynamic_update_slice x80, local copies, waits for them, and re-layouts, collide_layers(): lax.map(lambda layer: collide_block(layer, weights, hermite)[0], layers)  72.8 us
    psum x1, blocking collectives, per_device(): lax.psum((totals[0], totals[1], totals[2], totals[3]), ('space', 'traj'))  37.4 us
    concatenate x220, other arithmetic, roll_plane(): return jnp.roll(grid, (along_x, along_y), (1, 2)).reshape(depth, NX * NY)  16.6 us
    ppermute x5, waiting for transfers between devices, padded_2(): before = lax.ppermute(last, axis, up)  16.4 us
    another operation x160, local copies, waits for them, and re-layouts, stream_local(): return jnp.stack(moved)  14 us
    ppermute x5, starting transfers between devices, padded_2(): after = lax.ppermute(first, axis, down)  13.5 us
    another operation x160, local copies, waits for them, and re-layouts, roll_plane(): grid = rows.reshape(depth, NX, NY)  12.1 us
  transfers between devices with their start and end apart: 11, of which 8 were waited for; matrix products, arithmetic and copies ran while one was open for 2% of the time, Pallas kernels for 0%

commit v1 on v0

v1 whole, which is shorter than its diff:
```python
import math

import jax
import jax.numpy as jnp
import numpy as np
from jax import lax
from jax.experimental import pallas as pl
from jax.experimental.pallas import tpu as pltpu
from jax.sharding import PartitionSpec as P

STEPS = 3
NX = 16
NY = 16
Q = 39
QP = 48
MOM = 20
MP = 32
REACH = 3
BLOCK = 40
CHUNK = 128
BF = jnp.bfloat16
F32 = jnp.float32


def velocity_table():
    rows = [(0, 0, 0)]
    for axis_one in range(3):
        for sign in (1, -1):
            entry = [0, 0, 0]
            entry[axis_one] = sign
            rows.append(tuple(entry))
    for along_x in (1, -1):
        for along_y in (1, -1):
            for along_z in (1, -1):
                rows.append((along_x, along_y, along_z))
    for axis_one in range(3):
        for sign in (1, -1):
            entry = [0, 0, 0]
            entry[axis_one] = 2 * sign
            rows.append(tuple(entry))
    for first, second in ((0, 1), (0, 2), (1, 2)):
        for sign_one in (2, -2):
            for sign_two in (2, -2):
                entry = [0, 0, 0]
                entry[first] = sign_one
                entry[second] = sign_two
                rows.append(tuple(entry))
    for axis_one in range(3):
        for sign in (1, -1):
            entry = [0, 0, 0]
            entry[axis_one] = 3 * sign
            rows.append(tuple(entry))
    return rows


def opposite_index(velocity):
    return [velocity.index((-row[0], -row[1], -row[2])) for row in velocity]


def hermite_table(velocity):
    sound = 2.0 / 3.0
    ident = [[1.0 if a == b else 0.0 for b in range(3)] for a in range(3)]
    speed = [[float(v) for v in row] for row in velocity]
    rows = [[1.0 for row in speed]]
    for first in range(3):
        rows.append([row[first] for row in speed])
    for first in range(3):
        for second in range(first, 3):
            rows.append([row[first] * row[second] - sound * ident[first][second] for row in speed])
    for first in range(3):
        for second in range(first, 3):
            for third in range(second, 3):
                rows.append(
                    [
                        row[first] * row[second] * row[third]
                        - sound
                        * (
                            row[first] * ident[second][third]
                            + row[second] * ident[first][third]
                            + row[third] * ident[first][second]
                        )
                        for row in speed
                    ]
                )
    normed = []
    for values in rows:
        length = math.sqrt(sum((v * v for v in values)))
        normed.append([v / length for v in values])
    return np.asarray(normed, np.float32)


VEL = velocity_table()
OPP = opposite_index(VEL)
HERM = hermite_table(VEL)


def reaching(sign):
    return [(k, q) for k in range(1, REACH + 1) for q in range(Q) if sign * VEL[q][2] >= k]


N_REACH = len(reaching(1))
SEND_ONE = REACH * BLOCK + 2 * N_REACH + REACH + 1
SEND_TWO = REACH * BLOCK + N_REACH + 6


def split_hi_lo(table):
    hi = table.astype(BF)
    lo = (table - np.asarray(hi, np.float32)).astype(BF)
    return hi, lo


def hermite_operands():
    wide = np.zeros((MP, QP), np.float32)
    wide[:MOM, :Q] = HERM
    hi, lo = split_hi_lo(wide)
    forward = np.concatenate([hi, hi, lo], axis=1)
    hi, lo = split_hi_lo(np.ascontiguousarray(wide.T))
    backward = np.concatenate([hi, hi, lo], axis=1)
    return jnp.asarray(forward), jnp.asarray(backward)


def dot(a, b):
    return jnp.dot(a, b, preferred_element_type=F32)


def dot_nt(a, b, precision=None):
    return lax.dot_general(
        a, b, (((1,), (1,)), ((), ())), preferred_element_type=F32, precision=precision
    )


def halves(value):
    lanes = value.shape[1] // 2
    return value[:, :lanes], value[:, lanes:]


def get_layer(buf, layer, stride, count=QP):
    return jnp.concatenate([buf[half, pl.ds(layer, count, stride=stride), :] for half in (0, 1)], axis=1)


def put_layer(buf, layer, stride, value):
    count = value.shape[0]
    for half, part in enumerate(halves(value)):
        buf[half, pl.ds(layer, count, stride=stride), :] = part


def get_rows(buf, q, stride, first, count):
    start = q * stride + first
    return jnp.concatenate([buf[half, start : start + count, :] for half in (0, 1)], axis=1)


def put_rows(buf, q, stride, first, value):
    start = q * stride + first
    for half, part in enumerate(halves(value)):
        buf[half, start : start + value.shape[0], :] = part


def clear_pad(buf, stride):
    lanes = buf.shape[2]
    for half in (0, 1):
        buf[half, Q * stride : QP * stride, :] = jnp.zeros(((QP - Q) * stride, lanes), F32)


def roll_plane(value, along_x, along_y):
    lanes = value.shape[1]
    shift = NY * along_x + along_y

    def turned(by):
        by = by % lanes
        return value if by == 0 else pltpu.roll(value, by, 1)

    if along_y == 0:
        return turned(shift)
    column = lax.broadcasted_iota(jnp.int32, value.shape, 1) % NY
    if along_y > 0:
        return jnp.where(column < along_y, turned(shift - NY), turned(shift))
    return jnp.where(column >= NY + along_y, turned(shift + NY), turned(shift))


def split_concat(value):
    hi = value.astype(BF)
    lo = (value - hi.astype(F32)).astype(BF)
    return jnp.concatenate([hi, lo, hi], axis=0)


def moments_of(x, herm):
    moments = dot(herm, split_concat(x))
    row = lax.broadcasted_iota(jnp.int32, moments.shape, 0)
    ones = jnp.where((row >= MOM) & (row < MOM + 3), 1.0, 0.0)
    return (moments + ones).astype(BF)


def hidden_into(h_ref, lanes, w1, mb):
    for start in range(0, w1.shape[0], CHUNK):
        act = dot(w1[start : start + CHUNK, :], mb)
        h_ref[start : start + CHUNK, lanes] = jnp.tanh(act).astype(BF)


def adjoint_layer(gp, gb, h_ref, h_lanes, da_ref, da_lanes, w_out, w_in, herm_t):
    for start in range(0, w_out.shape[0], CHUNK):
        d_hidden = dot(w_out[start : start + CHUNK, :], gb)
        hidden = h_ref[start : start + CHUNK, h_lanes].astype(F32)
        da_ref[start : start + CHUNK, da_lanes] = (d_hidden * (1.0 - hidden * hidden)).astype(BF)
    d_moments = dot(w_in[...], da_ref[:, da_lanes])
    return gp + dot(herm_t, split_concat(d_moments))


def first_kernel(
    field, cot, solid, w_in, b_in, w_out, b_out, herm,
    send_up, send_dn, post, h0, mb0, w1_o, w_in_o, w2_o, w_out_o, b_col_o,
    state, wide, tall,
):
    depth, plane = solid.shape
    hid = w_in.shape[1]
    wide[...] = jnp.zeros(wide.shape, F32)
    wide[:MOM, :] = w_in[...].astype(F32)
    w_in_o[...] = wide[...].astype(BF)
    rest = b_in[...]
    for part in range(3):
        piece = rest.astype(BF).astype(F32)
        wide[MOM + part : MOM + part + 1, :] = piece
        rest = rest - piece
    w1_o[...] = wide[...].T.astype(BF)
    tall[...] = jnp.zeros(tall.shape, F32)
    tall[:Q, :] = w_out[...].astype(F32).T
    w2_o[...] = tall[...].astype(BF)
    w_out_o[...] = tall[...].T.astype(BF)
    tall[0:8, :] = jnp.zeros((8, hid), F32)
    tall[0:1, 0:Q] = b_out[...]
    column = tall[0:8, 0:128].T
    b_col_o[...] = jnp.broadcast_to(column[:QP, 0:1], (QP, plane))

    for q in range(Q):
        put_rows(state, q, depth, 0, field[q * depth : (q + 1) * depth, :])
    clear_pad(state, depth)
    for z in range(depth):
        lanes = slice(z * plane, (z + 1) * plane)
        x = get_layer(state, z, depth)
        mb = moments_of(x, herm[...])
        mb0[:, lanes] = mb
        hidden_into(h0, lanes, w1_o, mb)
        out = x + dot(w2_o[...], h0[:, lanes]) + b_col_o[...]
        put_layer(post, z, depth, out[:Q])
        if z < REACH:
            send_dn[z * BLOCK : z * BLOCK + Q, :] = out[:Q]
        if depth - 1 - z < REACH:
            d = depth - 1 - z
            send_up[d * BLOCK : d * BLOCK + Q, :] = out[:Q]

    wall = solid[...].astype(F32)
    for sign, send in ((1, send_up), (-1, send_dn)):
        layer = (lambda d: depth - d) if sign > 0 else (lambda d: d - 1)
        row = REACH * BLOCK
        for k, q in reaching(sign):
            send[row : row + 1, :] = get_rows(post, q, depth, layer(REACH + k), 1)
            row += 1
        for k, q in reaching(-sign):
            z = layer(k)
            at = q * depth + z
            send[row : row + 1, :] = cot[at : at + 1, :] * (1.0 - wall[z : z + 1, :])
            row += 1
        for d in range(1, REACH + 1):
            send[row : row + 1, :] = wall[layer(d) : layer(d) + 1, :]
            row += 1


def second_kernel(
    post, below, above, cot, solid, w1, w_in, w2, w_out, b_col, herm, herm_t,
    send_up, send_dn, g2, wall_o, h1, mb1, h2, mb2, da2, gb2, gsum,
    p0, s1, p1, s2, gx, gp2,
):
    depth, plane = solid.shape
    edge = REACH + 1
    mid = depth + 2 * edge
    ext = depth + 16
    wall_o[...] = jnp.zeros(wall_o.shape, F32)
    wall_o[edge : edge + depth, :] = solid[...].astype(F32)
    row = REACH * BLOCK + 2 * N_REACH
    for d in range(1, REACH + 1):
        wall_o[edge - d : edge - d + 1, :] = below[row + d - 1 : row + d, :]
        wall_o[edge + depth + d - 1 : edge + depth + d, :] = above[row + d - 1 : row + d, :]
    wall_ext = wall_o[...]
    wall = wall_o[edge : edge + depth, :]

    for q in range(Q):
        put_rows(p0, q, ext, 8, get_rows(post, q, depth, 0, depth))
    for d in range(1, REACH + 1):
        put_layer(p0, 8 - d, ext, below[(d - 1) * BLOCK : (d - 1) * BLOCK + Q, :])
        put_layer(p0, 7 + depth + d, ext, above[(d - 1) * BLOCK : (d - 1) * BLOCK + Q, :])
    row = REACH * BLOCK
    for n, (k, q) in enumerate(reaching(1)):
        put_rows(p0, q, ext, 8 - REACH - k, below[row + n : row + n + 1, :])
    for n, (k, q) in enumerate(reaching(-1)):
        put_rows(p0, q, ext, 7 + depth + REACH + k, above[row + n : row + n + 1, :])

    for q in range(Q):
        ex, ey, ez = VEL[q]
        moved = roll_plane(get_rows(p0, q, ext, 8 - edge - ez, mid), ex, ey)
        bounced = get_rows(p0, OPP[q], ext, 8 - edge, mid)
        put_rows(s1, q, mid, 0, jnp.where(wall_ext > 0.5, bounced, moved))
    clear_pad(s1, mid)
    for i in range(1, mid - 1):
        lanes = slice((i - 1) * plane, i * plane)
        x = get_layer(s1, i, mid)
        mb = moments_of(x, herm[...])
        mb1[:, lanes] = mb
        hidden_into(h1, lanes, w1, mb)
        out = x + dot(w2[...], h1[:, lanes]) + b_col[...]
        put_layer(p1, i, mid, out[:Q])

    for q in range(Q):
        ex, ey, ez = VEL[q]
        moved = roll_plane(get_rows(p1, q, mid, edge - ez, depth), ex, ey)
        bounced = get_rows(p1, OPP[q], mid, edge, depth)
        put_rows(s2, q, depth, 0, jnp.where(wall > 0.5, bounced, moved))
    clear_pad(s2, depth)
    for q in range(Q):
        put_rows(gx, q, mid, edge, cot[q * depth : (q + 1) * depth, :] * (1.0 - wall))
    row = REACH * BLOCK + N_REACH
    for n, (k, q) in enumerate(reaching(-1)):
        put_rows(gx, q, mid, edge - k, below[row + n : row + n + 1, :])
    for n, (k, q) in enumerate(reaching(1)):
        put_rows(gx, q, mid, edge + depth - 1 + k, above[row + n : row + n + 1, :])
    for q in range(Q):
        ex, ey, ez = VEL[q]
        moved = roll_plane(get_rows(gx, q, mid, edge + ez, depth), -ex, -ey)
        at = OPP[q] * depth
        put_rows(gp2, q, depth, 0, moved + wall * cot[at : at + depth, :])
    clear_pad(gp2, depth)

    total = jnp.zeros((QP, plane), F32)
    for z in range(depth):
        lanes = slice(z * plane, (z + 1) * plane)
        mb = moments_of(get_layer(s2, z, depth), herm[...])
        mb2[:, lanes] = mb
        hidden_into(h2, lanes, w1, mb)
        gp = get_layer(gp2, z, depth)
        gb = gp.astype(BF)
        gb2[:, lanes] = gb
        total = total + gp
        g = adjoint_layer(gp, gb, h2, lanes, da2, lanes, w_out, w_in, herm_t[...])[:Q]
        put_layer(g2, z, depth, g)
        if z < REACH:
            send_dn[z * BLOCK : z * BLOCK + Q, :] = g
        if depth - 1 - z < REACH:
            d = depth - 1 - z
            send_up[d * BLOCK : d * BLOCK + Q, :] = g
    gsum[...] = total

    for sign, send in ((1, send_up), (-1, send_dn)):
        row = REACH * BLOCK
        for k, q in reaching(-sign):
            z = depth - REACH - k if sign > 0 else REACH + k - 1
            open_cells = 1.0 - wall_o[edge + z : edge + z + 1, :]
            send[row : row + 1, :] = get_rows(g2, q, depth, z, 1) * open_cells
            row += 1


def sums_kernel(mb2, da2, gb2, h2, acc):
    acc[0:MP, :] = dot_nt(mb2[...], da2[...])
    acc[MP : MP + QP, :] = dot_nt(gb2[...], h2[...])


def third_kernel(
    g2, below, above, wall_i, h1, mb1, h0, mb0, acc, gsum, w_in, w_out, herm_t,
    d_field, sums,
    gx, raw, gp1, g1, raw1, gp0, da1, da0, gb1, gb0, out0,
):
    mid, plane = wall_i.shape
    edge = REACH + 1
    depth = mid - 2 * edge
    ext = depth + 16
    wall_ext = wall_i[...]
    open_ext = 1.0 - wall_ext
    wall = wall_i[edge : edge + depth, :]

    for q in range(Q):
        put_rows(raw, q, mid, edge, get_rows(g2, q, depth, 0, depth))
    for d in range(1, REACH + 1):
        put_layer(raw, edge - d, mid, below[(d - 1) * BLOCK : (d - 1) * BLOCK + Q, :])
        put_layer(raw, edge + depth - 1 + d, mid, above[(d - 1) * BLOCK : (d - 1) * BLOCK + Q, :])
    for q in range(Q):
        put_rows(gx, q, ext, 8 - edge, get_rows(raw, q, mid, 0, mid) * open_ext)
    row = REACH * BLOCK
    for n, (k, q) in enumerate(reaching(-1)):
        put_rows(gx, q, ext, 8 - REACH - k, below[row + n : row + n + 1, :])
    for n, (k, q) in enumerate(reaching(1)):
        put_rows(gx, q, ext, 7 + depth + REACH + k, above[row + n : row + n + 1, :])
    for q in range(Q):
        ex, ey, ez = VEL[q]
        moved = roll_plane(get_rows(gx, q, ext, 8 - edge + ez, mid), -ex, -ey)
        put_rows(gp1, q, mid, 0, moved + wall_ext * get_rows(raw, OPP[q], mid, 0, mid))
    clear_pad(gp1, mid)

    total = gsum[...]
    for i in range(1, mid - 1):
        lanes = slice((i - 1) * plane, i * plane)
        gp = get_layer(gp1, i, mid)
        gb = gp.astype(BF)
        if edge <= i < edge + depth:
            gb1[:, (i - edge) * plane : (i - edge + 1) * plane] = gb
            total = total + gp
        g = adjoint_layer(gp, gb, h1, lanes, da1, lanes, w_out, w_in, herm_t[...])[:Q]
        put_layer(raw1, i, mid, g)
        put_layer(g1, i, mid, g * open_ext[i : i + 1, :])

    for q in range(Q):
        ex, ey, ez = VEL[q]
        moved = roll_plane(get_rows(g1, q, mid, edge + ez, depth), -ex, -ey)
        put_rows(gp0, q, depth, 0, moved + wall * get_rows(raw1, OPP[q], mid, edge, depth))
    clear_pad(gp0, depth)
    for z in range(depth):
        lanes = slice(z * plane, (z + 1) * plane)
        gp = get_layer(gp0, z, depth)
        gb = gp.astype(BF)
        gb0[:, lanes] = gb
        total = total + gp
        g = adjoint_layer(gp, gb, h0, lanes, da0, lanes, w_out, w_in, herm_t[...])[:Q]
        put_layer(out0, z, depth, g)
    for q in range(Q):
        d_field[q * depth : (q + 1) * depth, :] = get_rows(out0, q, depth, 0, depth)

    own = slice(REACH * plane, (REACH + depth) * plane)
    part = acc[0:MP, :] + dot_nt(mb1[:, own], da1[:, own]) + dot_nt(mb0[...], da0[...])
    sums[0:24, :] = part[0:24, :]
    part = acc[MP : MP + QP, :] + dot_nt(gb1[...], h1[:, own]) + dot_nt(gb0[...], h0[...])
    sums[24 : 24 + Q + 1, :] = part[0 : Q + 1, :]
    line = dot_nt(jnp.ones((8, plane), F32), total, lax.Precision.HIGHEST)
    sums[MOM + 1 : MOM + 2, 0:QP] = line[0:1, :]


def last_kernel(scale, core, mine, other, g_w_in, g_b_in, g_w_out, g_b_out):
    first = core[0] == 0
    low = jnp.where(first, mine[...], other[...]) * scale
    high = jnp.where(first, other[...], mine[...]) * scale
    g_w_in[...] = low[:MOM, :]
    g_b_in[...] = low[MOM : MOM + 1, :]
    g_b_out[...] = low[MOM + 1 : MOM + 2, :Q]
    turned = jnp.concatenate([low[24:, :], high], axis=0).T
    g_w_out[...] = turned[:, :Q]


def call(kernel, outs, scratch, args, flops, smem=()):
    vmem = pl.BlockSpec(memory_space=pltpu.VMEM)
    scalars = pl.BlockSpec(memory_space=pltpu.SMEM)
    return pl.pallas_call(
        kernel,
        out_shape=[jax.ShapeDtypeStruct(shape, kind) for shape, kind in outs],
        in_specs=[scalars if n in smem else vmem for n in range(len(args))],
        out_specs=[vmem] * len(outs),
        scratch_shapes=[pltpu.VMEM(shape, kind) for shape, kind in scratch],
        compiler_params=pltpu.CompilerParams(vmem_limit_bytes=28 * 1024 * 1024),
        cost_estimate=pl.CostEstimate(flops=flops, bytes_accessed=2000000, transcendentals=0),
    )(*args)


def factor_stages(space, traj):
    core = 2 if space % 2 == 0 else 1
    rest = space // core
    stride = traj * core
    stages = []
    first = [(1, traj)] if traj > 1 else []
    if rest % 2 == 0 and traj <= 2:
        first.append((stride, 2))
        stride, rest = stride * 2, rest // 2
    if first:
        stages.append(first)
    while rest > 1:
        size = next((f for f in (4, 3, 2) if rest % f == 0), rest)
        stages.append([(stride, size)])
        stride, rest = stride * size, rest // size
    return core, stages


def partners(total, digits):
    shifts = [()]
    for _, size in digits:
        shifts = [s + (k,) for s in shifts for k in range(size)]
    result = []
    for shift in shifts[1:]:
        pairs = []
        for index in range(total):
            to = index
            for (stride, size), k in zip(digits, shift):
                digit = index // stride % size
                to += ((digit + k) % size - digit) * stride
            pairs.append((index, to))
        result.append(pairs)
    return result


def per_device(field, solid, cotangent, w_in, b_in, w_out, b_out):
    local, pops, depth, plane = field.shape
    hid = w_in.shape[1]
    space, traj = lax.axis_size("space"), lax.axis_size("traj")
    axes = ("space", "traj")
    up = [(i, (i + 1) % space) for i in range(space)]
    down = [(j, i) for i, j in up]
    herm, herm_t = hermite_operands()
    edge = REACH + 1
    mid, ext = depth + 2 * edge, depth + 16
    work = mid - 2
    half = plane // 2
    field = field.reshape(pops * depth, plane)
    cot = cotangent.reshape(pops * depth, plane)
    solid = solid.reshape(depth, plane)

    def pops_buf(rows, count=QP):
        return ((2, count * rows, half), F32)

    send_up, send_dn, post, h0, mb0, w1, w_in_p, w2, w_out_p, b_col = call(
        first_kernel,
        [
            ((SEND_ONE, plane), F32),
            ((SEND_ONE, plane), F32),
            pops_buf(depth, Q),
            ((hid, depth * plane), BF),
            ((MP, depth * plane), BF),
            ((hid, MP), BF),
            ((MP, hid), BF),
            ((QP, hid), BF),
            ((hid, QP), BF),
            ((QP, plane), F32),
        ],
        [pops_buf(depth), ((MP, hid), F32), ((QP, hid), F32)],
        [field, cot, solid, w_in, b_in.reshape(1, hid), w_out, b_out.reshape(1, pops), herm],
        10**9,
    )
    below = lax.ppermute(send_up, "space", up)
    above = lax.ppermute(send_dn, "space", down)
    send_up, send_dn, g2, wall, h1, mb1, h2, mb2, da2, gb2, gsum = call(
        second_kernel,
        [
            ((SEND_TWO, plane), F32),
            ((SEND_TWO, plane), F32),
            pops_buf(depth, Q),
            ((mid, plane), F32),
            ((hid, work * plane), BF),
            ((MP, work * plane), BF),
            ((hid, depth * plane), BF),
            ((MP, depth * plane), BF),
            ((hid, depth * plane), BF),
            ((QP, depth * plane), BF),
            ((QP, plane), F32),
        ],
        [pops_buf(ext), pops_buf(mid), pops_buf(mid), pops_buf(depth), pops_buf(mid), pops_buf(depth)],
        [post, below, above, cot, solid, w1, w_in_p, w2, w_out_p, b_col, herm, herm_t],
        3 * 10**9,
    )
    below = lax.ppermute(send_up, "space", up)
    above = lax.ppermute(send_dn, "space", down)
    (acc,) = call(sums_kernel, [((MP + QP, hid), F32)], [], [mb2, da2, gb2, h2], 10**9)
    d_field, sums = call(
        third_kernel,
        [((pops * depth, plane), F32), ((64, hid), F32)],
        [
            pops_buf(ext), pops_buf(mid), pops_buf(mid), pops_buf(mid), pops_buf(mid), pops_buf(depth),
            ((hid, work * plane), BF), ((hid, depth * plane), BF),
            ((QP, depth * plane), BF), ((QP, depth * plane), BF), pops_buf(depth),
        ],
        [g2, below, above, wall, h1, mb1, h0, mb0, acc, gsum, w_in_p, w_out_p, herm_t],
        3 * 10**9,
    )

    core, stages = factor_stages(space, traj)
    total = space * traj
    me = lax.axis_index("space") % core
    swap = partners(total, [(traj, core)])[0]
    rows = sums.shape[0] // 2
    mine = lax.dynamic_slice_in_dim(sums, me * rows, rows, 0)
    other = lax.dynamic_slice_in_dim(sums, (1 - me) * rows, rows, 0)
    mine = mine + lax.ppermute(other, axes, swap)
    for digits in stages:
        moved = [lax.ppermute(mine, axes, pairs) for pairs in partners(total, digits)]
        for value in moved:
            mine = mine + value
    other = lax.ppermute(mine, axes, swap)

    cells = traj * local * space * depth * plane * STEPS
    scale = 1.0 / math.sqrt(float(cells))
    g_w_in, g_b_in, g_w_out, g_b_out = call(
        lambda *refs: last_kernel(scale, *refs),
        [((MOM, hid), F32), ((1, hid), F32), ((hid, pops), F32), ((1, pops), F32)],
        [],
        [me.reshape(1).astype(jnp.int32), mine, other],
        10**6,
        smem=(0,),
    )
    return (
        d_field.reshape(local, pops, depth, plane),
        g_w_in,
        g_b_in.reshape(hid),
        g_w_out,
        g_b_out.reshape(pops),
    )


def solution(mesh):
    return jax.shard_map(
        per_device,
        mesh=mesh,
        in_specs=(
            P("traj", None, "space", None),
            P("traj", "space", None),
            P("traj", None, "space", None),
            P(),
            P(),
            P(),
            P(),
        ),
        out_specs=(P("traj", None, "space", None), P(), P(), P(), P()),
        check_vma=False,
    )
```

time: 369 us -> 75.2 us (0.20)
  local copies, waits for them, and re-layouts: 112 us -> 16.7 us
  waiting for transfers between devices: 100 us -> 14.7 us
  matrix products: 47.5 us -> 0 us
  blocking collectives: 37.4 us -> 0 us
  other arithmetic: 31.2 us -> 0.05 us
  Pallas kernels: 0 us -> 23.4 us
  between operations: 20.6 us -> 0.82 us
    psum x1 -> x0, waiting for transfers between devices: 78.1 us -> none  [per_device(): lax.psum((totals[0], totals[1], totals[2], totals[3]), ('space', 'traj'))]
    dynamic_update_slice x80 -> x0, local copies, waits for them, and re-layouts: 72.8 us -> none  [collide_layers(): lax.map(lambda layer: collide_block(layer, weights, hermite)[0], layers)]
    dot_general x200 -> x0, matrix products: 47.5 us -> none  [the longest x40 9.95 us: collide_block(): jnp.dot(hermite, block, precision=lax.Precision.HIGHEST, preferred_elemen...]
    psum x1 -> x0, blocking collectives: 37.4 us -> none  [per_device(): lax.psum((totals[0], totals[1], totals[2], totals[3]), ('space', 'traj'))]
    another operation x325 -> x0, local copies, waits for them, and re-layouts: 26.2 us -> none  [the longest x160 14 us: stream_local(): return jnp.stack(moved)]
    pallas_call x0 -> x5, Pallas kernels: none -> 23.4 us  [call(): pl.pallas_call(kernel, out_shape=[jax.ShapeDtypeStruct(shape, kind) for s...]
    concatenate x220 -> x0, other arithmetic: 16.6 us -> none  [roll_plane(): return jnp.roll(grid, (along_x, along_y), (1, 2)).reshape(depth, NX * NY)]
    unnamed x180 -> x48, local copies, waits for them, and re-layouts: 4.69 us -> 16.7 us
  transfers between devices with their start and end apart: 11 -> 12, of which waited for: 8 -> 8; matrix products, arithmetic and copies ran while one was open for 2% -> 0% of each run, Pallas kernels for 0% -> 2%
where the time goes in v1:
time: 75.2 us; the launch traced here: 74.6 us
  Pallas kernels  23.4 us (31%)
  starting transfers between devices  18.9 us (25%)
  local copies, waits for them, and re-layouts  16.7 us (22%)
  waiting for transfers between devices  14.7 us (20%)
  between operations  0.82 us (1%)
    pallas_call x5, Pallas kernels, call(): pl.pallas_call(kernel, out_shape=[jax.ShapeDtypeStruct(shape, kind) for s...  23.4 us
    unnamed x48, local copies, waits for them, and re-layouts  16.7 us
    ppermute x6, waiting for transfers between devices, per_device(): lax.ppermute(mine, axes, pairs)  9.13 us
    ppermute x6, starting transfers between devices, per_device(): lax.ppermute(mine, axes, pairs)  8.84 us
    ppermute x2, starting transfers between devices, per_device(): above = lax.ppermute(send_dn, 'space', down)  8.41 us
    ppermute x2, waiting for transfers between devices, per_device(): below = lax.ppermute(send_up, 'space', up)  3.11 us
  transfers between devices with their start and end apart: 12, of which 8 were waited for; matrix products, arithmetic and copies ran while one was open for 0% of the time, Pallas kernels for 2%

profile of v1, /device:TPU:0, one launch (start us, length us, event | category | flops | bytes accessed | tf_op | source)
XLA Modules:
  0.0 74.6 jit_solution(9848833289689919131)
XLA Ops:
  0.6 0.0 copy-start.11
  0.6 0.0 copy-start.12
  0.7 0.0 copy-start.7
  0.7 0.9 %copy.14.w_out = bf16[512,39]{1,0:T(8,128)(2,1)S(1)} copy(bf16[512,39]{0,1:T(8,128)(2,1)} %param.14) | data formatting | bytes 79872 | tf_op args[5]
  1.6 0.0 copy-start.2
  1.6 1.0 %copy-done.2 = f32[1,39,8,256]{3,2,1,0:T(8,128)S(1)} copy-done((f32[1,39,8,256]{3,2,1,0:T(8,128)S(1)}, f32[1,39,8,256]{3,2,1,0:T(8,128)}, u32[]{:S(2)}) %copy-start.2) | copy-done | bytes 319512
  2.6 0.0 copy-start.3
  2.6 1.0 %copy-done.3 = f32[1,39,8,256]{3,2,1,0:T(8,128)S(1)} copy-done((f32[1,39,8,256]{3,2,1,0:T(8,128)S(1)}, f32[1,39,8,256]{3,2,1,0:T(8,128)}, u32[]{:S(2)}) %copy-start.3) | copy-done | bytes 319512
  3.5 0.0 copy-start.5
  3.5 0.7 copy-done.5
  4.3 0.0 copy-start.6
  4.3 0.7 copy-done.6
  5.0 0.0 copy-start.8
  5.0 0.7 copy-done.8
  5.7 0.7 copy-done.9
  6.3 0.7 copy-done.10
  7.0 2.1 %shard_map.128 = (f32[160,256]{1,0:T(8,128)S(1)}, f32[160,256]{1,0:T(8,128)S(1)}, f32[2,312,128]{2,1,0:T(8,128)S(1)}, bf16[512,2048]{1,0:T(8,128)(2,1)S(1)}, bf1...) custom-call(f32[312,256]{1,0:T(8,128)S(1)} %bitcast.9, ...), custom_call_target="tpu_custom_call" | custom-call | flops 1000000000 | bytes 2000000 | tf_op jit(solution)/shard_map/pallas_call | solution.py:446
  9.2 0.0 copy-start.13
  9.2 1.3 %copy-done.13 = bf16[512,2048]{1,0:T(8,128)(2,1)} copy-done((bf16[512,2048]{1,0:T(8,128)(2,1)}, bf16[512,2048]{1,0:T(8,128)(2,1)S(1)}, u32[]{:S(2)}) %copy-start.13) | copy-done | bytes 2097176
  10.5 0.5 collective-permute-start
  11.0 5.0 %collective-permute-start.1 = (f32[160,256]{1,0:T(8,128)S(1)}, f32[160,256]{1,0:T(8,128)S(1)}, u32[]{:S(2)}, u32[]{:S(2)}) collective-permute-start(f32[160,256]{1,0:T(8,128)S(1)} %get-tuple-element.34), channel_id=1, source_target_pairs={{2,0},{4,2},{6,4},{8,6},{10,8},{12,10},{14,12},{16,14},{18,16},{20... | collective-permute-start | bytes 491528 | tf_op jit(solution)/shard_map/ppermute | solution.py:530
  16.0 3.1 %collective-permute-done.below = f32[160,256]{1,0:T(8,128)S(1)} collective-permute-done((f32[160,256]{1,0:T(8,128)S(1)}, f32[160,256]{1,0:T(8,128)S(1)}, u32[]{:S(2)}, u32[]{:S(2)}) %collective-permute-start) | collective-permute-done | bytes 163872 | tf_op jit(solution)/shard_map/ppermute | solution.py:529
  19.1 0.0 collective-permute-done.1.above
  19.1 0.0 copy-done.11
  19.1 0.0 copy-done.12
  19.1 0.0 copy-done.7
  19.1 0.0 copy-done.4
  19.1 8.4 %shard_map.129 = (f32[144,256]{1,0:T(8,128)S(1)}, f32[144,256]{1,0:T(8,128)S(1)}, f32[2,312,128]{2,1,0:T(8,128)S(1)}, f32[16,256]{1,0:T(8,128)S(1)}, bf16[512,35...) custom-call(f32[2,312,128]{2,1,0:T(8,128)S(1)} %get-tuple-element.32, ...), custom_call_target="tpu_custom_call" | custom-call | flops 3000000000 | bytes 2000000 | tf_op jit(solution)/shard_map/pallas_call | solution.py:446
  27.5 0.0 copy-done.17
  27.5 0.0 copy-start
  27.5 1.3 %copy-done = bf16[512,2048]{1,0:T(8,128)(2,1)} copy-done((bf16[512,2048]{1,0:T(8,128)(2,1)}, bf16[512,2048]{1,0:T(8,128)(2,1)S(1)}, u32[]{:S(2)}) %copy-start) | copy-done | bytes 2097176
  28.9 1.8 %copy-done.15 = bf16[512,3584]{1,0:T(8,128)(2,1)} copy-done((bf16[512,3584]{1,0:T(8,128)(2,1)}, bf16[512,3584]{1,0:T(8,128)(2,1)S(1)}, u32[]{:S(2)}) %copy-start.15) | copy-done | bytes 3670040
  30.7 0.7 copy-done.19
  31.3 0.6 copy-done.21
  32.0 1.0 %collective-permute-start.2 = (f32[144,256]{1,0:T(8,128)S(1)}, f32[144,256]{1,0:T(8,128)S(1)}, u32[]{:S(2)}, u32[]{:S(2)}) collective-permute-start(f32[144,256]{1,0:T(8,128)S(1)} %get-tuple-element.41), channel_id=1, source_target_pairs={{0,2},{2,4},{4,6},{6,8},{8,10},{10,12},{12,14},{14,16},{16,18},{18... | collective-permute-start | bytes 442376 | tf_op jit(solution)/shard_map/ppermute | solution.py:550
  33.0 3.4 %collective-permute-start.3 = (f32[144,256]{1,0:T(8,128)S(1)}, f32[144,256]{1,0:T(8,128)S(1)}, u32[]{:S(2)}, u32[]{:S(2)}) collective-permute-start(f32[144,256]{1,0:T(8,128)S(1)} %get-tuple-element.42), channel_id=1, source_target_pairs={{2,0},{4,2},{6,4},{8,6},{10,8},{12,10},{14,12},{16,14},{18,16},{20... | collective-permute-start | bytes 442376 | tf_op jit(solution)/shard_map/ppermute | solution.py:551
  36.4 1.6 %copy-done.1 = bf16[512,2048]{1,0:T(8,128)(2,1)S(1)} copy-done((bf16[512,2048]{1,0:T(8,128)(2,1)S(1)}, bf16[512,2048]{1,0:T(8,128)(2,1)}, u32[]{:S(2)}) %copy-start.1) | copy-done | bytes 2097176
  38.0 1.4 %shard_map.130.acc = f32[80,512]{1,0:T(8,128)S(1)} custom-call(bf16[32,2048]{1,0:T(8,128)(2,1)S(1)} %get-tuple-element.48.mb2, bf16[512,2048]{1,0:T(8,128)(2,1)S(1)} %copy-done.1, bf16[48,2048]{1,0:T(8,128)(2,1)S(1)} %get-tuple-element.50.gb2, bf16[512,2048]{1,0:T(8,128)(2,1)S(1)} %get-tuple-element.51.h2), custom_call_target="tpu_custom_call" | custom-call | flops 1000000000 | bytes 2000000 | tf_op jit(solution)/shard_map/pallas_call | solution.py:446
  39.4 0.0 collective-permute-done.2.below
  39.4 0.0 collective-permute-done.3.above
  39.4 0.2 copy-done.14
  39.6 0.0 copy-done.18
  39.6 0.0 copy-done.20
  39.6 0.0 copy-done.22
  39.6 2.0 %copy-done.16 = bf16[512,3584]{1,0:T(8,128)(2,1)S(1)} copy-done((bf16[512,3584]{1,0:T(8,128)(2,1)S(1)}, bf16[512,3584]{1,0:T(8,128)(2,1)}, u32[]{:S(2)}) %copy-start.16) | copy-done | bytes 3670040
  41.7 10.9 %shard_map.131 = (f32[312,256]{1,0:T(8,128)}, f32[64,512]{1,0:T(8,128)S(1)}) custom-call(f32[2,312,128]{2,1,0:T(8,128)S(1)} %get-tuple-element.40.g2, f32[144,256]{1,0:T(8,128)S(1)} %collective-permute-done.2.below, f32[144,256]{1,0:T(8,128)S(1)} %collective-permute-done.3.above, f32[16,256]{1,0:T(8,128)S(1)} %get-tuple-element.43.wall_i, ...), custom_call_target="tpu_custom_call" | custom-call | flops 3000000000 | bytes 2000000 | tf_op jit(solution)/shard_map/pallas_call | solution.py:446
  52.6 0.1 collective-permute-start.4
  52.6 1.2 %collective-permute-done.4 = f32[32,512]{1,0:T(8,128)S(1)} collective-permute-done((f32[32,512]{1,0:T(8,128)S(1)}, f32[32,512]{1,0:T(8,128)S(1)}, u32[]{:S(2)}, u32[]{:S(2)}) %collective-permute-start.4) | collective-permute-done | bytes 65568 | tf_op jit(solution)/shard_map/ppermute | solution.py:572
  53.9 0.1 collective-permute-start.5
  54.0 2.0 %collective-permute-start.6 = (f32[32,512]{1,0:T(8,128)S(1)}, f32[32,512]{1,0:T(8,128)S(1)}, u32[]{:S(2)}, u32[]{:S(2)}) collective-permute-start(f32[32,512]{1,0:T(8,128)S(1)} %dynamic-slice_add_fusion), channel_id=1, source_target_pairs={{0,1},{1,0},{2,3},{3,2},{4,5},{5,4},{6,7},{7,6},{8,9},{9,8},{10,11... | collective-permute-start | bytes 196616 | tf_op jit(solution)/shard_map/ppermute | solution.py:574
  56.0 1.5 %collective-permute-start.7 = (f32[32,512]{1,0:T(8,128)S(1)}, f32[32,512]{1,0:T(8,128)S(1)}, u32[]{:S(2)}, u32[]{:S(2)}) collective-permute-start(f32[32,512]{1,0:T(8,128)S(1)} %dynamic-slice_add_fusion), channel_id=1, source_target_pairs={{0,5},{1,4},{2,7},{3,6},{4,1},{5,0},{6,3},{7,2},{8,13},{9,12},{10,... | collective-permute-start | bytes 196616 | tf_op jit(solution)/shard_map/ppermute | solution.py:574
  57.4 0.8 %collective-permute-done.5 = f32[32,512]{1,0:T(8,128)S(1)} collective-permute-done((f32[32,512]{1,0:T(8,128)S(1)}, f32[32,512]{1,0:T(8,128)S(1)}, u32[]{:S(2)}, u32[]{:S(2)}) %collective-permute-start.5) | collective-permute-done | bytes 65568 | tf_op jit(solution)/shard_map/ppermute | solution.py:574
  58.2 0.2 collective-permute-done.6
  58.4 2.7 %collective-permute-done.7 = f32[32,512]{1,0:T(8,128)S(1)} collective-permute-done((f32[32,512]{1,0:T(8,128)S(1)}, f32[32,512]{1,0:T(8,128)S(1)}, u32[]{:S(2)}, u32[]{:S(2)}) %collective-permute-start.7) | collective-permute-done | bytes 65568 | tf_op jit(solution)/shard_map/ppermute | solution.py:574
  61.2 4.7 %collective-permute-start.10 = (f32[32,512]{1,0:T(8,128)S(1)}, f32[32,512]{1,0:T(8,128)S(1)}, u32[]{:S(2)}, u32[]{:S(2)}) collective-permute-start(f32[32,512]{1,0:T(8,128)S(1)} %add_add_fusion.1), channel_id=1, source_target_pairs={{0,24},{1,25},{2,26},{3,27},{4,28},{5,29},{6,30},{7,31},{8,0},{9,1... | collective-permute-start | bytes 196616 | tf_op jit(solution)/shard_map/ppermute | solution.py:574
  65.8 0.0 collective-permute-start.8
  65.8 0.6 collective-permute-start.9
  66.5 1.3 %collective-permute-done.10 = f32[32,512]{1,0:T(8,128)S(1)} collective-permute-done((f32[32,512]{1,0:T(8,128)S(1)}, f32[32,512]{1,0:T(8,128)S(1)}, u32[]{:S(2)}, u32[]{:S(2)}) %collective-permute-start.10) | collective-permute-done | bytes 65568 | tf_op jit(solution)/shard_map/ppermute | solution.py:574
  67.7 4.2 %collective-permute-done.8 = f32[32,512]{1,0:T(8,128)S(1)} collective-permute-done((f32[32,512]{1,0:T(8,128)S(1)}, f32[32,512]{1,0:T(8,128)S(1)}, u32[]{:S(2)}, u32[]{:S(2)}) %collective-permute-start.8) | collective-permute-done | bytes 65568 | tf_op jit(solution)/shard_map/ppermute | solution.py:574
  71.9 0.0 collective-permute-done.9
  71.9 0.1 collective-permute-start.11
  72.0 1.2 %collective-permute-done.11.refs_2_ = f32[32,512]{1,0:T(8,128)S(1)} collective-permute-done((f32[32,512]{1,0:T(8,128)S(1)}, f32[32,512]{1,0:T(8,128)S(1)}, u32[]{:S(2)}, u32[]{:S(2)}) %collective-permute-start.11) | collective-permute-done | bytes 65568 | tf_op jit(solution)/shard_map/ppermute | solution.py:577
  73.2 0.6 shard_map.132
  73.9 0.8 %copy.15 = f32[512,39]{0,1:T(8,128)} copy(f32[512,39]{1,0:T(8,128)S(1)} %get-tuple-element.62) | data formatting | bytes 159744
  (17 shorter events, 0.1 us)
Async XLA Ops:
  0.6 18.4 %copy-start.11 = (bf16[32,144]{1,0:T(8,128)(2,1)S(1)}, bf16[32,144]{1,0:T(8,128)(2,1)}, u32[]{:S(2)}) copy-start(bf16[32,144]{1,0:T(8,128)(2,1)} %constant.29.clone.herm) | copy-start | bytes 27652
  0.6 18.4 %copy-start.12 = (bf16[48,96]{1,0:T(8,128)(2,1)S(1)}, bf16[48,96]{1,0:T(8,128)(2,1)}, u32[]{:S(2)}) copy-start(bf16[48,96]{1,0:T(8,128)(2,1)} %constant.30.clone.herm_t) | copy-start | bytes 27652
  0.7 18.4 %copy-start.7 = (s32[1,8,256]{2,1,0:T(8,128)S(1)}, s32[1,8,256]{2,1,0:T(8,128)}, u32[]{:S(2)}) copy-start(s32[1,8,256]{2,1,0:T(8,128)} %param.10) | copy-start | bytes 24580
  1.6 1.0 %copy-start.2 = (f32[1,39,8,256]{3,2,1,0:T(8,128)S(1)}, f32[1,39,8,256]{3,2,1,0:T(8,128)}, u32[]{:S(2)}) copy-start(f32[1,39,8,256]{3,2,1,0:T(8,128)} %param.9) | copy-start | bytes 958468
  2.6 1.0 %copy-start.3 = (f32[1,39,8,256]{3,2,1,0:T(8,128)S(1)}, f32[1,39,8,256]{3,2,1,0:T(8,128)}, u32[]{:S(2)}) copy-start(f32[1,39,8,256]{3,2,1,0:T(8,128)} %param.11) | copy-start | bytes 958468
  3.5 0.7 copy-start.5
  4.3 0.7 copy-start.6
  5.0 0.7 copy-start.8
  5.7 0.7 copy-start.9
  6.3 0.7 copy-start.10
  7.0 12.1 %copy-start.4 = (f32[1,39,8,256]{3,2,1,0:T(8,128)S(1)}, f32[1,39,8,256]{3,2,1,0:T(8,128)}, u32[]{:S(2)}) copy-start(f32[1,39,8,256]{3,2,1,0:T(8,128)} %param.11) | copy-start | bytes 958468
  9.2 1.3 %copy-start.13 = (bf16[512,2048]{1,0:T(8,128)(2,1)}, bf16[512,2048]{1,0:T(8,128)(2,1)S(1)}, u32[]{:S(2)}) copy-start(bf16[512,2048]{1,0:T(8,128)(2,1)S(1)} %get-tuple-element.46.h0) | copy-start | bytes 6291460
  10.5 17.0 %copy-start.17 = (bf16[512,48]{1,0:T(8,128)(2,1)}, bf16[512,48]{1,0:T(8,128)(2,1)S(1)}, u32[]{:S(2)}) copy-start(bf16[512,48]{1,0:T(8,128)(2,1)S(1)} %get-tuple-element.38.w_out) | copy-start | bytes 147460
  10.5 8.6 %collective-permute-start = (f32[160,256]{1,0:T(8,128)S(1)}, f32[160,256]{1,0:T(8,128)S(1)}, u32[]{:S(2)}, u32[]{:S(2)}) collective-permute-start(f32[160,256]{1,0:T(8,128)S(1)} %get-tuple-element.33), channel_id=1, source_target_pairs={{0,2},{2,4},{4,6},{6,8},{8,10},{10,12},{12,14},{14,16},{16,18},{18... | collective-permute-start | bytes 491528 | tf_op jit(solution)/shard_map/ppermute | solution.py:529
  11.0 8.1 %collective-permute-start.1 = (f32[160,256]{1,0:T(8,128)S(1)}, f32[160,256]{1,0:T(8,128)S(1)}, u32[]{:S(2)}, u32[]{:S(2)}) collective-permute-start(f32[160,256]{1,0:T(8,128)S(1)} %get-tuple-element.34), channel_id=1, source_target_pairs={{2,0},{4,2},{6,4},{8,6},{10,8},{12,10},{14,12},{16,14},{18,16},{20... | collective-permute-start | bytes 491528 | tf_op jit(solution)/shard_map/ppermute | solution.py:530
  27.5 1.3 %copy-start = (bf16[512,2048]{1,0:T(8,128)(2,1)}, bf16[512,2048]{1,0:T(8,128)(2,1)S(1)}, u32[]{:S(2)}) copy-start(bf16[512,2048]{1,0:T(8,128)(2,1)S(1)} %get-tuple-element.49.da2) | copy-start | bytes 6291460
  28.9 1.8 %copy-start.15 = (bf16[512,3584]{1,0:T(8,128)(2,1)}, bf16[512,3584]{1,0:T(8,128)(2,1)S(1)}, u32[]{:S(2)}) copy-start(bf16[512,3584]{1,0:T(8,128)(2,1)S(1)} %get-tuple-element.44.h1) | copy-start | bytes 11010052
  30.7 0.7 copy-start.19
  31.3 0.6 copy-start.21
  32.0 7.4 %collective-permute-start.2 = (f32[144,256]{1,0:T(8,128)S(1)}, f32[144,256]{1,0:T(8,128)S(1)}, u32[]{:S(2)}, u32[]{:S(2)}) collective-permute-start(f32[144,256]{1,0:T(8,128)S(1)} %get-tuple-element.41), channel_id=1, source_target_pairs={{0,2},{2,4},{4,6},{6,8},{8,10},{10,12},{12,14},{14,16},{16,18},{18... | collective-permute-start | bytes 442376 | tf_op jit(solution)/shard_map/ppermute | solution.py:550
  33.0 6.4 %collective-permute-start.3 = (f32[144,256]{1,0:T(8,128)S(1)}, f32[144,256]{1,0:T(8,128)S(1)}, u32[]{:S(2)}, u32[]{:S(2)}) collective-permute-start(f32[144,256]{1,0:T(8,128)S(1)} %get-tuple-element.42), channel_id=1, source_target_pairs={{2,0},{4,2},{6,4},{8,6},{10,8},{12,10},{14,12},{16,14},{18,16},{20... | collective-permute-start | bytes 442376 | tf_op jit(solution)/shard_map/ppermute | solution.py:551
  36.4 1.6 %copy-start.1 = (bf16[512,2048]{1,0:T(8,128)(2,1)S(1)}, bf16[512,2048]{1,0:T(8,128)(2,1)}, u32[]{:S(2)}) copy-start(bf16[512,2048]{1,0:T(8,128)(2,1)} %copy-done) | copy-start | bytes 6291460
  38.0 1.6 %copy-start.14 = (bf16[512,2048]{1,0:T(8,128)(2,1)S(1)}, bf16[512,2048]{1,0:T(8,128)(2,1)}, u32[]{:S(2)}) copy-start(bf16[512,2048]{1,0:T(8,128)(2,1)} %copy-done.13) | copy-start | bytes 6291460
  38.0 1.6 %copy-start.18 = (bf16[512,48]{1,0:T(8,128)(2,1)S(1)}, bf16[512,48]{1,0:T(8,128)(2,1)}, u32[]{:S(2)}) copy-start(bf16[512,48]{1,0:T(8,128)(2,1)} %copy-done.17) | copy-start | bytes 147460
  38.0 1.6 %copy-start.20 = (bf16[32,3584]{1,0:T(8,128)(2,1)S(1)}, bf16[32,3584]{1,0:T(8,128)(2,1)}, u32[]{:S(2)}) copy-start(bf16[32,3584]{1,0:T(8,128)(2,1)} %copy-done.19) | copy-start | bytes 688132
  38.0 1.6 %copy-start.22 = (f32[48,256]{1,0:T(8,128)S(1)}, f32[48,256]{1,0:T(8,128)}, u32[]{:S(2)}) copy-start(f32[48,256]{1,0:T(8,128)} %copy-done.21) | copy-start | bytes 147460
  39.6 2.0 %copy-start.16 = (bf16[512,3584]{1,0:T(8,128)(2,1)S(1)}, bf16[512,3584]{1,0:T(8,128)(2,1)}, u32[]{:S(2)}) copy-start(bf16[512,3584]{1,0:T(8,128)(2,1)} %copy-done.15) | copy-start | bytes 11010052
  52.6 1.3 %collective-permute-start.4 = (f32[32,512]{1,0:T(8,128)S(1)}, f32[32,512]{1,0:T(8,128)S(1)}, u32[]{:S(2)}, u32[]{:S(2)}) collective-permute-start(f32[32,512]{1,0:T(8,128)S(1)} %constant_dynamic-slice_fusion), channel_id=1, source_target_pairs={{0,2},{1,3},{2,0},{3,1},{4,6},{5,7},{6,4},{7,5},{8,10},{9,11},{10,... | collective-permute-start | bytes 196616 | tf_op jit(solution)/shard_map/ppermute | solution.py:572
  53.9 4.3 %collective-permute-start.5 = (f32[32,512]{1,0:T(8,128)S(1)}, f32[32,512]{1,0:T(8,128)S(1)}, u32[]{:S(2)}, u32[]{:S(2)}) collective-permute-start(f32[32,512]{1,0:T(8,128)S(1)} %dynamic-slice_add_fusion), channel_id=1, source_target_pairs={{0,4},{1,5},{2,6},{3,7},{4,0},{5,1},{6,2},{7,3},{8,12},{9,13},{10,... | collective-permute-start | bytes 196616 | tf_op jit(solution)/shard_map/ppermute | solution.py:574
  54.0 4.4 %collective-permute-start.6 = (f32[32,512]{1,0:T(8,128)S(1)}, f32[32,512]{1,0:T(8,128)S(1)}, u32[]{:S(2)}, u32[]{:S(2)}) collective-permute-start(f32[32,512]{1,0:T(8,128)S(1)} %dynamic-slice_add_fusion), channel_id=1, source_target_pairs={{0,1},{1,0},{2,3},{3,2},{4,5},{5,4},{6,7},{7,6},{8,9},{9,8},{10,11... | collective-permute-start | bytes 196616 | tf_op jit(solution)/shard_map/ppermute | solution.py:574
  56.0 5.2 %collective-permute-start.7 = (f32[32,512]{1,0:T(8,128)S(1)}, f32[32,512]{1,0:T(8,128)S(1)}, u32[]{:S(2)}, u32[]{:S(2)}) collective-permute-start(f32[32,512]{1,0:T(8,128)S(1)} %dynamic-slice_add_fusion), channel_id=1, source_target_pairs={{0,5},{1,4},{2,7},{3,6},{4,1},{5,0},{6,3},{7,2},{8,13},{9,12},{10,... | collective-permute-start | bytes 196616 | tf_op jit(solution)/shard_map/ppermute | solution.py:574
  61.2 6.6 %collective-permute-start.10 = (f32[32,512]{1,0:T(8,128)S(1)}, f32[32,512]{1,0:T(8,128)S(1)}, u32[]{:S(2)}, u32[]{:S(2)}) collective-permute-start(f32[32,512]{1,0:T(8,128)S(1)} %add_add_fusion.1), channel_id=1, source_target_pairs={{0,24},{1,25},{2,26},{3,27},{4,28},{5,29},{6,30},{7,31},{8,0},{9,1... | collective-permute-start | bytes 196616 | tf_op jit(solution)/shard_map/ppermute | solution.py:574
  65.8 6.1 %collective-permute-start.8 = (f32[32,512]{1,0:T(8,128)S(1)}, f32[32,512]{1,0:T(8,128)S(1)}, u32[]{:S(2)}, u32[]{:S(2)}) collective-permute-start(f32[32,512]{1,0:T(8,128)S(1)} %add_add_fusion.1), channel_id=1, source_target_pairs={{0,8},{1,9},{2,10},{3,11},{4,12},{5,13},{6,14},{7,15},{8,16},{9,17... | collective-permute-start | bytes 196616 | tf_op jit(solution)/shard_map/ppermute | solution.py:574
  65.8 6.1 %collective-permute-start.9 = (f32[32,512]{1,0:T(8,128)S(1)}, f32[32,512]{1,0:T(8,128)S(1)}, u32[]{:S(2)}, u32[]{:S(2)}) collective-permute-start(f32[32,512]{1,0:T(8,128)S(1)} %add_add_fusion.1), channel_id=1, source_target_pairs={{0,16},{1,17},{2,18},{3,19},{4,20},{5,21},{6,22},{7,23},{8,24},{9,... | collective-permute-start | bytes 196616 | tf_op jit(solution)/shard_map/ppermute | solution.py:574
  71.9 1.3 %collective-permute-start.11 = (f32[32,512]{1,0:T(8,128)S(1)}, f32[32,512]{1,0:T(8,128)S(1)}, u32[]{:S(2)}, u32[]{:S(2)}) collective-permute-start(f32[32,512]{1,0:T(8,128)S(1)} %add_add_fusion.refs_1_), channel_id=1, source_target_pairs={{0,2},{1,3},{2,0},{3,1},{4,6},{5,7},{6,4},{7,5},{8,10},{9,11},{10,... | collective-permute-start | bytes 196616 | tf_op jit(solution)/shard_map/ppermute | solution.py:577

commit v2 on v1

--- a/solution.py
+++ b/solution.py
@@ -18,6 +18,7 @@
 REACH = 3
 BLOCK = 40
 CHUNK = 128
+MIB = 1024 * 1024
 BF = jnp.bfloat16
 F32 = jnp.float32
 
@@ -190,28 +191,62 @@
     return (moments + ones).astype(BF)
 
 
-def hidden_into(h_ref, lanes, w1, mb):
+def hidden_into(h, w1, mb):
     for start in range(0, w1.shape[0], CHUNK):
         act = dot(w1[start : start + CHUNK, :], mb)
-        h_ref[start : start + CHUNK, lanes] = jnp.tanh(act).astype(BF)
-
-
-def adjoint_layer(gp, gb, h_ref, h_lanes, da_ref, da_lanes, w_out, w_in, herm_t):
+        h[start : start + CHUNK, :] = jnp.tanh(act).astype(BF)
+
+
+def d_act_into(da, h, w_out, gb):
     for start in range(0, w_out.shape[0], CHUNK):
         d_hidden = dot(w_out[start : start + CHUNK, :], gb)
-        hidden = h_ref[start : start + CHUNK, h_lanes].astype(F32)
-        da_ref[start : start + CHUNK, da_lanes] = (d_hidden * (1.0 - hidden * hidden)).astype(BF)
-    d_moments = dot(w_in[...], da_ref[:, da_lanes])
-    return gp + dot(herm_t, split_concat(d_moments))
+        hidden = h[start : start + CHUNK, :].astype(F32)
+        da[start : start + CHUNK, :] = (d_hidden * (1.0 - hidden * hidden)).astype(BF)
+
+
+def staggered(count, *stages):
+    for turn in range(count + len(stages) - 1):
+        for late, stage in enumerate(stages):
+            if 0 <= turn - late < count:
+                stage(turn - late)
+
+
+def add_sums(acc, mb, da, gb, h):
+    acc[0:MP, :] += dot_nt(mb, da[...])
+    acc[MP : MP + QP, :] += dot_nt(gb, h[...])
+
+
+class Copies:
+    def __init__(self, sems):
+        self.sems, self.used, self.open = sems, 0, []
+
+    def start(self, source, target):
+        copy = pltpu.make_async_copy(source, target, self.sems.at[self.used])
+        self.used += 1
+        copy.start()
+        self.open.append(copy)
+        return copy
+
+    def wait(self):
+        for copy in self.open:
+            copy.wait()
+        self.open = []
 
 
 def first_kernel(
-    field, cot, solid, w_in, b_in, w_out, b_out, herm,
-    send_up, send_dn, post, h0, mb0, w1_o, w_in_o, w2_o, w_out_o, b_col_o,
-    state, wide, tall,
+    w_in_h, b_in_h, w_out_h, b_out_h, herm_h, field_h, solid_h, cot_h,
+    send_up, send_dn, post, mb0_h, w1_o, w_in_o, w2_o, w_out_o, b_col_o,
+    state, wide, tall, w_in, b_in, w_out, b_out, herm, field, solid, cot, h, mb0, sems,
 ):
+    sources = (w_in_h, b_in_h, w_out_h, b_out_h, herm_h, field_h, solid_h, cot_h)
+    targets = (w_in, b_in, w_out, b_out, herm, field, solid, cot)
+    moves = Copies(sems)
+    copies = [moves.start(a, b) for a, b in zip(sources, targets)]
+    moves.open = []
     depth, plane = solid.shape
     hid = w_in.shape[1]
+    for copy in copies[:4]:
+        copy.wait()
     wide[...] = jnp.zeros(wide.shape, F32)
     wide[:MOM, :] = w_in[...].astype(F32)
     w_in_o[...] = wide[...].astype(BF)
@@ -222,7 +257,7 @@
         rest = rest - piece
     w1_o[...] = wide[...].T.astype(BF)
     tall[...] = jnp.zeros(tall.shape, F32)
-    tall[:Q, :] = w_out[...].astype(F32).T
+    tall[:Q, :] = w_out[...].astype(F32)
     w2_o[...] = tall[...].astype(BF)
     w_out_o[...] = tall[...].T.astype(BF)
     tall[0:8, :] = jnp.zeros((8, hid), F32)
@@ -230,23 +265,31 @@
     column = tall[0:8, 0:128].T
     b_col_o[...] = jnp.broadcast_to(column[:QP, 0:1], (QP, plane))
 
+    for copy in copies[4:6]:
+        copy.wait()
     for q in range(Q):
         put_rows(state, q, depth, 0, field[q * depth : (q + 1) * depth, :])
     clear_pad(state, depth)
     for z in range(depth):
-        lanes = slice(z * plane, (z + 1) * plane)
-        x = get_layer(state, z, depth)
-        mb = moments_of(x, herm[...])
-        mb0[:, lanes] = mb
-        hidden_into(h0, lanes, w1_o, mb)
-        out = x + dot(w2_o[...], h0[:, lanes]) + b_col_o[...]
-        put_layer(post, z, depth, out[:Q])
+        mb0[z] = moments_of(get_layer(state, z, depth), herm[...])
+    moves.start(mb0, mb0_h)
+
+    def hide(z):
+        hidden_into(h.at[z % 2], w1_o, mb0[z])
+
+    def finish(z):
+        out = get_layer(state, z, depth) + dot(w2_o[...], h[z % 2]) + b_col_o[...]
+        out = out[:Q]
+        put_layer(post, z, depth, out)
         if z < REACH:
-            send_dn[z * BLOCK : z * BLOCK + Q, :] = out[:Q]
+            send_dn[z * BLOCK : z * BLOCK + Q, :] = out
         if depth - 1 - z < REACH:
             d = depth - 1 - z
-            send_up[d * BLOCK : d * BLOCK + Q, :] = out[:Q]
-
+            send_up[d * BLOCK : d * BLOCK + Q, :] = out
+
+    staggered(depth, hide, finish)
+    for copy in copies[6:]:
+        copy.wait()
     wall = solid[...].astype(F32)
     for sign, send in ((1, send_up), (-1, send_dn)):
         layer = (lambda d: depth - d) if sign > 0 else (lambda d: d - 1)
@@ -262,13 +305,15 @@
         for d in range(1, REACH + 1):
             send[row : row + 1, :] = wall[layer(d) : layer(d) + 1, :]
             row += 1
+    moves.wait()
 
 
 def second_kernel(
     post, below, above, cot, solid, w1, w_in, w2, w_out, b_col, herm, herm_t,
-    send_up, send_dn, g2, wall_o, h1, mb1, h2, mb2, da2, gb2, gsum,
-    p0, s1, p1, s2, gx, gp2,
+    send_up, send_dn, g2, wall_o, h1_h, mb1_h, mb2_h, gb2_h,
+    p0, s1, p1, s2, gx, gp2, h1, mb1, mb2, gb2, h2, da2, dm, sems,
 ):
+    moves = Copies(sems)
     depth, plane = solid.shape
     edge = REACH + 1
     mid = depth + 2 * edge
@@ -279,7 +324,7 @@
     for d in range(1, REACH + 1):
         wall_o[edge - d : edge - d + 1, :] = below[row + d - 1 : row + d, :]
         wall_o[edge + depth + d - 1 : edge + depth + d, :] = above[row + d - 1 : row + d, :]
-    wall_ext = wall_o[...]
+    wall_ext = wall_o[0:mid, :]
     wall = wall_o[edge : edge + depth, :]
 
     for q in range(Q):
@@ -299,14 +344,19 @@
         bounced = get_rows(p0, OPP[q], ext, 8 - edge, mid)
         put_rows(s1, q, mid, 0, jnp.where(wall_ext > 0.5, bounced, moved))
     clear_pad(s1, mid)
-    for i in range(1, mid - 1):
-        lanes = slice((i - 1) * plane, i * plane)
-        x = get_layer(s1, i, mid)
-        mb = moments_of(x, herm[...])
-        mb1[:, lanes] = mb
-        hidden_into(h1, lanes, w1, mb)
-        out = x + dot(w2[...], h1[:, lanes]) + b_col[...]
-        put_layer(p1, i, mid, out[:Q])
+    def moments(n):
+        mb1[n] = moments_of(get_layer(s1, n + 1, mid), herm[...])
+
+    def hide(n):
+        hidden_into(h1.at[n], w1, mb1[n])
+        moves.start(h1.at[n], h1_h.at[n])
+
+    def finish(n):
+        out = get_layer(s1, n + 1, mid) + dot(w2[...], h1[n]) + b_col[...]
+        put_layer(p1, n + 1, mid, out[:Q])
+
+    staggered(mid - 2, moments, hide, finish)
+    moves.start(mb1, mb1_h)
 
     for q in range(Q):
         ex, ey, ez = VEL[q]
@@ -330,22 +380,33 @@
 
     total = jnp.zeros((QP, plane), F32)
     for z in range(depth):
-        lanes = slice(z * plane, (z + 1) * plane)
-        mb = moments_of(get_layer(s2, z, depth), herm[...])
-        mb2[:, lanes] = mb
-        hidden_into(h2, lanes, w1, mb)
+        mb2[z] = moments_of(get_layer(s2, z, depth), herm[...])
         gp = get_layer(gp2, z, depth)
-        gb = gp.astype(BF)
-        gb2[:, lanes] = gb
+        gb2[z] = gp.astype(BF)
         total = total + gp
-        g = adjoint_layer(gp, gb, h2, lanes, da2, lanes, w_out, w_in, herm_t[...])[:Q]
+    wall_o[mid : mid + QP, :] = total
+    moves.start(mb2, mb2_h)
+    moves.start(gb2, gb2_h)
+
+    def hide_two(z):
+        hidden_into(h2.at[z % 2], w1, mb2[z])
+
+    def act(z):
+        d_act_into(da2.at[z % 2], h2.at[z % 2], w_out, gb2[z])
+
+    def back(z):
+        dm[z % 2] = split_concat(dot(w_in[...], da2[z % 2]))
+
+    def finish_two(z):
+        g = (get_layer(gp2, z, depth) + dot(herm_t[...], dm[z % 2]))[:Q]
         put_layer(g2, z, depth, g)
         if z < REACH:
             send_dn[z * BLOCK : z * BLOCK + Q, :] = g
         if depth - 1 - z < REACH:
             d = depth - 1 - z
             send_up[d * BLOCK : d * BLOCK + Q, :] = g
-    gsum[...] = total
+
+    staggered(depth, hide_two, act, back, finish_two)
 
     for sign, send in ((1, send_up), (-1, send_dn)):
         row = REACH * BLOCK
@@ -354,23 +415,48 @@
             open_cells = 1.0 - wall_o[edge + z : edge + z + 1, :]
             send[row : row + 1, :] = get_rows(g2, q, depth, z, 1) * open_cells
             row += 1
-
-
-def sums_kernel(mb2, da2, gb2, h2, acc):
-    acc[0:MP, :] = dot_nt(mb2[...], da2[...])
-    acc[MP : MP + QP, :] = dot_nt(gb2[...], h2[...])
+    moves.wait()
+
+
+def sums_kernel(
+    mb2_h, gb2_h, mb0_h, mb1_h, h1_h, w1, w_out, acc, h0, mb0, h1, mb1, mb2, gb2, h2, da2, sems
+):
+    moves = Copies(sems)
+    pairs = ((mb2_h, mb2), (gb2_h, gb2), (mb0_h, mb0), (mb1_h, mb1), (h1_h, h1))
+    copies = [moves.start(source, target) for source, target in pairs]
+    acc[...] = jnp.zeros(acc.shape, F32)
+    for copy in copies[:3]:
+        copy.wait()
+
+    def hide(z):
+        hidden_into(h2.at[z % 3], w1, mb2[z])
+
+    def act(z):
+        d_act_into(da2.at[z % 2], h2.at[z % 3], w_out, gb2[z])
+
+    def add(z):
+        add_sums(acc, mb2[z], da2.at[z % 2], gb2[z], h2.at[z % 3])
+
+    def hide_first(z):
+        hidden_into(h0.at[z], w1, mb0[z])
+
+    staggered(mb2.shape[0], hide, act, add, hide_first)
+    for copy in copies[3:]:
+        copy.wait()
 
 
 def third_kernel(
-    g2, below, above, wall_i, h1, mb1, h0, mb0, acc, gsum, w_in, w_out, herm_t,
+    g2, below, above, wall_i, h1, mb1, h0, mb0, acc_i, w_in, w_out, herm_t,
     d_field, sums,
-    gx, raw, gp1, g1, raw1, gp0, da1, da0, gb1, gb0, out0,
+    gx, raw, gp1, g1, raw1, gp0, out0, gb, da, dm, acc,
 ):
-    mid, plane = wall_i.shape
+    plane = wall_i.shape[1]
+    mid = wall_i.shape[0] - QP
     edge = REACH + 1
     depth = mid - 2 * edge
     ext = depth + 16
-    wall_ext = wall_i[...]
+    acc[...] = acc_i[...]
+    wall_ext = wall_i[0:mid, :]
     open_ext = 1.0 - wall_ext
     wall = wall_i[edge : edge + depth, :]
 
@@ -392,17 +478,28 @@
         put_rows(gp1, q, mid, 0, moved + wall_ext * get_rows(raw, OPP[q], mid, 0, mid))
     clear_pad(gp1, mid)
 
-    total = gsum[...]
-    for i in range(1, mid - 1):
-        lanes = slice((i - 1) * plane, i * plane)
-        gp = get_layer(gp1, i, mid)
-        gb = gp.astype(BF)
-        if edge <= i < edge + depth:
-            gb1[:, (i - edge) * plane : (i - edge + 1) * plane] = gb
-            total = total + gp
-        g = adjoint_layer(gp, gb, h1, lanes, da1, lanes, w_out, w_in, herm_t[...])[:Q]
+    total = wall_i[mid : mid + QP, :]
+    for i in range(edge, edge + depth):
+        total = total + get_layer(gp1, i, mid)
+
+    def act_one(n):
+        gb[n % 4] = get_layer(gp1, n + 1, mid).astype(BF)
+        d_act_into(da.at[n % 4], h1.at[n], w_out, gb[n % 4])
+
+    def back(n):
+        dm[n % 2] = split_concat(dot(w_in[...], da[n % 4]))
+
+    def finish_one(n):
+        i = n + 1
+        g = (get_layer(gp1, i, mid) + dot(herm_t[...], dm[n % 2]))[:Q]
         put_layer(raw1, i, mid, g)
         put_layer(g1, i, mid, g * open_ext[i : i + 1, :])
+
+    def add_one(n):
+        if edge <= n + 1 < edge + depth:
+            add_sums(acc, mb1[n], da.at[n % 4], gb[n % 4], h1.at[n])
+
+    staggered(mid - 2, act_one, back, finish_one, add_one)
 
     for q in range(Q):
         ex, ey, ez = VEL[q]
@@ -410,21 +507,25 @@
         put_rows(gp0, q, depth, 0, moved + wall * get_rows(raw1, OPP[q], mid, edge, depth))
     clear_pad(gp0, depth)
     for z in range(depth):
-        lanes = slice(z * plane, (z + 1) * plane)
-        gp = get_layer(gp0, z, depth)
-        gb = gp.astype(BF)
-        gb0[:, lanes] = gb
-        total = total + gp
-        g = adjoint_layer(gp, gb, h0, lanes, da0, lanes, w_out, w_in, herm_t[...])[:Q]
+        total = total + get_layer(gp0, z, depth)
+
+    def act_two(z):
+        gb[z % 4] = get_layer(gp0, z, depth).astype(BF)
+        d_act_into(da.at[z % 4], h0.at[z], w_out, gb[z % 4])
+
+    def finish_two(z):
+        g = (get_layer(gp0, z, depth) + dot(herm_t[...], dm[z % 2]))[:Q]
         put_layer(out0, z, depth, g)
+
+    def add_two(z):
+        add_sums(acc, mb0[z], da.at[z % 4], gb[z % 4], h0.at[z])
+
+    staggered(depth, act_two, back, finish_two, add_two)
     for q in range(Q):
         d_field[q * depth : (q + 1) * depth, :] = get_rows(out0, q, depth, 0, depth)
 
-    own = slice(REACH * plane, (REACH + depth) * plane)
-    part = acc[0:MP, :] + dot_nt(mb1[:, own], da1[:, own]) + dot_nt(mb0[...], da0[...])
-    sums[0:24, :] = part[0:24, :]
-    part = acc[MP : MP + QP, :] + dot_nt(gb1[...], h1[:, own]) + dot_nt(gb0[...], h0[...])
-    sums[24 : 24 + Q + 1, :] = part[0 : Q + 1, :]
+    sums[0:24, :] = acc[0:24, :]
+    sums[24 : 24 + Q + 1, :] = acc[MP : MP + Q + 1, :]
     line = dot_nt(jnp.ones((8, plane), F32), total, lax.Precision.HIGHEST)
     sums[MOM + 1 : MOM + 2, 0:QP] = line[0:1, :]
 
@@ -436,22 +537,34 @@
     g_w_in[...] = low[:MOM, :]
     g_b_in[...] = low[MOM : MOM + 1, :]
     g_b_out[...] = low[MOM + 1 : MOM + 2, :Q]
-    turned = jnp.concatenate([low[24:, :], high], axis=0).T
-    g_w_out[...] = turned[:, :Q]
-
-
-def call(kernel, outs, scratch, args, flops, smem=()):
+    g_w_out[0:8, :] = low[24:, :]
+    g_w_out[8:Q, :] = high[: Q - 8, :]
+
+
+def call(kernel, outs, scratch, args, flops, limit, smem=(), hbm=()):
     vmem = pl.BlockSpec(memory_space=pltpu.VMEM)
     scalars = pl.BlockSpec(memory_space=pltpu.SMEM)
+    hbm_spec = pl.BlockSpec(memory_space=pltpu.HBM)
     return pl.pallas_call(
         kernel,
-        out_shape=[jax.ShapeDtypeStruct(shape, kind) for shape, kind in outs],
-        in_specs=[scalars if n in smem else vmem for n in range(len(args))],
-        out_specs=[vmem] * len(outs),
-        scratch_shapes=[pltpu.VMEM(shape, kind) for shape, kind in scratch],
-        compiler_params=pltpu.CompilerParams(vmem_limit_bytes=28 * 1024 * 1024),
+        out_shape=[
+            out[2](out[0], out[1]) if len(out) > 2 else jax.ShapeDtypeStruct(*out) for out in outs
+        ],
+        in_specs=[
+            scalars if n in smem else hbm_spec if n in hbm else vmem for n in range(len(args))
+        ],
+        out_specs=[hbm_spec if len(out) > 2 else vmem for out in outs],
+        scratch_shapes=[
+            pltpu.VMEM(shape, kind) if kind != "sem" else pltpu.SemaphoreType.DMA(shape)
+            for shape, kind in scratch
+        ],
+        compiler_params=pltpu.CompilerParams(vmem_limit_bytes=limit * MIB),
         cost_estimate=pl.CostEstimate(flops=flops, bytes_accessed=2000000, transcendentals=0),
     )(*args)
+
+
+def outside(value):
+    return pltpu.with_memory_space_constraint(value, pltpu.HBM)
 
 
 def factor_stages(space, traj):
@@ -508,58 +621,82 @@
     def pops_buf(rows, count=QP):
         return ((2, count * rows, half), F32)
 
-    send_up, send_dn, post, h0, mb0, w1, w_in_p, w2, w_out_p, b_col = call(
+    raw = [w_in, b_in.reshape(1, hid), w_out.T, b_out.reshape(1, pops), herm, field, solid, cot]
+    raw = [outside(value) for value in raw]
+    send_up, send_dn, post, mb0, w1, w_in_p, w2, w_out_p, b_col = call(
         first_kernel,
         [
             ((SEND_ONE, plane), F32),
             ((SEND_ONE, plane), F32),
             pops_buf(depth, Q),
-            ((hid, depth * plane), BF),
-            ((MP, depth * plane), BF),
+            ((depth, MP, plane), BF, pltpu.HBM),
             ((hid, MP), BF),
             ((MP, hid), BF),
             ((QP, hid), BF),
             ((hid, QP), BF),
             ((QP, plane), F32),
         ],
-        [pops_buf(depth), ((MP, hid), F32), ((QP, hid), F32)],
-        [field, cot, solid, w_in, b_in.reshape(1, hid), w_out, b_out.reshape(1, pops), herm],
+        [pops_buf(depth), ((MP, hid), F32), ((QP, hid), F32)]
+        + [(value.shape, value.dtype) for value in raw]
+        + [((2, hid, plane), BF), ((depth, MP, plane), BF), ((len(raw) + 1,), "sem")],
+        raw,
         10**9,
+        5,
+        hbm=range(len(raw)),
     )
     below = lax.ppermute(send_up, "space", up)
     above = lax.ppermute(send_dn, "space", down)
-    send_up, send_dn, g2, wall, h1, mb1, h2, mb2, da2, gb2, gsum = call(
+    send_up, send_dn, g2, wall, h1, mb1, mb2, gb2 = call(
         second_kernel,
         [
             ((SEND_TWO, plane), F32),
             ((SEND_TWO, plane), F32),
             pops_buf(depth, Q),
-            ((mid, plane), F32),
-            ((hid, work * plane), BF),
-            ((MP, work * plane), BF),
-            ((hid, depth * plane), BF),
-            ((MP, depth * plane), BF),
-            ((hid, depth * plane), BF),
-            ((QP, depth * plane), BF),
-            ((QP, plane), F32),
-        ],
-        [pops_buf(ext), pops_buf(mid), pops_buf(mid), pops_buf(depth), pops_buf(mid), pops_buf(depth)],
+            ((mid + QP, plane), F32),
+            ((work, hid, plane), BF, pltpu.HBM),
+            ((work, MP, plane), BF, pltpu.HBM),
+            ((depth, MP, plane), BF, pltpu.HBM),
+            ((depth, QP, plane), BF, pltpu.HBM),
+        ],
+        [
+            pops_buf(ext), pops_buf(mid), pops_buf(mid), pops_buf(depth), pops_buf(mid), pops_buf(depth),
+            ((work, hid, plane), BF), ((work, MP, plane), BF), ((depth, MP, plane), BF),
+            ((depth, QP, plane), BF), ((2, hid, plane), BF), ((2, hid, plane), BF),
+            ((2, 3 * MP, plane), BF), ((work + 3,), "sem"),
+        ],
         [post, below, above, cot, solid, w1, w_in_p, w2, w_out_p, b_col, herm, herm_t],
-        3 * 10**9,
+        10**9,
+        12,
     )
     below = lax.ppermute(send_up, "space", up)
     above = lax.ppermute(send_dn, "space", down)
-    (acc,) = call(sums_kernel, [((MP + QP, hid), F32)], [], [mb2, da2, gb2, h2], 10**9)
+    acc, h0, mb0, h1, mb1 = call(
+        sums_kernel,
+        [
+            ((MP + QP, hid), F32),
+            ((depth, hid, plane), BF), ((depth, MP, plane), BF),
+            ((work, hid, plane), BF), ((work, MP, plane), BF),
+        ],
+        [
+            ((depth, MP, plane), BF), ((depth, QP, plane), BF),
+            ((3, hid, plane), BF), ((2, hid, plane), BF), ((5,), "sem"),
+        ],
+        [outside(mb2), outside(gb2), outside(mb0), outside(mb1), outside(h1), w1, w_out_p],
+        10**9,
+        4,
+        hbm=range(5),
+    )
     d_field, sums = call(
         third_kernel,
         [((pops * depth, plane), F32), ((64, hid), F32)],
         [
             pops_buf(ext), pops_buf(mid), pops_buf(mid), pops_buf(mid), pops_buf(mid), pops_buf(depth),
-            ((hid, work * plane), BF), ((hid, depth * plane), BF),
-            ((QP, depth * plane), BF), ((QP, depth * plane), BF), pops_buf(depth),
-        ],
-        [g2, below, above, wall, h1, mb1, h0, mb0, acc, gsum, w_in_p, w_out_p, herm_t],
-        3 * 10**9,
+            pops_buf(depth), ((4, QP, plane), BF),
+            ((4, hid, plane), BF), ((2, 3 * MP, plane), BF), ((MP + QP, hid), F32),
+        ],
+        [g2, below, above, wall, h1, mb1, h0, mb0, acc, w_in_p, w_out_p, herm_t],
+        10**9,
+        9,
     )
 
     core, stages = factor_stages(space, traj)
@@ -580,17 +717,18 @@
     scale = 1.0 / math.sqrt(float(cells))
     g_w_in, g_b_in, g_w_out, g_b_out = call(
         lambda *refs: last_kernel(scale, *refs),
-        [((MOM, hid), F32), ((1, hid), F32), ((hid, pops), F32), ((1, pops), F32)],
+        [((MOM, hid), F32), ((1, hid), F32), ((pops, hid), F32), ((1, pops), F32)],
         [],
         [me.reshape(1).astype(jnp.int32), mine, other],
-        10**6,
+        10**9,
+        1,
         smem=(0,),
     )
     return (
         d_field.reshape(local, pops, depth, plane),
         g_w_in,
         g_b_in.reshape(hid),
-        g_w_out,
+        g_w_out.T,
         g_b_out.reshape(pops),
     )
 

time: 75.2 us -> 51.7 us (0.69)
  local copies, waits for them, and re-layouts: 16.7 us -> 0.03 us
  Pallas kernels: 23.4 us -> 19.3 us
  starting transfers between devices: 18.9 us -> 17.4 us
    unnamed x48 -> x8, local copies, waits for them, and re-layouts: 16.7 us -> 0.02 us
    pallas_call x5, Pallas kernels: 23.4 us -> 19.3 us  [call(): pl.pallas_call(kernel, out_shape=[out[2](out[0], out[1]) if len(out) > 2...]
    ppermute x6, starting transfers between devices: 8.84 us -> 7.09 us  [per_device(): lax.ppermute(mine, axes, pairs)]
  transfers between devices with their start and end apart: 12 -> 12, of which waited for: 8 -> 9; matrix products, arithmetic and copies ran while one was open for 0% -> 0% of each run, Pallas kernels for 2% -> 8%
where the time goes in v2:
time: 51.7 us; the launch traced here: 51.6 us
  Pallas kernels  19.3 us (37%)
  starting transfers between devices  17.4 us (34%)
  waiting for transfers between devices  14 us (27%)
  between operations  0.77 us (1%)
    pallas_call x5, Pallas kernels, call(): pl.pallas_call(kernel, out_shape=[out[2](out[0], out[1]) if len(out) > 2...  19.3 us
    ppermute x2, starting transfers between devices, per_device(): above = lax.ppermute(send_dn, 'space', down)  8.65 us
    ppermute x6, waiting for transfers between devices, per_device(): lax.ppermute(mine, axes, pairs)  8.47 us
    ppermute x6, starting transfers between devices, per_device(): lax.ppermute(mine, axes, pairs)  7.09 us
    ppermute x2, waiting for transfers between devices, per_device(): below = lax.ppermute(send_up, 'space', up)  3.05 us
    ppermute x2, starting transfers between devices, per_device(): below = lax.ppermute(send_up, 'space', up)  1.58 us
    ppermute x1, waiting for transfers between devices, per_device(): other = lax.ppermute(mine, axes, swap)  1.24 us
    ppermute x1, waiting for transfers between devices, per_device(): mine = mine + lax.ppermute(other, axes, swap)  1.24 us
  transfers between devices with their start and end apart: 12, of which 9 were waited for; matrix products, arithmetic and copies ran while one was open for 0% of the time, Pallas kernels for 8%

profile of v2, /device:TPU:0, one launch (start us, length us, event | category | flops | bytes accessed | tf_op | source)
XLA Modules:
  0.0 51.6 jit_solution(15662910136227025573)
XLA Ops:
  0.6 0.0 copy-start.3
  0.6 0.0 copy-start
  0.7 0.0 copy-start.2
  0.7 0.0 copy-start.1
  0.7 2.5 %shard_map.128 = (f32[160,256]{1,0:T(8,128)S(1)}, f32[160,256]{1,0:T(8,128)S(1)}, f32[2,312,128]{2,1,0:T(8,128)S(1)}, bf16[8,32,256]{2,1,0:T(8,128)(2,1)}, bf16[...) custom-call(bf16[20,512]{1,0:T(8,128)(2,1)} %w_in_h.1, ...), custom_call_target="tpu_custom_call" | custom-call | flops 1000000000 | bytes 2000000 | tf_op jit(solution)/shard_map/pallas_call | solution.py:548
  3.2 0.5 %collective-permute-start = (f32[160,256]{1,0:T(8,128)S(1)}, f32[160,256]{1,0:T(8,128)S(1)}, u32[]{:S(2)}, u32[]{:S(2)}) collective-permute-start(f32[160,256]{1,0:T(8,128)S(1)} %get-tuple-element.34), channel_id=1, source_target_pairs={{0,2},{2,4},{4,6},{6,8},{8,10},{10,12},{12,14},{14,16},{16,18},{18... | collective-permute-start | bytes 491528 | tf_op jit(solution)/shard_map/ppermute | solution.py:647
  3.7 5.0 %collective-permute-start.1 = (f32[160,256]{1,0:T(8,128)S(1)}, f32[160,256]{1,0:T(8,128)S(1)}, u32[]{:S(2)}, u32[]{:S(2)}) collective-permute-start(f32[160,256]{1,0:T(8,128)S(1)} %get-tuple-element.35), channel_id=1, source_target_pairs={{2,0},{4,2},{6,4},{8,6},{10,8},{12,10},{14,12},{16,14},{18,16},{20... | collective-permute-start | bytes 491528 | tf_op jit(solution)/shard_map/ppermute | solution.py:648
  8.8 3.0 %collective-permute-done.below = f32[160,256]{1,0:T(8,128)S(1)} collective-permute-done((f32[160,256]{1,0:T(8,128)S(1)}, f32[160,256]{1,0:T(8,128)S(1)}, u32[]{:S(2)}, u32[]{:S(2)}) %collective-permute-start) | collective-permute-done | bytes 163872 | tf_op jit(solution)/shard_map/ppermute | solution.py:647
  11.8 0.0 collective-permute-done.1.above
  11.8 0.0 copy-done.3
  11.8 0.0 copy-done
  11.8 0.0 copy-done.2
  11.9 0.0 copy-done.1
  11.9 5.2 %shard_map.129 = (f32[144,256]{1,0:T(8,128)S(1)}, f32[144,256]{1,0:T(8,128)S(1)}, f32[2,312,128]{2,1,0:T(8,128)S(1)}, f32[64,256]{1,0:T(8,128)S(1)}, bf16[14,512...) custom-call(f32[2,312,128]{2,1,0:T(8,128)S(1)} %get-tuple-element.33, ...), custom_call_target="tpu_custom_call" | custom-call | flops 1000000000 | bytes 2000000 | tf_op jit(solution)/shard_map/pallas_call | solution.py:548
  17.1 1.1 %collective-permute-start.2 = (f32[144,256]{1,0:T(8,128)S(1)}, f32[144,256]{1,0:T(8,128)S(1)}, u32[]{:S(2)}, u32[]{:S(2)}) collective-permute-start(f32[144,256]{1,0:T(8,128)S(1)} %get-tuple-element.42), channel_id=1, source_target_pairs={{0,2},{2,4},{4,6},{6,8},{8,10},{10,12},{12,14},{14,16},{16,18},{18... | collective-permute-start | bytes 442376 | tf_op jit(solution)/shard_map/ppermute | solution.py:671
  18.2 3.6 %collective-permute-start.3 = (f32[144,256]{1,0:T(8,128)S(1)}, f32[144,256]{1,0:T(8,128)S(1)}, u32[]{:S(2)}, u32[]{:S(2)}) collective-permute-start(f32[144,256]{1,0:T(8,128)S(1)} %get-tuple-element.43), channel_id=1, source_target_pairs={{2,0},{4,2},{6,4},{8,6},{10,8},{12,10},{14,12},{16,14},{18,16},{20... | collective-permute-start | bytes 442376 | tf_op jit(solution)/shard_map/ppermute | solution.py:672
  21.8 4.2 %shard_map.130 = (f32[80,512]{1,0:T(8,128)S(1)}, bf16[8,512,256]{2,1,0:T(8,128)(2,1)S(1)}, bf16[8,32,256]{2,1,0:T(8,128)(2,1)S(1)}, bf16[14,512,256]{2,1,0:T(8,128)(2,1)S(1)}, bf16[14,32,256]{2,1,0:T(8,128)(2,1)S(1)}) custom-call(bf16[8,32,256]{2,1,0:T(8,128)(2,1)} %get-tuple-element.45.mb2_h, bf16[8,48,256]{2,1,0:T(8,128)(2,1)} %get-tuple-element.46.gb2_h, ...), custom_call_target="tpu_custom_call" | custom-call | flops 1000000000 | bytes 2000000 | tf_op jit(solution)/shard_map/pallas_call | solution.py:548
  26.0 0.0 collective-permute-done.2.below
  26.0 0.0 collective-permute-done.3.above
  26.0 6.7 %shard_map.131 = (f32[312,256]{1,0:T(8,128)}, f32[64,512]{1,0:T(8,128)S(1)}) custom-call(f32[2,312,128]{2,1,0:T(8,128)S(1)} %get-tuple-element.41.g2, f32[144,256]{1,0:T(8,128)S(1)} %collective-permute-done.2.below, f32[144,256]{1,0:T(8,128)S(1)} %collective-permute-done.3.above, f32[64,256]{1,0:T(8,128)S(1)} %get-tuple-element.44.wall_i, ...), custom_call_target="tpu_custom_call" | custom-call | flops 1000000000 | bytes 2000000 | tf_op jit(solution)/shard_map/pallas_call | solution.py:548
  32.7 0.0 collective-permute-start.4
  32.7 1.2 %collective-permute-done.4 = f32[32,512]{1,0:T(8,128)S(1)} collective-permute-done((f32[32,512]{1,0:T(8,128)S(1)}, f32[32,512]{1,0:T(8,128)S(1)}, u32[]{:S(2)}, u32[]{:S(2)}) %collective-permute-start.4) | collective-permute-done | bytes 65568 | tf_op jit(solution)/shard_map/ppermute | solution.py:709
  33.9 0.1 collective-permute-start.7
  34.0 1.9 %collective-permute-start.6 = (f32[32,512]{1,0:T(8,128)S(1)}, f32[32,512]{1,0:T(8,128)S(1)}, u32[]{:S(2)}, u32[]{:S(2)}) collective-permute-start(f32[32,512]{1,0:T(8,128)S(1)} %dynamic-slice_add_fusion), channel_id=1, source_target_pairs={{0,1},{1,0},{2,3},{3,2},{4,5},{5,4},{6,7},{7,6},{8,9},{9,8},{10,11... | collective-permute-start | bytes 196616 | tf_op jit(solution)/shard_map/ppermute | solution.py:711
  36.0 1.5 %collective-permute-start.5 = (f32[32,512]{1,0:T(8,128)S(1)}, f32[32,512]{1,0:T(8,128)S(1)}, u32[]{:S(2)}, u32[]{:S(2)}) collective-permute-start(f32[32,512]{1,0:T(8,128)S(1)} %dynamic-slice_add_fusion), channel_id=1, source_target_pairs={{0,4},{1,5},{2,6},{3,7},{4,0},{5,1},{6,2},{7,3},{8,12},{9,13},{10,... | collective-permute-start | bytes 196616 | tf_op jit(solution)/shard_map/ppermute | solution.py:711
  37.5 1.8 %collective-permute-done.7 = f32[32,512]{1,0:T(8,128)S(1)} collective-permute-done((f32[32,512]{1,0:T(8,128)S(1)}, f32[32,512]{1,0:T(8,128)S(1)}, u32[]{:S(2)}, u32[]{:S(2)}) %collective-permute-start.7) | collective-permute-done | bytes 65568 | tf_op jit(solution)/shard_map/ppermute | solution.py:711
  39.3 0.4 collective-permute-done.6
  39.7 0.8 %collective-permute-done.5 = f32[32,512]{1,0:T(8,128)S(1)} collective-permute-done((f32[32,512]{1,0:T(8,128)S(1)}, f32[32,512]{1,0:T(8,128)S(1)}, u32[]{:S(2)}, u32[]{:S(2)}) %collective-permute-start.5) | collective-permute-done | bytes 65568 | tf_op jit(solution)/shard_map/ppermute | solution.py:711
  40.6 2.9 %collective-permute-start.10 = (f32[32,512]{1,0:T(8,128)S(1)}, f32[32,512]{1,0:T(8,128)S(1)}, u32[]{:S(2)}, u32[]{:S(2)}) collective-permute-start(f32[32,512]{1,0:T(8,128)S(1)} %add_add_fusion.1), channel_id=1, source_target_pairs={{0,24},{1,25},{2,26},{3,27},{4,28},{5,29},{6,30},{7,31},{8,0},{9,1... | collective-permute-start | bytes 196616 | tf_op jit(solution)/shard_map/ppermute | solution.py:711
  43.5 0.0 collective-permute-start.9
  43.5 0.6 %collective-permute-start.8 = (f32[32,512]{1,0:T(8,128)S(1)}, f32[32,512]{1,0:T(8,128)S(1)}, u32[]{:S(2)}, u32[]{:S(2)}) collective-permute-start(f32[32,512]{1,0:T(8,128)S(1)} %add_add_fusion.1), channel_id=1, source_target_pairs={{0,8},{1,9},{2,10},{3,11},{4,12},{5,13},{6,14},{7,15},{8,16},{9,17... | collective-permute-start | bytes 196616 | tf_op jit(solution)/shard_map/ppermute | solution.py:711
  44.1 1.3 %collective-permute-done.10 = f32[32,512]{1,0:T(8,128)S(1)} collective-permute-done((f32[32,512]{1,0:T(8,128)S(1)}, f32[32,512]{1,0:T(8,128)S(1)}, u32[]{:S(2)}, u32[]{:S(2)}) %collective-permute-start.10) | collective-permute-done | bytes 65568 | tf_op jit(solution)/shard_map/ppermute | solution.py:711
  45.4 3.4 %collective-permute-done.9 = f32[32,512]{1,0:T(8,128)S(1)} collective-permute-done((f32[32,512]{1,0:T(8,128)S(1)}, f32[32,512]{1,0:T(8,128)S(1)}, u32[]{:S(2)}, u32[]{:S(2)}) %collective-permute-start.9) | collective-permute-done | bytes 65568 | tf_op jit(solution)/shard_map/ppermute | solution.py:711
  48.8 0.7 %collective-permute-done.8 = f32[32,512]{1,0:T(8,128)S(1)} collective-permute-done((f32[32,512]{1,0:T(8,128)S(1)}, f32[32,512]{1,0:T(8,128)S(1)}, u32[]{:S(2)}, u32[]{:S(2)}) %collective-permute-start.8) | collective-permute-done | bytes 65568 | tf_op jit(solution)/shard_map/ppermute | solution.py:711
  49.6 0.1 collective-permute-start.11
  49.6 1.2 %collective-permute-done.11.refs_2_ = f32[32,512]{1,0:T(8,128)S(1)} collective-permute-done((f32[32,512]{1,0:T(8,128)S(1)}, f32[32,512]{1,0:T(8,128)S(1)}, u32[]{:S(2)}, u32[]{:S(2)}) %collective-permute-start.11) | collective-permute-done | bytes 65568 | tf_op jit(solution)/shard_map/ppermute | solution.py:714
  50.9 0.7 %shard_map.132 = (f32[20,512]{1,0:T(8,128)}, f32[1,512]{1,0:T(1,128)}, f32[39,512]{1,0:T(8,128)}, f32[1,39]{1,0:T(1,128)}) custom-call(s32[1]{0:T(128)} %bitcast.7.refs_0_, f32[32,512]{1,0:T(8,128)S(1)} %add_add_fusion.refs_1_, f32[32,512]{1,0:T(8,128)S(1)} %collective-permute-done.11.refs_2_), custom_call_target="tpu_custom_call" | custom-call | flops 1000000000 | bytes 2000000 | tf_op jit(solution)/shard_map/pallas_call | solution.py:548
  (4 shorter events, 0.1 us)
Async XLA Ops:
  0.6 11.2 %copy-start.3 = (bf16[32,144]{1,0:T(8,128)(2,1)S(1)}, bf16[32,144]{1,0:T(8,128)(2,1)}, u32[]{:S(2)}) copy-start(bf16[32,144]{1,0:T(8,128)(2,1)} %constant.29.clone.herm_h.herm) | copy-start | bytes 27652
  0.6 11.2 %copy-start = (bf16[48,96]{1,0:T(8,128)(2,1)S(1)}, bf16[48,96]{1,0:T(8,128)(2,1)}, u32[]{:S(2)}) copy-start(bf16[48,96]{1,0:T(8,128)(2,1)} %constant.30.clone.herm_t) | copy-start | bytes 27652
  0.7 11.2 %copy-start.2 = (s32[1,8,256]{2,1,0:T(8,128)S(1)}, s32[1,8,256]{2,1,0:T(8,128)}, u32[]{:S(2)}) copy-start(s32[1,8,256]{2,1,0:T(8,128)} %param.10) | copy-start | bytes 24580
  0.7 11.2 %copy-start.1 = (f32[1,39,8,256]{3,2,1,0:T(8,128)S(1)}, f32[1,39,8,256]{3,2,1,0:T(8,128)}, u32[]{:S(2)}) copy-start(f32[1,39,8,256]{3,2,1,0:T(8,128)} %param.11) | copy-start | bytes 958468
  3.2 8.6 %collective-permute-start = (f32[160,256]{1,0:T(8,128)S(1)}, f32[160,256]{1,0:T(8,128)S(1)}, u32[]{:S(2)}, u32[]{:S(2)}) collective-permute-start(f32[160,256]{1,0:T(8,128)S(1)} %get-tuple-element.34), channel_id=1, source_target_pairs={{0,2},{2,4},{4,6},{6,8},{8,10},{10,12},{12,14},{14,16},{16,18},{18... | collective-permute-start | bytes 491528 | tf_op jit(solution)/shard_map/ppermute | solution.py:647
  3.7 8.1 %collective-permute-start.1 = (f32[160,256]{1,0:T(8,128)S(1)}, f32[160,256]{1,0:T(8,128)S(1)}, u32[]{:S(2)}, u32[]{:S(2)}) collective-permute-start(f32[160,256]{1,0:T(8,128)S(1)} %get-tuple-element.35), channel_id=1, source_target_pairs={{2,0},{4,2},{6,4},{8,6},{10,8},{12,10},{14,12},{16,14},{18,16},{20... | collective-permute-start | bytes 491528 | tf_op jit(solution)/shard_map/ppermute | solution.py:648
  17.1 8.9 %collective-permute-start.2 = (f32[144,256]{1,0:T(8,128)S(1)}, f32[144,256]{1,0:T(8,128)S(1)}, u32[]{:S(2)}, u32[]{:S(2)}) collective-permute-start(f32[144,256]{1,0:T(8,128)S(1)} %get-tuple-element.42), channel_id=1, source_target_pairs={{0,2},{2,4},{4,6},{6,8},{8,10},{10,12},{12,14},{14,16},{16,18},{18... | collective-permute-start | bytes 442376 | tf_op jit(solution)/shard_map/ppermute | solution.py:671
  18.2 7.8 %collective-permute-start.3 = (f32[144,256]{1,0:T(8,128)S(1)}, f32[144,256]{1,0:T(8,128)S(1)}, u32[]{:S(2)}, u32[]{:S(2)}) collective-permute-start(f32[144,256]{1,0:T(8,128)S(1)} %get-tuple-element.43), channel_id=1, source_target_pairs={{2,0},{4,2},{6,4},{8,6},{10,8},{12,10},{14,12},{16,14},{18,16},{20... | collective-permute-start | bytes 442376 | tf_op jit(solution)/shard_map/ppermute | solution.py:672
  32.7 1.3 %collective-permute-start.4 = (f32[32,512]{1,0:T(8,128)S(1)}, f32[32,512]{1,0:T(8,128)S(1)}, u32[]{:S(2)}, u32[]{:S(2)}) collective-permute-start(f32[32,512]{1,0:T(8,128)S(1)} %constant_dynamic-slice_fusion), channel_id=1, source_target_pairs={{0,2},{1,3},{2,0},{3,1},{4,6},{5,7},{6,4},{7,5},{8,10},{9,11},{10,... | collective-permute-start | bytes 196616 | tf_op jit(solution)/shard_map/ppermute | solution.py:709
  33.9 5.3 %collective-permute-start.7 = (f32[32,512]{1,0:T(8,128)S(1)}, f32[32,512]{1,0:T(8,128)S(1)}, u32[]{:S(2)}, u32[]{:S(2)}) collective-permute-start(f32[32,512]{1,0:T(8,128)S(1)} %dynamic-slice_add_fusion), channel_id=1, source_target_pairs={{0,5},{1,4},{2,7},{3,6},{4,1},{5,0},{6,3},{7,2},{8,13},{9,12},{10,... | collective-permute-start | bytes 196616 | tf_op jit(solution)/shard_map/ppermute | solution.py:711
  34.0 5.7 %collective-permute-start.6 = (f32[32,512]{1,0:T(8,128)S(1)}, f32[32,512]{1,0:T(8,128)S(1)}, u32[]{:S(2)}, u32[]{:S(2)}) collective-permute-start(f32[32,512]{1,0:T(8,128)S(1)} %dynamic-slice_add_fusion), channel_id=1, source_target_pairs={{0,1},{1,0},{2,3},{3,2},{4,5},{5,4},{6,7},{7,6},{8,9},{9,8},{10,11... | collective-permute-start | bytes 196616 | tf_op jit(solution)/shard_map/ppermute | solution.py:711
  36.0 4.6 %collective-permute-start.5 = (f32[32,512]{1,0:T(8,128)S(1)}, f32[32,512]{1,0:T(8,128)S(1)}, u32[]{:S(2)}, u32[]{:S(2)}) collective-permute-start(f32[32,512]{1,0:T(8,128)S(1)} %dynamic-slice_add_fusion), channel_id=1, source_target_pairs={{0,4},{1,5},{2,6},{3,7},{4,0},{5,1},{6,2},{7,3},{8,12},{9,13},{10,... | collective-permute-start | bytes 196616 | tf_op jit(solution)/shard_map/ppermute | solution.py:711
  40.6 4.8 %collective-permute-start.10 = (f32[32,512]{1,0:T(8,128)S(1)}, f32[32,512]{1,0:T(8,128)S(1)}, u32[]{:S(2)}, u32[]{:S(2)}) collective-permute-start(f32[32,512]{1,0:T(8,128)S(1)} %add_add_fusion.1), channel_id=1, source_target_pairs={{0,24},{1,25},{2,26},{3,27},{4,28},{5,29},{6,30},{7,31},{8,0},{9,1... | collective-permute-start | bytes 196616 | tf_op jit(solution)/shard_map/ppermute | solution.py:711
  43.5 5.3 %collective-permute-start.9 = (f32[32,512]{1,0:T(8,128)S(1)}, f32[32,512]{1,0:T(8,128)S(1)}, u32[]{:S(2)}, u32[]{:S(2)}) collective-permute-start(f32[32,512]{1,0:T(8,128)S(1)} %add_add_fusion.1), channel_id=1, source_target_pairs={{0,16},{1,17},{2,18},{3,19},{4,20},{5,21},{6,22},{7,23},{8,24},{9,... | collective-permute-start | bytes 196616 | tf_op jit(solution)/shard_map/ppermute | solution.py:711
  43.5 6.1 %collective-permute-start.8 = (f32[32,512]{1,0:T(8,128)S(1)}, f32[32,512]{1,0:T(8,128)S(1)}, u32[]{:S(2)}, u32[]{:S(2)}) collective-permute-start(f32[32,512]{1,0:T(8,128)S(1)} %add_add_fusion.1), channel_id=1, source_target_pairs={{0,8},{1,9},{2,10},{3,11},{4,12},{5,13},{6,14},{7,15},{8,16},{9,17... | collective-permute-start | bytes 196616 | tf_op jit(solution)/shard_map/ppermute | solution.py:711
  49.6 1.3 %collective-permute-start.11 = (f32[32,512]{1,0:T(8,128)S(1)}, f32[32,512]{1,0:T(8,128)S(1)}, u32[]{:S(2)}, u32[]{:S(2)}) collective-permute-start(f32[32,512]{1,0:T(8,128)S(1)} %add_add_fusion.refs_1_), channel_id=1, source_target_pairs={{0,2},{1,3},{2,0},{3,1},{4,6},{5,7},{6,4},{7,5},{8,10},{9,11},{10,... | collective-permute-start | bytes 196616 | tf_op jit(solution)/shard_map/ppermute | solution.py:714

commit v3 on v2

--- a/solution.py
+++ b/solution.py
@@ -234,10 +234,11 @@
 
 
 def first_kernel(
-    w_in_h, b_in_h, w_out_h, b_out_h, herm_h, field_h, solid_h, cot_h,
-    send_up, send_dn, post, mb0_h, w1_o, w_in_o, w2_o, w_out_o, b_col_o,
-    state, wide, tall, w_in, b_in, w_out, b_out, herm, field, solid, cot, h, mb0, sems,
+    core, w_in_h, b_in_h, w_out_h, b_out_h, herm_h, field_h, solid_h, cot_h,
+    send_on, send_off, post, mb0_h, w1_o, w2_o, b_col_o,
+    state, wide, tall, w_in, b_in, w_out, b_out, herm, field, solid, cot, h, mb0, ways, sems,
 ):
+    send_up, send_dn = ways.at[0], ways.at[1]
     sources = (w_in_h, b_in_h, w_out_h, b_out_h, herm_h, field_h, solid_h, cot_h)
     targets = (w_in, b_in, w_out, b_out, herm, field, solid, cot)
     moves = Copies(sems)
@@ -249,7 +250,6 @@
         copy.wait()
     wide[...] = jnp.zeros(wide.shape, F32)
     wide[:MOM, :] = w_in[...].astype(F32)
-    w_in_o[...] = wide[...].astype(BF)
     rest = b_in[...]
     for part in range(3):
         piece = rest.astype(BF).astype(F32)
@@ -259,7 +259,6 @@
     tall[...] = jnp.zeros(tall.shape, F32)
     tall[:Q, :] = w_out[...].astype(F32)
     w2_o[...] = tall[...].astype(BF)
-    w_out_o[...] = tall[...].T.astype(BF)
     tall[0:8, :] = jnp.zeros((8, hid), F32)
     tall[0:1, 0:Q] = b_out[...]
     column = tall[0:8, 0:128].T
@@ -275,10 +274,10 @@
     moves.start(mb0, mb0_h)
 
     def hide(z):
-        hidden_into(h.at[z % 2], w1_o, mb0[z])
+        hidden_into(h.at[z], w1_o, mb0[z])
 
     def finish(z):
-        out = get_layer(state, z, depth) + dot(w2_o[...], h[z % 2]) + b_col_o[...]
+        out = get_layer(state, z, depth) + dot(w2_o[...], h[z]) + b_col_o[...]
         out = out[:Q]
         put_layer(post, z, depth, out)
         if z < REACH:
@@ -305,58 +304,176 @@
         for d in range(1, REACH + 1):
             send[row : row + 1, :] = wall[layer(d) : layer(d) + 1, :]
             row += 1
+    send_on[...] = ways[core[0]]
+    send_off[...] = ways[1 - core[0]]
     moves.wait()
 
 
-def second_kernel(
-    post, below, above, cot, solid, w1, w_in, w2, w_out, b_col, herm, herm_t,
-    send_up, send_dn, g2, wall_o, h1_h, mb1_h, mb2_h, gb2_h,
-    p0, s1, p1, s2, gx, gp2, h1, mb1, mb2, gb2, h2, da2, dm, sems,
+def between_kernel(
+    w_in_h, w_out_h, mb0_h, w1, h0_h, w_in_o, w_out_o, w_in, w_out, mb0, h0, wide, tall, sems
 ):
     moves = Copies(sems)
+    copies = [moves.start(a, b) for a, b in ((mb0_h, mb0), (w_in_h, w_in), (w_out_h, w_out))]
+    moves.open = []
+    copies[0].wait()
+    for z in range(mb0.shape[0]):
+        hidden_into(h0.at[z], w1, mb0[z])
+        moves.start(h0.at[z], h0_h.at[z])
+    for copy in copies[1:]:
+        copy.wait()
+    wide[...] = jnp.zeros(wide.shape, F32)
+    wide[:MOM, :] = w_in[...].astype(F32)
+    w_in_o[...] = wide[...].astype(BF)
+    tall[...] = jnp.zeros(tall.shape, F32)
+    tall[:Q, :] = w_out[...].astype(F32)
+    w_out_o[...] = tall[...].T.astype(BF)
+    moves.wait()
+
+
+def by_side(core, run):
+    for place, side in ((0, 1), (1, -1)):
+        pl.when(core[0] == place)(lambda side=side: run(side))
+
+
+def near_layers(side, depth):
+    edge = REACH + 1
+    return (edge + REACH, 2 * edge + depth - 1) if side > 0 else (1, edge + depth - REACH)
+
+
+def far_layers(side, depth):
+    edge = REACH + 1
+    return (1, edge + REACH) if side > 0 else (edge + depth - REACH, 2 * edge + depth - 1)
+
+
+def fill_wall(wall, solid, below, above):
+    depth = solid.shape[0]
+    edge = REACH + 1
+    wall[...] = jnp.zeros(wall.shape, F32)
+    wall[edge : edge + depth, :] = solid[...].astype(F32)
+    row = REACH * BLOCK + 2 * N_REACH
+    for d in range(1, REACH + 1):
+        if below is not None:
+            wall[edge - d : edge - d + 1, :] = below[row + d - 1 : row + d, :]
+        if above is not None:
+            wall[edge + depth + d - 1 : edge + depth + d, :] = above[row + d - 1 : row + d, :]
+
+
+def fill_blocks(buf, zero_row, stride, below, above, depth):
+    for d in range(1, REACH + 1):
+        rows = slice((d - 1) * BLOCK, (d - 1) * BLOCK + Q)
+        if below is not None:
+            put_layer(buf, zero_row - d, stride, below[rows, :])
+        if above is not None:
+            put_layer(buf, zero_row + depth - 1 + d, stride, above[rows, :])
+
+
+def fill_single(buf, zero_row, stride, below, above, depth, row, sign, beyond):
+    if below is not None:
+        for n, (k, q) in enumerate(reaching(sign)):
+            put_rows(buf, q, stride, zero_row - beyond - k, below[row + n : row + n + 1, :])
+    if above is not None:
+        for n, (k, q) in enumerate(reaching(-sign)):
+            put_rows(buf, q, stride, zero_row + depth - 1 + beyond + k, above[row + n : row + n + 1, :])
+
+
+def fill_post(p0, post, below, above, depth):
+    ext = depth + 16
+    for q in range(Q):
+        put_rows(p0, q, ext, 8, get_rows(post, q, depth, 0, depth))
+    fill_blocks(p0, 8, ext, below, above, depth)
+    fill_single(p0, 8, ext, below, above, depth, REACH * BLOCK, 1, REACH)
+
+
+def stream_post(target, rows, p0, wall, base, depth):
+    ext = depth + 16
+    start = 8 - REACH - 1 + base
+    solid = wall[base : base + rows, :] > 0.5
+    for q in range(Q):
+        ex, ey, ez = VEL[q]
+        moved = roll_plane(get_rows(p0, q, ext, start - ez, rows), ex, ey)
+        bounced = get_rows(p0, OPP[q], ext, start, rows)
+        put_rows(target, q, rows, 0, jnp.where(solid, bounced, moved))
+    clear_pad(target, rows)
+
+
+def collide_layers(first, last, s1, rows, base, p1, h1, mb1, w1, w2, b_col, herm, after):
+    def moments(n):
+        mb1[n] = moments_of(get_layer(s1, first + n - base, rows), herm[...])
+
+    def hide(n):
+        hidden_into(h1.at[n], w1, mb1[n])
+        after(n)
+
+    def finish(n):
+        out = get_layer(s1, first + n - base, rows) + dot(w2[...], h1[n]) + b_col[...]
+        p1(first + n, out[:Q])
+
+    staggered(last - first, moments, hide, finish)
+
+
+def near_kernel(
+    core, post, on, solid, w1, w2, b_col, herm,
+    p1, h1_h, mb1_h,
+    p0, s1, wall, h1, mb1, sems,
+):
+    depth = solid.shape[0]
+    mid = depth + 2 * REACH + 2
+    count = h1.shape[0]
+    copies = [pltpu.make_async_copy(h1.at[n], h1_h.at[n], sems.at[n]) for n in range(count)]
+    last_copy = pltpu.make_async_copy(mb1, mb1_h, sems.at[count])
+
+    def run(side):
+        below, above = (None, on) if side > 0 else (on, None)
+        fill_wall(wall, solid, below, above)
+        fill_post(p0, post, below, above, depth)
+        stream_post(s1, mid, p0, wall, 0, depth)
+        first, last = near_layers(side, depth)
+        collide_layers(
+            first, last, s1, mid, 0, lambda i, out: put_layer(p1, i, mid, out),
+            h1, mb1, w1, w2, b_col, herm, lambda n: copies[n].start(),
+        )
+
+    by_side(core, run)
+    last_copy.start()
+    for copy in copies:
+        copy.wait()
+    last_copy.wait()
+
+
+def second_kernel(
+    core, post, on, off, cot, solid, p1_near, w1, w_in, w2, w_out, b_col, herm, herm_t,
+    send_on, send_off, g2, wall_o, h1_h, mb1_h, mb2_h, gb2_h,
+    p0, s1, p1, s2, gx, gp2, h1, mb1, mb2, gb2, h2, da2, dm, ways, sems,
+):
+    moves = Copies(sems)
+    send_up, send_dn = ways.at[0], ways.at[1]
     depth, plane = solid.shape
     edge = REACH + 1
     mid = depth + 2 * edge
-    ext = depth + 16
-    wall_o[...] = jnp.zeros(wall_o.shape, F32)
-    wall_o[edge : edge + depth, :] = solid[...].astype(F32)
-    row = REACH * BLOCK + 2 * N_REACH
-    for d in range(1, REACH + 1):
-        wall_o[edge - d : edge - d + 1, :] = below[row + d - 1 : row + d, :]
-        wall_o[edge + depth + d - 1 : edge + depth + d, :] = above[row + d - 1 : row + d, :]
-    wall_ext = wall_o[0:mid, :]
+    some = s1.shape[1] // QP
+    wall_ext = wall_o.at[0:mid, :]
+    for q in range(Q):
+        put_rows(p1, q, mid, 0, get_rows(p1_near, q, mid, 0, mid))
+
+    def run(side):
+        below, above = (off, on) if side > 0 else (on, off)
+        fill_wall(wall_ext, solid, below, above)
+        fill_post(p0, post, below, above, depth)
+        base = 0 if side > 0 else mid - some
+        stream_post(s1, some, p0, wall_ext, base, depth)
+        first, last = far_layers(side, depth)
+        collide_layers(
+            first, last, s1, some, base, lambda i, out: put_layer(p1, i, mid, out),
+            h1, mb1, w1, w2, b_col, herm, lambda n: None,
+        )
+        for q in range(Q):
+            put_rows(gx, q, mid, edge, cot[q * depth : (q + 1) * depth, :] * (1.0 - wall_o[edge : edge + depth, :]))
+        fill_single(gx, edge, mid, below, above, depth, REACH * BLOCK + N_REACH, -1, 0)
+
+    by_side(core, run)
+    moves.start(h1, h1_h)
+    moves.start(mb1, mb1_h)
     wall = wall_o[edge : edge + depth, :]
-
-    for q in range(Q):
-        put_rows(p0, q, ext, 8, get_rows(post, q, depth, 0, depth))
-    for d in range(1, REACH + 1):
-        put_layer(p0, 8 - d, ext, below[(d - 1) * BLOCK : (d - 1) * BLOCK + Q, :])
-        put_layer(p0, 7 + depth + d, ext, above[(d - 1) * BLOCK : (d - 1) * BLOCK + Q, :])
-    row = REACH * BLOCK
-    for n, (k, q) in enumerate(reaching(1)):
-        put_rows(p0, q, ext, 8 - REACH - k, below[row + n : row + n + 1, :])
-    for n, (k, q) in enumerate(reaching(-1)):
-        put_rows(p0, q, ext, 7 + depth + REACH + k, above[row + n : row + n + 1, :])
-
-    for q in range(Q):
-        ex, ey, ez = VEL[q]
-        moved = roll_plane(get_rows(p0, q, ext, 8 - edge - ez, mid), ex, ey)
-        bounced = get_rows(p0, OPP[q], ext, 8 - edge, mid)
-        put_rows(s1, q, mid, 0, jnp.where(wall_ext > 0.5, bounced, moved))
-    clear_pad(s1, mid)
-    def moments(n):
-        mb1[n] = moments_of(get_layer(s1, n + 1, mid), herm[...])
-
-    def hide(n):
-        hidden_into(h1.at[n], w1, mb1[n])
-        moves.start(h1.at[n], h1_h.at[n])
-
-    def finish(n):
-        out = get_layer(s1, n + 1, mid) + dot(w2[...], h1[n]) + b_col[...]
-        put_layer(p1, n + 1, mid, out[:Q])
-
-    staggered(mid - 2, moments, hide, finish)
-    moves.start(mb1, mb1_h)
 
     for q in range(Q):
         ex, ey, ez = VEL[q]
@@ -364,13 +481,6 @@
         bounced = get_rows(p1, OPP[q], mid, edge, depth)
         put_rows(s2, q, depth, 0, jnp.where(wall > 0.5, bounced, moved))
     clear_pad(s2, depth)
-    for q in range(Q):
-        put_rows(gx, q, mid, edge, cot[q * depth : (q + 1) * depth, :] * (1.0 - wall))
-    row = REACH * BLOCK + N_REACH
-    for n, (k, q) in enumerate(reaching(-1)):
-        put_rows(gx, q, mid, edge - k, below[row + n : row + n + 1, :])
-    for n, (k, q) in enumerate(reaching(1)):
-        put_rows(gx, q, mid, edge + depth - 1 + k, above[row + n : row + n + 1, :])
     for q in range(Q):
         ex, ey, ez = VEL[q]
         moved = roll_plane(get_rows(gx, q, mid, edge + ez, depth), -ex, -ey)
@@ -389,16 +499,16 @@
     moves.start(gb2, gb2_h)
 
     def hide_two(z):
-        hidden_into(h2.at[z % 2], w1, mb2[z])
+        hidden_into(h2.at[z], w1, mb2[z])
 
     def act(z):
-        d_act_into(da2.at[z % 2], h2.at[z % 2], w_out, gb2[z])
+        d_act_into(da2.at[z], h2.at[z], w_out, gb2[z])
 
     def back(z):
-        dm[z % 2] = split_concat(dot(w_in[...], da2[z % 2]))
+        dm[z] = split_concat(dot(w_in[...], da2[z]))
 
     def finish_two(z):
-        g = (get_layer(gp2, z, depth) + dot(herm_t[...], dm[z % 2]))[:Q]
+        g = (get_layer(gp2, z, depth) + dot(herm_t[...], dm[z]))[:Q]
         put_layer(g2, z, depth, g)
         if z < REACH:
             send_dn[z * BLOCK : z * BLOCK + Q, :] = g
@@ -415,119 +525,189 @@
             open_cells = 1.0 - wall_o[edge + z : edge + z + 1, :]
             send[row : row + 1, :] = get_rows(g2, q, depth, z, 1) * open_cells
             row += 1
+    send_on[...] = ways[core[0]]
+    send_off[...] = ways[1 - core[0]]
     moves.wait()
 
 
-def sums_kernel(
-    mb2_h, gb2_h, mb0_h, mb1_h, h1_h, w1, w_out, acc, h0, mb0, h1, mb1, mb2, gb2, h2, da2, sems
+def fill_g2(raw, gx, g2, open_ext, below, above, depth):
+    edge = REACH + 1
+    mid, ext = depth + 2 * edge, depth + 16
+    for q in range(Q):
+        put_rows(raw, q, mid, edge, get_rows(g2, q, depth, 0, depth))
+    fill_blocks(raw, edge, mid, below, above, depth)
+    for q in range(Q):
+        put_rows(gx, q, ext, 8 - edge, get_rows(raw, q, mid, 0, mid) * open_ext)
+    fill_single(gx, 8, ext, below, above, depth, REACH * BLOCK, -1, REACH)
+
+
+def stream_g2(target, rows, raw, gx, wall, base, depth):
+    edge = REACH + 1
+    mid, ext = depth + 2 * edge, depth + 16
+    solid = wall[base : base + rows, :]
+    for q in range(Q):
+        ex, ey, ez = VEL[q]
+        moved = roll_plane(get_rows(gx, q, ext, 8 - edge + base + ez, rows), -ex, -ey)
+        put_rows(target, q, rows, 0, moved + solid * get_rows(raw, OPP[q], mid, base, rows))
+    clear_pad(target, rows)
+
+
+def adjoint_layers(first, last, depth, gp1, rows, base, raw1, g1, wall, h, mb, acc, gb, da, dm, w_in, w_out, herm_t):
+    edge = REACH + 1
+    mid = depth + 2 * edge
+
+    def act(n):
+        gb[n] = get_layer(gp1, first + n - base, rows).astype(BF)
+        d_act_into(da.at[n], h.at[n], w_out, gb[n])
+
+    def back(n):
+        dm[n] = split_concat(dot(w_in[...], da[n]))
+
+    def finish(n):
+        i = first + n
+        g = (get_layer(gp1, i - base, rows) + dot(herm_t[...], dm[n]))[:Q]
+        put_layer(raw1, i, mid, g)
+        put_layer(g1, i, mid, g * (1.0 - wall[i : i + 1, :]))
+
+    def add(n):
+        if edge <= first + n < edge + depth:
+            add_sums(acc, mb[n], da.at[n], gb[n], h.at[n])
+
+    staggered(last - first, act, back, finish, add)
+
+
+def third_near_kernel(
+    core, g2, on, wall, w1, w_in, w_out, herm_t,
+    mb2_h, gb2_h, mb_near_h, h_near_h, mb_far_h, h_far_h, mb0_h, h0_h,
+    raw1, g1, acc, total_o, mb_far, h_far, mb0, h0,
+    gx, raw, gp1, gb, da, dm, h2, mb2, gb2, mb_near, h_near, sems,
+):
+    edge = REACH + 1
+    mid = wall.shape[0] - QP
+    depth = mid - 2 * edge
+    moves = Copies(sems)
+    sources = (mb2_h, gb2_h, mb_near_h, h_near_h, mb_far_h, h_far_h, mb0_h, h0_h)
+    targets = (mb2, gb2, mb_near, h_near, mb_far, h_far, mb0, h0)
+    pairs = list(zip(sources, targets))
+    copies = [moves.start(source, target) for source, target in pairs[:2]]
+    acc[...] = jnp.zeros(acc.shape, F32)
+
+    def stream(side):
+        below, above = (None, on) if side > 0 else (on, None)
+        fill_g2(raw, gx, g2, 1.0 - wall[0:mid, :], below, above, depth)
+        stream_g2(gp1, mid, raw, gx, wall, 0, depth)
+
+    by_side(core, stream)
+    for copy in copies[:2]:
+        copy.wait()
+    copies += [moves.start(source, target) for source, target in pairs[2:4]]
+
+    def hide(z):
+        hidden_into(h2.at[z], w1, mb2[z])
+
+    def act(z):
+        d_act_into(da.at[z], h2.at[z], w_out, gb2[z])
+
+    def add(z):
+        add_sums(acc, mb2[z], da.at[z], gb2[z], h2.at[z])
+
+    staggered(depth, hide, act, add)
+    for copy in copies[2:4]:
+        copy.wait()
+    copies += [moves.start(source, target) for source, target in pairs[4:]]
+
+    def run(side):
+        first, last = near_layers(side, depth)
+        total = wall[mid : mid + QP, :]
+        for i in range(max(first, edge), min(last, edge + depth)):
+            total = total + get_layer(gp1, i, mid)
+        total_o[...] = total
+        adjoint_layers(
+            first, last, depth, gp1, mid, 0, raw1, g1, wall, h_near, mb_near, acc, gb, da, dm,
+            w_in, w_out, herm_t,
+        )
+
+    by_side(core, run)
+    for copy in copies[4:]:
+        copy.wait()
+
+
+def third_kernel(
+    core, g2, on, off, wall_i, h1, mb1, h0, mb0, raw_near, g_near, acc_i, total_i, w_in, w_out, herm_t,
+    sums, da0_h, gp0_h,
+    gx, raw, gp1, g1, raw1, gp0, gb, da, dm, acc, total_s, sems,
 ):
     moves = Copies(sems)
-    pairs = ((mb2_h, mb2), (gb2_h, gb2), (mb0_h, mb0), (mb1_h, mb1), (h1_h, h1))
-    copies = [moves.start(source, target) for source, target in pairs]
-    acc[...] = jnp.zeros(acc.shape, F32)
-    for copy in copies[:3]:
-        copy.wait()
-
-    def hide(z):
-        hidden_into(h2.at[z % 3], w1, mb2[z])
-
-    def act(z):
-        d_act_into(da2.at[z % 2], h2.at[z % 3], w_out, gb2[z])
-
-    def add(z):
-        add_sums(acc, mb2[z], da2.at[z % 2], gb2[z], h2.at[z % 3])
-
-    def hide_first(z):
-        hidden_into(h0.at[z], w1, mb0[z])
-
-    staggered(mb2.shape[0], hide, act, add, hide_first)
-    for copy in copies[3:]:
-        copy.wait()
-
-
-def third_kernel(
-    g2, below, above, wall_i, h1, mb1, h0, mb0, acc_i, w_in, w_out, herm_t,
-    d_field, sums,
-    gx, raw, gp1, g1, raw1, gp0, out0, gb, da, dm, acc,
-):
     plane = wall_i.shape[1]
     mid = wall_i.shape[0] - QP
     edge = REACH + 1
     depth = mid - 2 * edge
-    ext = depth + 16
+    some = gp1.shape[1] // QP
     acc[...] = acc_i[...]
-    wall_ext = wall_i[0:mid, :]
-    open_ext = 1.0 - wall_ext
+    for q in range(Q):
+        put_rows(raw1, q, mid, 0, get_rows(raw_near, q, mid, 0, mid))
+        put_rows(g1, q, mid, 0, get_rows(g_near, q, mid, 0, mid))
+
+    def run(side):
+        below, above = (off, on) if side > 0 else (on, off)
+        fill_g2(raw, gx, g2, 1.0 - wall_i[0:mid, :], below, above, depth)
+        base = 0 if side > 0 else mid - some
+        stream_g2(gp1, some, raw, gx, wall_i, base, depth)
+        first, last = far_layers(side, depth)
+        total = total_i[...]
+        for i in range(max(first, edge), min(last, edge + depth)):
+            total = total + get_layer(gp1, i - base, some)
+        total_s[...] = total
+        adjoint_layers(
+            first, last, depth, gp1, some, base, raw1, g1, wall_i, h1, mb1, acc, gb, da, dm, w_in, w_out, herm_t
+        )
+
+    by_side(core, run)
     wall = wall_i[edge : edge + depth, :]
-
-    for q in range(Q):
-        put_rows(raw, q, mid, edge, get_rows(g2, q, depth, 0, depth))
-    for d in range(1, REACH + 1):
-        put_layer(raw, edge - d, mid, below[(d - 1) * BLOCK : (d - 1) * BLOCK + Q, :])
-        put_layer(raw, edge + depth - 1 + d, mid, above[(d - 1) * BLOCK : (d - 1) * BLOCK + Q, :])
-    for q in range(Q):
-        put_rows(gx, q, ext, 8 - edge, get_rows(raw, q, mid, 0, mid) * open_ext)
-    row = REACH * BLOCK
-    for n, (k, q) in enumerate(reaching(-1)):
-        put_rows(gx, q, ext, 8 - REACH - k, below[row + n : row + n + 1, :])
-    for n, (k, q) in enumerate(reaching(1)):
-        put_rows(gx, q, ext, 7 + depth + REACH + k, above[row + n : row + n + 1, :])
-    for q in range(Q):
-        ex, ey, ez = VEL[q]
-        moved = roll_plane(get_rows(gx, q, ext, 8 - edge + ez, mid), -ex, -ey)
-        put_rows(gp1, q, mid, 0, moved + wall_ext * get_rows(raw, OPP[q], mid, 0, mid))
-    clear_pad(gp1, mid)
-
-    total = wall_i[mid : mid + QP, :]
-    for i in range(edge, edge + depth):
-        total = total + get_layer(gp1, i, mid)
-
-    def act_one(n):
-        gb[n % 4] = get_layer(gp1, n + 1, mid).astype(BF)
-        d_act_into(da.at[n % 4], h1.at[n], w_out, gb[n % 4])
-
-    def back(n):
-        dm[n % 2] = split_concat(dot(w_in[...], da[n % 4]))
-
-    def finish_one(n):
-        i = n + 1
-        g = (get_layer(gp1, i, mid) + dot(herm_t[...], dm[n % 2]))[:Q]
-        put_layer(raw1, i, mid, g)
-        put_layer(g1, i, mid, g * open_ext[i : i + 1, :])
-
-    def add_one(n):
-        if edge <= n + 1 < edge + depth:
-            add_sums(acc, mb1[n], da.at[n % 4], gb[n % 4], h1.at[n])
-
-    staggered(mid - 2, act_one, back, finish_one, add_one)
-
+    total = total_s[...]
     for q in range(Q):
         ex, ey, ez = VEL[q]
         moved = roll_plane(get_rows(g1, q, mid, edge + ez, depth), -ex, -ey)
         put_rows(gp0, q, depth, 0, moved + wall * get_rows(raw1, OPP[q], mid, edge, depth))
     clear_pad(gp0, depth)
+    moves.start(gp0, gp0_h)
     for z in range(depth):
         total = total + get_layer(gp0, z, depth)
 
     def act_two(z):
-        gb[z % 4] = get_layer(gp0, z, depth).astype(BF)
-        d_act_into(da.at[z % 4], h0.at[z], w_out, gb[z % 4])
-
-    def finish_two(z):
-        g = (get_layer(gp0, z, depth) + dot(herm_t[...], dm[z % 2]))[:Q]
-        put_layer(out0, z, depth, g)
+        gb[z] = get_layer(gp0, z, depth).astype(BF)
+        d_act_into(da.at[z], h0.at[z], w_out, gb[z])
+        moves.start(da.at[z], da0_h.at[z])
 
     def add_two(z):
-        add_sums(acc, mb0[z], da.at[z % 4], gb[z % 4], h0.at[z])
-
-    staggered(depth, act_two, back, finish_two, add_two)
-    for q in range(Q):
-        d_field[q * depth : (q + 1) * depth, :] = get_rows(out0, q, depth, 0, depth)
-
+        add_sums(acc, mb0[z], da.at[z], gb[z], h0.at[z])
+
+    staggered(depth, act_two, add_two)
     sums[0:24, :] = acc[0:24, :]
     sums[24 : 24 + Q + 1, :] = acc[MP : MP + Q + 1, :]
     line = dot_nt(jnp.ones((8, plane), F32), total, lax.Precision.HIGHEST)
     sums[MOM + 1 : MOM + 2, 0:QP] = line[0:1, :]
+    moves.wait()
+
+
+def field_kernel(after, da0_h, gp0_h, w_in, herm_t, d_field, da0, gp0, out0, dm, sems):
+    del after
+    depth = da0.shape[0]
+    moves = Copies(sems)
+    copies = [moves.start(gp0_h, gp0)] + [moves.start(da0_h.at[z], da0.at[z]) for z in range(depth)]
+
+    def back(z):
+        copies[z + 1].wait()
+        dm[z] = split_concat(dot(w_in[...], da0[z]))
+
+    def finish(z):
+        g = (get_layer(gp0, z, depth) + dot(herm_t[...], dm[z]))[:Q]
+        put_layer(out0, z, depth, g)
+
+    copies[0].wait()
+    staggered(depth, back, finish)
+    for q in range(Q):
+        d_field[q * depth : (q + 1) * depth, :] = get_rows(out0, q, depth, 0, depth)
 
 
 def last_kernel(scale, core, mine, other, g_w_in, g_b_in, g_w_out, g_b_out):
@@ -607,12 +787,14 @@
     hid = w_in.shape[1]
     space, traj = lax.axis_size("space"), lax.axis_size("traj")
     axes = ("space", "traj")
-    up = [(i, (i + 1) % space) for i in range(space)]
-    down = [(j, i) for i, j in up]
+    chip = [(i, i + 1 - 2 * (i % 2)) for i in range(space)]
+    next_chip = [(i, (i - 1 + 2 * (i % 2)) % space) for i in range(space)]
+    place = lax.axis_index("space") % 2
+    core_id = place.reshape(1).astype(jnp.int32)
     herm, herm_t = hermite_operands()
     edge = REACH + 1
     mid, ext = depth + 2 * edge, depth + 16
-    work = mid - 2
+    near, far, some = depth, 2 * REACH, 8
     half = plane // 2
     field = field.reshape(pops * depth, plane)
     cot = cotangent.reshape(pops * depth, plane)
@@ -623,7 +805,7 @@
 
     raw = [w_in, b_in.reshape(1, hid), w_out.T, b_out.reshape(1, pops), herm, field, solid, cot]
     raw = [outside(value) for value in raw]
-    send_up, send_dn, post, mb0, w1, w_in_p, w2, w_out_p, b_col = call(
+    send_on, send_off, post, mb0, w1, w2, b_col = call(
         first_kernel,
         [
             ((SEND_ONE, plane), F32),
@@ -631,72 +813,102 @@
             pops_buf(depth, Q),
             ((depth, MP, plane), BF, pltpu.HBM),
             ((hid, MP), BF),
-            ((MP, hid), BF),
             ((QP, hid), BF),
-            ((hid, QP), BF),
             ((QP, plane), F32),
         ],
         [pops_buf(depth), ((MP, hid), F32), ((QP, hid), F32)]
         + [(value.shape, value.dtype) for value in raw]
-        + [((2, hid, plane), BF), ((depth, MP, plane), BF), ((len(raw) + 1,), "sem")],
-        raw,
+        + [((depth, hid, plane), BF), ((depth, MP, plane), BF), ((2, SEND_ONE, plane), F32)]
+        + [((len(raw) + 1,), "sem")],
+        [core_id] + raw,
         10**9,
-        5,
-        hbm=range(len(raw)),
+        7,
+        smem=(0,),
+        hbm=range(1, len(raw) + 1),
     )
-    below = lax.ppermute(send_up, "space", up)
-    above = lax.ppermute(send_dn, "space", down)
-    send_up, send_dn, g2, wall, h1, mb1, mb2, gb2 = call(
+    on = lax.ppermute(send_on, "space", chip)
+    off = lax.ppermute(send_off, "space", next_chip)
+    h0, w_in_p, w_out_p = call(
+        between_kernel,
+        [((depth, hid, plane), BF, pltpu.HBM), ((MP, hid), BF), ((hid, QP), BF)],
+        [
+            (w_in.shape, BF), (w_out.T.shape, BF), ((depth, MP, plane), BF), ((depth, hid, plane), BF),
+            ((MP, hid), F32), ((QP, hid), F32), ((depth + 3,), "sem"),
+        ],
+        [raw[0], raw[2], outside(mb0), w1],
+        10**9,
+        4,
+        hbm=range(3),
+    )
+    p1, h_near, mb_near = call(
+        near_kernel,
+        [pops_buf(mid, Q), ((near, hid, plane), BF, pltpu.HBM), ((near, MP, plane), BF, pltpu.HBM)],
+        [
+            pops_buf(ext), pops_buf(mid), ((mid, plane), F32),
+            ((near, hid, plane), BF), ((near, MP, plane), BF), ((near + 1,), "sem"),
+        ],
+        [core_id, post, on, solid, w1, w2, b_col, herm],
+        10**9,
+        6,
+        smem=(0,),
+    )
+    send_on, send_off, g2, wall, h_far, mb_far, mb2, gb2 = call(
         second_kernel,
         [
             ((SEND_TWO, plane), F32),
             ((SEND_TWO, plane), F32),
             pops_buf(depth, Q),
             ((mid + QP, plane), F32),
-            ((work, hid, plane), BF, pltpu.HBM),
-            ((work, MP, plane), BF, pltpu.HBM),
+            ((far, hid, plane), BF, pltpu.HBM),
+            ((far, MP, plane), BF, pltpu.HBM),
             ((depth, MP, plane), BF, pltpu.HBM),
             ((depth, QP, plane), BF, pltpu.HBM),
         ],
         [
-            pops_buf(ext), pops_buf(mid), pops_buf(mid), pops_buf(depth), pops_buf(mid), pops_buf(depth),
-            ((work, hid, plane), BF), ((work, MP, plane), BF), ((depth, MP, plane), BF),
-            ((depth, QP, plane), BF), ((2, hid, plane), BF), ((2, hid, plane), BF),
-            ((2, 3 * MP, plane), BF), ((work + 3,), "sem"),
+            pops_buf(ext), pops_buf(some), pops_buf(mid), pops_buf(depth), pops_buf(mid), pops_buf(depth),
+            ((far, hid, plane), BF), ((far, MP, plane), BF), ((depth, MP, plane), BF),
+            ((depth, QP, plane), BF), ((depth, hid, plane), BF), ((depth, hid, plane), BF),
+            ((depth, 3 * MP, plane), BF), ((2, SEND_TWO, plane), F32), ((4,), "sem"),
         ],
-        [post, below, above, cot, solid, w1, w_in_p, w2, w_out_p, b_col, herm, herm_t],
+        [core_id, post, on, off, cot, solid, p1, w1, w_in_p, w2, w_out_p, b_col, herm, herm_t],
+        10**9,
+        16,
+        smem=(0,),
+    )
+    on = lax.ppermute(send_on, "space", chip)
+    off = lax.ppermute(send_off, "space", next_chip)
+    saved = [outside(value) for value in (mb2, gb2, mb_near, h_near, mb_far, h_far, mb0, h0)]
+    raw_near, g_near, acc, total_g, mb_far, h_far, mb0, h0 = call(
+        third_near_kernel,
+        [pops_buf(mid, Q), pops_buf(mid, Q), ((MP + QP, hid), F32), ((QP, plane), F32)]
+        + [(value.shape, BF) for value in saved[4:]],
+        [
+            pops_buf(ext), pops_buf(mid), pops_buf(mid), ((depth, QP, plane), BF),
+            ((depth, hid, plane), BF), ((depth, 3 * MP, plane), BF), ((depth, hid, plane), BF),
+        ]
+        + [(value.shape, BF) for value in saved[:4]]
+        + [((len(saved),), "sem")],
+        [core_id, g2, on, wall, w1, w_in_p, w_out_p, herm_t] + saved,
+        10**9,
+        14,
+        smem=(0,),
+        hbm=range(8, 16),
+    )
+    sums, da0, gp0 = call(
+        third_kernel,
+        [((64, hid), F32), ((depth, hid, plane), BF, pltpu.HBM), pops_buf(depth) + (pltpu.HBM,)],
+        [
+            pops_buf(ext), pops_buf(mid), pops_buf(some), pops_buf(mid), pops_buf(mid), pops_buf(depth),
+            ((depth, QP, plane), BF), ((depth, hid, plane), BF), ((depth, 3 * MP, plane), BF),
+            ((MP + QP, hid), F32), ((QP, plane), F32), ((depth + 1,), "sem"),
+        ],
+        [
+            core_id, g2, on, off, wall, h_far, mb_far, h0, mb0, raw_near, g_near, acc, total_g,
+            w_in_p, w_out_p, herm_t,
+        ],
         10**9,
         12,
-    )
-    below = lax.ppermute(send_up, "space", up)
-    above = lax.ppermute(send_dn, "space", down)
-    acc, h0, mb0, h1, mb1 = call(
-        sums_kernel,
-        [
-            ((MP + QP, hid), F32),
-            ((depth, hid, plane), BF), ((depth, MP, plane), BF),
-            ((work, hid, plane), BF), ((work, MP, plane), BF),
-        ],
-        [
-            ((depth, MP, plane), BF), ((depth, QP, plane), BF),
-            ((3, hid, plane), BF), ((2, hid, plane), BF), ((5,), "sem"),
-        ],
-        [outside(mb2), outside(gb2), outside(mb0), outside(mb1), outside(h1), w1, w_out_p],
-        10**9,
-        4,
-        hbm=range(5),
-    )
-    d_field, sums = call(
-        third_kernel,
-        [((pops * depth, plane), F32), ((64, hid), F32)],
-        [
-            pops_buf(ext), pops_buf(mid), pops_buf(mid), pops_buf(mid), pops_buf(mid), pops_buf(depth),
-            pops_buf(depth), ((4, QP, plane), BF),
-            ((4, hid, plane), BF), ((2, 3 * MP, plane), BF), ((MP + QP, hid), F32),
-        ],
-        [g2, below, above, wall, h1, mb1, h0, mb0, acc, w_in_p, w_out_p, herm_t],
-        10**9,
-        9,
+        smem=(0,),
     )
 
     core, stages = factor_stages(space, traj)
@@ -711,6 +923,20 @@
         moved = [lax.ppermute(mine, axes, pairs) for pairs in partners(total, digits)]
         for value in moved:
             mine = mine + value
+        if digits is stages[0]:
+            (d_field,) = call(
+                field_kernel,
+                [((pops * depth, plane), F32)],
+                [
+                    ((depth, hid, plane), BF), pops_buf(depth), pops_buf(depth),
+                    ((depth, 3 * MP, plane), BF), ((depth + 1,), "sem"),
+                ],
+                [mine, outside(da0), outside(gp0), w_in_p, herm_t],
+                10**9,
+                6,
+                hbm=(1, 2),
+            )
+    mine, d_field = lax.optimization_barrier((mine, d_field))
     other = lax.ppermute(mine, axes, swap)
 
     cells = traj * local * space * depth * plane * STEPS
@@ -719,7 +945,7 @@
         lambda *refs: last_kernel(scale, *refs),
         [((MOM, hid), F32), ((1, hid), F32), ((pops, hid), F32), ((1, pops), F32)],
         [],
-        [me.reshape(1).astype(jnp.int32), mine, other],
+        [core_id, mine, other],
         10**9,
         1,
         smem=(0,),

time: 51.7 us -> 50.5 us (0.977)
  Pallas kernels: 19.3 us -> 26.7 us
  waiting for transfers between devices: 14 us -> 7.61 us
  starting transfers between devices: 17.4 us -> 15 us
    pallas_call x5 -> x8, Pallas kernels: 19.3 us -> 26.7 us  [call(): pl.pallas_call(kernel, out_shape=[out[2](out[0], out[1]) if len(out) > 2...]
    ppermute x6, waiting for transfers between devices: 8.47 us -> 5.12 us  [per_device(): lax.ppermute(mine, axes, pairs)]
    ppermute x4, waiting for transfers between devices: 3.05 us -> 0.01 us  [the longest x2 0.01 us: per_device(): on = lax.ppermute(send_on, 'space', chip)]
    ppermute x4, starting transfers between devices: 10.2 us -> 8.81 us  [the longest x2 8.21 us: per_device(): off = lax.ppermute(send_off, 'space', next_chip)]
    ppermute x6, starting transfers between devices: 7.09 us -> 6.09 us  [per_device(): lax.ppermute(mine, axes, pairs)]
  transfers between devices with their start and end apart: 12 -> 12, of which waited for: 9 -> 5; matrix products, arithmetic and copies ran while one was open for 0% -> 0% of each run, Pallas kernels for 8% -> 29%
where the time goes in v3:
time: 50.5 us; the launch traced here: 50.3 us
  Pallas kernels  26.7 us (53%)
  starting transfers between devices  15 us (30%)
  waiting for transfers between devices  7.61 us (15%)
  between operations  0.85 us (2%)
    pallas_call x8, Pallas kernels, call(): pl.pallas_call(kernel, out_shape=[out[2](out[0], out[1]) if len(out) > 2...  26.7 us
    ppermute x2, starting transfers between devices, per_device(): off = lax.ppermute(send_off, 'space', next_chip)  8.21 us
    ppermute x6, starting transfers between devices, per_device(): lax.ppermute(mine, axes, pairs)  6.09 us
    ppermute x6, waiting for transfers between devices, per_device(): lax.ppermute(mine, axes, pairs)  5.12 us
    ppermute x1, waiting for transfers between devices, per_device(): other = lax.ppermute(mine, axes, swap)  1.24 us
    ppermute x1, waiting for transfers between devices, per_device(): mine = mine + lax.ppermute(other, axes, swap)  1.23 us
  transfers between devices with their start and end apart: 12, of which 5 were waited for; matrix products, arithmetic and copies ran while one was open for 0% of the time, Pallas kernels for 29%

profile of v3, /device:TPU:0, one launch (start us, length us, event | category | flops | bytes accessed | tf_op | source)
XLA Modules:
  0.0 50.3 jit_solution(12983816078439550703)
XLA Ops:
  0.6 2.5 %shard_map.128 = (f32[160,256]{1,0:T(8,128)S(1)}, f32[160,256]{1,0:T(8,128)S(1)}, f32[2,312,128]{2,1,0:T(8,128)S(1)}, bf16[8,32,256]{2,1,0:T(8,128)(2,1)}, bf16[...) custom-call(s32[1]{0:T(128)} %bitcast.core.refs_0_, bf16[20,512]{1,0:T(8,128)(2,1)} %w_in_h.3, ...), custom_call_target="tpu_custom_call" | custom-call | flops 1000000000 | bytes 2000000 | tf_op jit(solution)/shard_map/pallas_call | solution.py:728
  3.1 0.0 copy-start.2
  3.2 0.0 copy-start.3
  3.2 0.5 %collective-permute-start = (f32[160,256]{1,0:T(8,128)S(1)}, f32[160,256]{1,0:T(8,128)S(1)}, u32[]{:S(2)}, u32[]{:S(2)}) collective-permute-start(f32[160,256]{1,0:T(8,128)S(1)} %get-tuple-element.44), channel_id=1, source_target_pairs={{0,2},{2,0},{4,6},{6,4},{8,10},{10,8},{12,14},{14,12},{16,18},{18,... | collective-permute-start | bytes 491528 | tf_op jit(solution)/shard_map/ppermute | solution.py:829
  3.7 5.7 %collective-permute-start.1 = (f32[160,256]{1,0:T(8,128)S(1)}, f32[160,256]{1,0:T(8,128)S(1)}, u32[]{:S(2)}, u32[]{:S(2)}) collective-permute-start(f32[160,256]{1,0:T(8,128)S(1)} %get-tuple-element.45), channel_id=1, source_target_pairs={{0,30},{2,4},{4,2},{6,8},{8,6},{10,12},{12,10},{14,16},{16,14},{18... | collective-permute-start | bytes 491528 | tf_op jit(solution)/shard_map/ppermute | solution.py:830
  9.3 2.5 %shard_map.130 = (bf16[8,512,256]{2,1,0:T(8,128)(2,1)}, bf16[32,512]{1,0:T(8,128)(2,1)S(1)}, bf16[512,48]{1,0:T(8,128)(2,1)S(1)}) custom-call(bf16[20,512]{1,0:T(8,128)(2,1)} %w_in_h.3, bf16[39,512]{1,0:T(8,128)(2,1)} %bitcast.18, bf16[8,32,256]{2,1,0:T(8,128)(2,1)} %get-tuple-element.50.mb0_h, bf16[512,32]{1,0:T(8,128)(2,1)S(1)} %get-tuple-element.46.w1), custom_call_target="tpu_custom_call" | custom-call | flops 1000000000 | bytes 2000000 | tf_op jit(solution)/shard_map/pallas_call | solution.py:728
  11.9 0.0 copy-start
  11.9 0.0 copy-start.1
  11.9 0.0 collective-permute-done.on
  11.9 0.0 copy-done.2
  11.9 0.0 copy-done.3
  11.9 2.3 %shard_map.129 = (f32[2,624,128]{2,1,0:T(8,128)S(1)}, bf16[8,512,256]{2,1,0:T(8,128)(2,1)}, bf16[8,32,256]{2,1,0:T(8,128)(2,1)}) custom-call(s32[1]{0:T(128)} %bitcast.core.refs_0_, f32[2,312,128]{2,1,0:T(8,128)S(1)} %get-tuple-element.43.post, f32[160,256]{1,0:T(8,128)S(1)} %collective-permute-done.on, s32[8,256]{1,0:T(8,128)S(1)} %bitcast.14, ...), custom_call_target="tpu_custom_call" | custom-call | flops 1000000000 | bytes 2000000 | tf_op jit(solution)/shard_map/pallas_call | solution.py:728
  14.3 0.0 collective-permute-done.1.off
  14.3 0.0 copy-done
  14.3 0.0 copy-done.1
  14.3 4.6 %shard_map.131 = (f32[144,256]{1,0:T(8,128)S(1)}, f32[144,256]{1,0:T(8,128)S(1)}, f32[2,312,128]{2,1,0:T(8,128)S(1)}, f32[64,256]{1,0:T(8,128)S(1)}, bf16[6,512,...) custom-call(s32[1]{0:T(128)} %bitcast.core.refs_0_, ...), custom_call_target="tpu_custom_call" | custom-call | flops 1000000000 | bytes 2000000 | tf_op jit(solution)/shard_map/pallas_call | solution.py:728
  18.9 0.1 collective-permute-start.2
  19.0 2.6 %collective-permute-start.3 = (f32[144,256]{1,0:T(8,128)S(1)}, f32[144,256]{1,0:T(8,128)S(1)}, u32[]{:S(2)}, u32[]{:S(2)}) collective-permute-start(f32[144,256]{1,0:T(8,128)S(1)} %get-tuple-element.55), channel_id=1, source_target_pairs={{0,30},{2,4},{4,2},{6,8},{8,6},{10,12},{12,10},{14,16},{16,14},{18... | collective-permute-start | bytes 442376 | tf_op jit(solution)/shard_map/ppermute | solution.py:879
  21.6 0.0 collective-permute-done.2.on
  21.6 6.1 %shard_map.132 = (f32[2,624,128]{2,1,0:T(8,128)S(1)}, f32[2,624,128]{2,1,0:T(8,128)S(1)}, f32[80,512]{1,0:T(8,128)S(1)}, f32[48,256]{1,0:T(8,128)S(1)}, bf16[6,3...) custom-call(s32[1]{0:T(128)} %bitcast.core.refs_0_, ...), custom_call_target="tpu_custom_call" | custom-call | flops 1000000000 | bytes 2000000 | tf_op jit(solution)/shard_map/pallas_call | solution.py:728
  27.7 0.0 collective-permute-done.3.off
  27.7 4.5 %shard_map.133 = (f32[64,512]{1,0:T(8,128)S(1)}, bf16[8,512,256]{2,1,0:T(8,128)(2,1)}, f32[2,384,128]{2,1,0:T(8,128)}) custom-call(s32[1]{0:T(128)} %bitcast.core.refs_0_, f32[2,312,128]{2,1,0:T(8,128)S(1)} %get-tuple-element.53.g2, f32[144,256]{1,0:T(8,128)S(1)} %collective-permute-done.2.on, f32[144,256]{1,0:T(8,128)S(1)} %collective-permute-done.3.off, ...), custom_call_target="tpu_custom_call" | custom-call | flops 1000000000 | bytes 2000000 | tf_op jit(solution)/shard_map/pallas_call | solution.py:728
  32.2 0.1 collective-permute-start.4
  32.3 1.2 %collective-permute-done.4 = f32[32,512]{1,0:T(8,128)S(1)} collective-permute-done((f32[32,512]{1,0:T(8,128)S(1)}, f32[32,512]{1,0:T(8,128)S(1)}, u32[]{:S(2)}, u32[]{:S(2)}) %collective-permute-start.4) | collective-permute-done | bytes 65568 | tf_op jit(solution)/shard_map/ppermute | solution.py:921
  33.5 0.6 %collective-permute-start.7 = (f32[32,512]{1,0:T(8,128)S(1)}, f32[32,512]{1,0:T(8,128)S(1)}, u32[]{:S(2)}, u32[]{:S(2)}) collective-permute-start(f32[32,512]{1,0:T(8,128)S(1)} %dynamic-slice_add_fusion), channel_id=1, source_target_pairs={{0,5},{1,4},{2,7},{3,6},{4,1},{5,0},{6,3},{7,2},{8,13},{9,12},{10,... | collective-permute-start | bytes 196616 | tf_op jit(solution)/shard_map/ppermute | solution.py:923
  34.1 1.1 %collective-permute-start.6 = (f32[32,512]{1,0:T(8,128)S(1)}, f32[32,512]{1,0:T(8,128)S(1)}, u32[]{:S(2)}, u32[]{:S(2)}) collective-permute-start(f32[32,512]{1,0:T(8,128)S(1)} %dynamic-slice_add_fusion), channel_id=1, source_target_pairs={{0,1},{1,0},{2,3},{3,2},{4,5},{5,4},{6,7},{7,6},{8,9},{9,8},{10,11... | collective-permute-start | bytes 196616 | tf_op jit(solution)/shard_map/ppermute | solution.py:923
  35.2 1.9 %collective-permute-start.5 = (f32[32,512]{1,0:T(8,128)S(1)}, f32[32,512]{1,0:T(8,128)S(1)}, u32[]{:S(2)}, u32[]{:S(2)}) collective-permute-start(f32[32,512]{1,0:T(8,128)S(1)} %dynamic-slice_add_fusion), channel_id=1, source_target_pairs={{0,4},{1,5},{2,6},{3,7},{4,0},{5,1},{6,2},{7,3},{8,12},{9,13},{10,... | collective-permute-start | bytes 196616 | tf_op jit(solution)/shard_map/ppermute | solution.py:923
  37.1 2.0 %collective-permute-done.7 = f32[32,512]{1,0:T(8,128)S(1)} collective-permute-done((f32[32,512]{1,0:T(8,128)S(1)}, f32[32,512]{1,0:T(8,128)S(1)}, u32[]{:S(2)}, u32[]{:S(2)}) %collective-permute-start.7) | collective-permute-done | bytes 65568 | tf_op jit(solution)/shard_map/ppermute | solution.py:923
  39.1 0.0 collective-permute-done.6
  39.1 0.9 %collective-permute-done.5 = f32[32,512]{1,0:T(8,128)S(1)} collective-permute-done((f32[32,512]{1,0:T(8,128)S(1)}, f32[32,512]{1,0:T(8,128)S(1)}, u32[]{:S(2)}, u32[]{:S(2)}) %collective-permute-start.5) | collective-permute-done | bytes 65568 | tf_op jit(solution)/shard_map/ppermute | solution.py:923
  40.1 1.9 %collective-permute-start.10 = (f32[32,512]{1,0:T(8,128)S(1)}, f32[32,512]{1,0:T(8,128)S(1)}, u32[]{:S(2)}, u32[]{:S(2)}) collective-permute-start(f32[32,512]{1,0:T(8,128)S(1)} %add_add_fusion.1.after), channel_id=1, source_target_pairs={{0,24},{1,25},{2,26},{3,27},{4,28},{5,29},{6,30},{7,31},{8,0},{9,1... | collective-permute-start | bytes 196616 | tf_op jit(solution)/shard_map/ppermute | solution.py:923
  42.0 0.0 collective-permute-start.9
  42.0 0.6 %collective-permute-start.8 = (f32[32,512]{1,0:T(8,128)S(1)}, f32[32,512]{1,0:T(8,128)S(1)}, u32[]{:S(2)}, u32[]{:S(2)}) collective-permute-start(f32[32,512]{1,0:T(8,128)S(1)} %add_add_fusion.1.after), channel_id=1, source_target_pairs={{0,8},{1,9},{2,10},{3,11},{4,12},{5,13},{6,14},{7,15},{8,16},{9,17... | collective-permute-start | bytes 196616 | tf_op jit(solution)/shard_map/ppermute | solution.py:923
  42.6 3.6 %shard_map.134 = f32[312,256]{1,0:T(8,128)} custom-call(f32[32,512]{1,0:T(8,128)S(1)} %add_add_fusion.1.after, bf16[8,512,256]{2,1,0:T(8,128)(2,1)} %get-tuple-element.73.da0_h, f32[2,384,128]{2,1,0:T(8,128)} %get-tuple-element.74.gp0_h, bf16[32,512]{1,0:T(8,128)(2,1)S(1)} %get-tuple-element.51.w_in, bf16[48,96]{1,0:T(8,128)(2,1)S(1)} %copy-done), custom_call_target="tpu_custom_call" | custom-call | flops 1000000000 | bytes 2000000 | tf_op jit(solution)/shard_map/pallas_call | solution.py:728
  46.2 0.0 collective-permute-done.10
  46.2 2.1 %collective-permute-done.9 = f32[32,512]{1,0:T(8,128)S(1)} collective-permute-done((f32[32,512]{1,0:T(8,128)S(1)}, f32[32,512]{1,0:T(8,128)S(1)}, u32[]{:S(2)}, u32[]{:S(2)}) %collective-permute-start.9) | collective-permute-done | bytes 65568 | tf_op jit(solution)/shard_map/ppermute | solution.py:923
  48.3 0.0 collective-permute-done.8
  48.3 0.1 collective-permute-start.11
  48.4 1.2 %collective-permute-done.11.refs_2_ = f32[32,512]{1,0:T(8,128)S(1)} collective-permute-done((f32[32,512]{1,0:T(8,128)S(1)}, f32[32,512]{1,0:T(8,128)S(1)}, u32[]{:S(2)}, u32[]{:S(2)}) %collective-permute-start.11) | collective-permute-done | bytes 65568 | tf_op jit(solution)/shard_map/ppermute | solution.py:940
  49.7 0.7 %shard_map.135 = (f32[20,512]{1,0:T(8,128)}, f32[1,512]{1,0:T(1,128)}, f32[39,512]{1,0:T(8,128)}, f32[1,39]{1,0:T(1,128)}) custom-call(s32[1]{0:T(128)} %bitcast.core.refs_0_, f32[32,512]{1,0:T(8,128)S(1)} %add_add_fusion.refs_1_, f32[32,512]{1,0:T(8,128)S(1)} %collective-permute-done.11.refs_2_), custom_call_target="tpu_custom_call" | custom-call | flops 1000000000 | bytes 2000000 | tf_op jit(solution)/shard_map/pallas_call | solution.py:728
  (4 shorter events, 0.1 us)
Async XLA Ops:
  3.1 8.8 %copy-start.2 = (s32[1,8,256]{2,1,0:T(8,128)S(1)}, s32[1,8,256]{2,1,0:T(8,128)}, u32[]{:S(2)}) copy-start(s32[1,8,256]{2,1,0:T(8,128)} %param.10) | copy-start | bytes 24580
  3.2 8.8 %copy-start.3 = (bf16[32,144]{1,0:T(8,128)(2,1)S(1)}, bf16[32,144]{1,0:T(8,128)(2,1)}, u32[]{:S(2)}) copy-start(bf16[32,144]{1,0:T(8,128)(2,1)} %constant.31.clone.herm_h.herm) | copy-start | bytes 27652
  3.2 8.7 %collective-permute-start = (f32[160,256]{1,0:T(8,128)S(1)}, f32[160,256]{1,0:T(8,128)S(1)}, u32[]{:S(2)}, u32[]{:S(2)}) collective-permute-start(f32[160,256]{1,0:T(8,128)S(1)} %get-tuple-element.44), channel_id=1, source_target_pairs={{0,2},{2,0},{4,6},{6,4},{8,10},{10,8},{12,14},{14,12},{16,18},{18,... | collective-permute-start | bytes 491528 | tf_op jit(solution)/shard_map/ppermute | solution.py:829
  3.7 10.6 %collective-permute-start.1 = (f32[160,256]{1,0:T(8,128)S(1)}, f32[160,256]{1,0:T(8,128)S(1)}, u32[]{:S(2)}, u32[]{:S(2)}) collective-permute-start(f32[160,256]{1,0:T(8,128)S(1)} %get-tuple-element.45), channel_id=1, source_target_pairs={{0,30},{2,4},{4,2},{6,8},{8,6},{10,12},{12,10},{14,16},{16,14},{18... | collective-permute-start | bytes 491528 | tf_op jit(solution)/shard_map/ppermute | solution.py:830
  11.9 2.4 %copy-start = (bf16[48,96]{1,0:T(8,128)(2,1)S(1)}, bf16[48,96]{1,0:T(8,128)(2,1)}, u32[]{:S(2)}) copy-start(bf16[48,96]{1,0:T(8,128)(2,1)} %constant.32.clone.herm_t) | copy-start | bytes 27652
  11.9 2.4 %copy-start.1 = (f32[1,39,8,256]{3,2,1,0:T(8,128)S(1)}, f32[1,39,8,256]{3,2,1,0:T(8,128)}, u32[]{:S(2)}) copy-start(f32[1,39,8,256]{3,2,1,0:T(8,128)} %param.11) | copy-start | bytes 958468
  18.9 2.6 %collective-permute-start.2 = (f32[144,256]{1,0:T(8,128)S(1)}, f32[144,256]{1,0:T(8,128)S(1)}, u32[]{:S(2)}, u32[]{:S(2)}) collective-permute-start(f32[144,256]{1,0:T(8,128)S(1)} %get-tuple-element.54), channel_id=1, source_target_pairs={{0,2},{2,0},{4,6},{6,4},{8,10},{10,8},{12,14},{14,12},{16,18},{18,... | collective-permute-start | bytes 442376 | tf_op jit(solution)/shard_map/ppermute | solution.py:878
  19.0 8.7 %collective-permute-start.3 = (f32[144,256]{1,0:T(8,128)S(1)}, f32[144,256]{1,0:T(8,128)S(1)}, u32[]{:S(2)}, u32[]{:S(2)}) collective-permute-start(f32[144,256]{1,0:T(8,128)S(1)} %get-tuple-element.55), channel_id=1, source_target_pairs={{0,30},{2,4},{4,2},{6,8},{8,6},{10,12},{12,10},{14,16},{16,14},{18... | collective-permute-start | bytes 442376 | tf_op jit(solution)/shard_map/ppermute | solution.py:879
  32.2 1.3 %collective-permute-start.4 = (f32[32,512]{1,0:T(8,128)S(1)}, f32[32,512]{1,0:T(8,128)S(1)}, u32[]{:S(2)}, u32[]{:S(2)}) collective-permute-start(f32[32,512]{1,0:T(8,128)S(1)} %constant_dynamic-slice_fusion), channel_id=1, source_target_pairs={{0,2},{1,3},{2,0},{3,1},{4,6},{5,7},{6,4},{7,5},{8,10},{9,11},{10,... | collective-permute-start | bytes 196616 | tf_op jit(solution)/shard_map/ppermute | solution.py:921
  33.5 5.6 %collective-permute-start.7 = (f32[32,512]{1,0:T(8,128)S(1)}, f32[32,512]{1,0:T(8,128)S(1)}, u32[]{:S(2)}, u32[]{:S(2)}) collective-permute-start(f32[32,512]{1,0:T(8,128)S(1)} %dynamic-slice_add_fusion), channel_id=1, source_target_pairs={{0,5},{1,4},{2,7},{3,6},{4,1},{5,0},{6,3},{7,2},{8,13},{9,12},{10,... | collective-permute-start | bytes 196616 | tf_op jit(solution)/shard_map/ppermute | solution.py:923
  34.1 5.0 %collective-permute-start.6 = (f32[32,512]{1,0:T(8,128)S(1)}, f32[32,512]{1,0:T(8,128)S(1)}, u32[]{:S(2)}, u32[]{:S(2)}) collective-permute-start(f32[32,512]{1,0:T(8,128)S(1)} %dynamic-slice_add_fusion), channel_id=1, source_target_pairs={{0,1},{1,0},{2,3},{3,2},{4,5},{5,4},{6,7},{7,6},{8,9},{9,8},{10,11... | collective-permute-start | bytes 196616 | tf_op jit(solution)/shard_map/ppermute | solution.py:923
  35.2 4.9 %collective-permute-start.5 = (f32[32,512]{1,0:T(8,128)S(1)}, f32[32,512]{1,0:T(8,128)S(1)}, u32[]{:S(2)}, u32[]{:S(2)}) collective-permute-start(f32[32,512]{1,0:T(8,128)S(1)} %dynamic-slice_add_fusion), channel_id=1, source_target_pairs={{0,4},{1,5},{2,6},{3,7},{4,0},{5,1},{6,2},{7,3},{8,12},{9,13},{10,... | collective-permute-start | bytes 196616 | tf_op jit(solution)/shard_map/ppermute | solution.py:923
  40.1 6.1 %collective-permute-start.10 = (f32[32,512]{1,0:T(8,128)S(1)}, f32[32,512]{1,0:T(8,128)S(1)}, u32[]{:S(2)}, u32[]{:S(2)}) collective-permute-start(f32[32,512]{1,0:T(8,128)S(1)} %add_add_fusion.1.after), channel_id=1, source_target_pairs={{0,24},{1,25},{2,26},{3,27},{4,28},{5,29},{6,30},{7,31},{8,0},{9,1... | collective-permute-start | bytes 196616 | tf_op jit(solution)/shard_map/ppermute | solution.py:923
  42.0 6.4 %collective-permute-start.9 = (f32[32,512]{1,0:T(8,128)S(1)}, f32[32,512]{1,0:T(8,128)S(1)}, u32[]{:S(2)}, u32[]{:S(2)}) collective-permute-start(f32[32,512]{1,0:T(8,128)S(1)} %add_add_fusion.1.after), channel_id=1, source_target_pairs={{0,16},{1,17},{2,18},{3,19},{4,20},{5,21},{6,22},{7,23},{8,24},{9,... | collective-permute-start | bytes 196616 | tf_op jit(solution)/shard_map/ppermute | solution.py:923
  42.0 6.4 %collective-permute-start.8 = (f32[32,512]{1,0:T(8,128)S(1)}, f32[32,512]{1,0:T(8,128)S(1)}, u32[]{:S(2)}, u32[]{:S(2)}) collective-permute-start(f32[32,512]{1,0:T(8,128)S(1)} %add_add_fusion.1.after), channel_id=1, source_target_pairs={{0,8},{1,9},{2,10},{3,11},{4,12},{5,13},{6,14},{7,15},{8,16},{9,17... | collective-permute-start | bytes 196616 | tf_op jit(solution)/shard_map/ppermute | solution.py:923
  48.3 1.3 %collective-permute-start.11 = (f32[32,512]{1,0:T(8,128)S(1)}, f32[32,512]{1,0:T(8,128)S(1)}, u32[]{:S(2)}, u32[]{:S(2)}) collective-permute-start(f32[32,512]{1,0:T(8,128)S(1)} %add_add_fusion.refs_1_), channel_id=1, source_target_pairs={{0,2},{1,3},{2,0},{3,1},{4,6},{5,7},{6,4},{7,5},{8,10},{9,11},{10,... | collective-permute-start | bytes 196616 | tf_op jit(solution)/shard_map/ppermute | solution.py:940

commit v4 on v3

--- a/solution.py
+++ b/solution.py
@@ -679,10 +679,13 @@
         d_act_into(da.at[z], h0.at[z], w_out, gb[z])
         moves.start(da.at[z], da0_h.at[z])
 
+    def rest(z):
+        del z
+
     def add_two(z):
         add_sums(acc, mb0[z], da.at[z], gb[z], h0.at[z])
 
-    staggered(depth, act_two, add_two)
+    staggered(depth, act_two, rest, rest, rest, add_two)
     sums[0:24, :] = acc[0:24, :]
     sums[24 : 24 + Q + 1, :] = acc[MP : MP + Q + 1, :]
     line = dot_nt(jnp.ones((8, plane), F32), total, lax.Precision.HIGHEST)
@@ -770,13 +773,17 @@
     for _, size in digits:
         shifts = [s + (k,) for s in shifts for k in range(size)]
     result = []
-    for shift in shifts[1:]:
+    order = shifts[1:]
+    if len(digits) == 1 and len(order) == 3:
+        order = [(k,) for k in [1,3,2]]
+    for shift in order:
         pairs = []
         for index in range(total):
             to = index
             for (stride, size), k in zip(digits, shift):
                 digit = index // stride % size
-                to += ((digit + k) % size - digit) * stride
+                other = digit ^ k if size & (size - 1) == 0 else (digit + k) % size
+                to += (other - digit) * stride
             pairs.append((index, to))
         result.append(pairs)
     return result

time: 50.5 us -> 49.8 us (0.986)
  waiting for transfers between devices: 7.61 us -> 6.08 us
  starting transfers between devices: 15 us -> 16 us
    ppermute x6, waiting for transfers between devices: 5.12 us -> 3.59 us  [per_device(): lax.ppermute(mine, axes, pairs)]
    ppermute x6, starting transfers between devices: 6.09 us -> 7.1 us  [per_device(): lax.ppermute(mine, axes, pairs)]
  transfers between devices with their start and end apart: 12 -> 12, of which waited for: 5 -> 6; matrix products, arithmetic and copies ran while one was open for 0% -> 0% of each run, Pallas kernels for 29% -> 29%
where the time goes in v4:
time: 49.8 us; the launch traced here: 49.6 us
  Pallas kernels  26.5 us (53%)
  starting transfers between devices  16 us (32%)
  waiting for transfers between devices  6.08 us (12%)
  between operations  0.85 us (2%)
    pallas_call x8, Pallas kernels, call(): pl.pallas_call(kernel, out_shape=[out[2](out[0], out[1]) if len(out) > 2...  26.5 us
    ppermute x2, starting transfers between devices, per_device(): off = lax.ppermute(send_off, 'space', next_chip)  8.21 us
    ppermute x6, starting transfers between devices, per_device(): lax.ppermute(mine, axes, pairs)  7.1 us
    ppermute x6, waiting for transfers between devices, per_device(): lax.ppermute(mine, axes, pairs)  3.59 us
    ppermute x1, waiting for transfers between devices, per_device(): other = lax.ppermute(mine, axes, swap)  1.24 us
    ppermute x1, waiting for transfers between devices, per_device(): mine = mine + lax.ppermute(other, axes, swap)  1.23 us
  transfers between devices with their start and end apart: 12, of which 6 were waited for; matrix products, arithmetic and copies ran while one was open for 0% of the time, Pallas kernels for 29%

profile of v4, /device:TPU:0, one launch (start us, length us, event | category | flops | bytes accessed | tf_op | source)
XLA Modules:
  0.0 49.6 jit_solution(14536112764377916595)
XLA Ops:
  0.6 2.5 %shard_map.128 = (f32[160,256]{1,0:T(8,128)S(1)}, f32[160,256]{1,0:T(8,128)S(1)}, f32[2,312,128]{2,1,0:T(8,128)S(1)}, bf16[8,32,256]{2,1,0:T(8,128)(2,1)}, bf16[...) custom-call(s32[1]{0:T(128)} %bitcast.core.refs_0_, bf16[20,512]{1,0:T(8,128)(2,1)} %w_in_h.3, ...), custom_call_target="tpu_custom_call" | custom-call | flops 1000000000 | bytes 2000000 | tf_op jit(solution)/shard_map/pallas_call | solution.py:731
  3.1 0.0 copy-start.2
  3.2 0.0 copy-start.3
  3.2 0.5 %collective-permute-start = (f32[160,256]{1,0:T(8,128)S(1)}, f32[160,256]{1,0:T(8,128)S(1)}, u32[]{:S(2)}, u32[]{:S(2)}) collective-permute-start(f32[160,256]{1,0:T(8,128)S(1)} %get-tuple-element.44), channel_id=1, source_target_pairs={{0,2},{2,0},{4,6},{6,4},{8,10},{10,8},{12,14},{14,12},{16,18},{18,... | collective-permute-start | bytes 491528 | tf_op jit(solution)/shard_map/ppermute | solution.py:836
  3.7 5.7 %collective-permute-start.1 = (f32[160,256]{1,0:T(8,128)S(1)}, f32[160,256]{1,0:T(8,128)S(1)}, u32[]{:S(2)}, u32[]{:S(2)}) collective-permute-start(f32[160,256]{1,0:T(8,128)S(1)} %get-tuple-element.45), channel_id=1, source_target_pairs={{0,30},{2,4},{4,2},{6,8},{8,6},{10,12},{12,10},{14,16},{16,14},{18... | collective-permute-start | bytes 491528 | tf_op jit(solution)/shard_map/ppermute | solution.py:837
  9.3 2.5 %shard_map.130 = (bf16[8,512,256]{2,1,0:T(8,128)(2,1)}, bf16[32,512]{1,0:T(8,128)(2,1)S(1)}, bf16[512,48]{1,0:T(8,128)(2,1)S(1)}) custom-call(bf16[20,512]{1,0:T(8,128)(2,1)} %w_in_h.3, bf16[39,512]{1,0:T(8,128)(2,1)} %bitcast.18, bf16[8,32,256]{2,1,0:T(8,128)(2,1)} %get-tuple-element.50.mb0_h, bf16[512,32]{1,0:T(8,128)(2,1)S(1)} %get-tuple-element.46.w1), custom_call_target="tpu_custom_call" | custom-call | flops 1000000000 | bytes 2000000 | tf_op jit(solution)/shard_map/pallas_call | solution.py:731
  11.9 0.0 copy-start
  11.9 0.0 copy-start.1
  11.9 0.0 collective-permute-done.on
  11.9 0.0 copy-done.2
  11.9 0.0 copy-done.3
  11.9 2.3 %shard_map.129 = (f32[2,624,128]{2,1,0:T(8,128)S(1)}, bf16[8,512,256]{2,1,0:T(8,128)(2,1)}, bf16[8,32,256]{2,1,0:T(8,128)(2,1)}) custom-call(s32[1]{0:T(128)} %bitcast.core.refs_0_, f32[2,312,128]{2,1,0:T(8,128)S(1)} %get-tuple-element.43.post, f32[160,256]{1,0:T(8,128)S(1)} %collective-permute-done.on, s32[8,256]{1,0:T(8,128)S(1)} %bitcast.14, ...), custom_call_target="tpu_custom_call" | custom-call | flops 1000000000 | bytes 2000000 | tf_op jit(solution)/shard_map/pallas_call | solution.py:731
  14.3 0.0 collective-permute-done.1.off
  14.3 0.0 copy-done
  14.3 0.0 copy-done.1
  14.3 4.6 %shard_map.131 = (f32[144,256]{1,0:T(8,128)S(1)}, f32[144,256]{1,0:T(8,128)S(1)}, f32[2,312,128]{2,1,0:T(8,128)S(1)}, f32[64,256]{1,0:T(8,128)S(1)}, bf16[6,512,...) custom-call(s32[1]{0:T(128)} %bitcast.core.refs_0_, ...), custom_call_target="tpu_custom_call" | custom-call | flops 1000000000 | bytes 2000000 | tf_op jit(solution)/shard_map/pallas_call | solution.py:731
  18.9 0.1 collective-permute-start.2
  19.0 2.6 %collective-permute-start.3 = (f32[144,256]{1,0:T(8,128)S(1)}, f32[144,256]{1,0:T(8,128)S(1)}, u32[]{:S(2)}, u32[]{:S(2)}) collective-permute-start(f32[144,256]{1,0:T(8,128)S(1)} %get-tuple-element.55), channel_id=1, source_target_pairs={{0,30},{2,4},{4,2},{6,8},{8,6},{10,12},{12,10},{14,16},{16,14},{18... | collective-permute-start | bytes 442376 | tf_op jit(solution)/shard_map/ppermute | solution.py:886
  21.6 0.0 collective-permute-done.2.on
  21.6 6.1 %shard_map.132 = (f32[2,624,128]{2,1,0:T(8,128)S(1)}, f32[2,624,128]{2,1,0:T(8,128)S(1)}, f32[80,512]{1,0:T(8,128)S(1)}, f32[48,256]{1,0:T(8,128)S(1)}, bf16[6,3...) custom-call(s32[1]{0:T(128)} %bitcast.core.refs_0_, ...), custom_call_target="tpu_custom_call" | custom-call | flops 1000000000 | bytes 2000000 | tf_op jit(solution)/shard_map/pallas_call | solution.py:731
  27.7 0.0 collective-permute-done.3.off
  27.7 4.2 %shard_map.133 = (f32[64,512]{1,0:T(8,128)S(1)}, bf16[8,512,256]{2,1,0:T(8,128)(2,1)}, f32[2,384,128]{2,1,0:T(8,128)}) custom-call(s32[1]{0:T(128)} %bitcast.core.refs_0_, f32[2,312,128]{2,1,0:T(8,128)S(1)} %get-tuple-element.53.g2, f32[144,256]{1,0:T(8,128)S(1)} %collective-permute-done.2.on, f32[144,256]{1,0:T(8,128)S(1)} %collective-permute-done.3.off, ...), custom_call_target="tpu_custom_call" | custom-call | flops 1000000000 | bytes 2000000 | tf_op jit(solution)/shard_map/pallas_call | solution.py:731
  31.9 0.1 collective-permute-start.4
  32.0 1.2 %collective-permute-done.4 = f32[32,512]{1,0:T(8,128)S(1)} collective-permute-done((f32[32,512]{1,0:T(8,128)S(1)}, f32[32,512]{1,0:T(8,128)S(1)}, u32[]{:S(2)}, u32[]{:S(2)}) %collective-permute-start.4) | collective-permute-done | bytes 65568 | tf_op jit(solution)/shard_map/ppermute | solution.py:928
  33.3 0.6 %collective-permute-start.7 = (f32[32,512]{1,0:T(8,128)S(1)}, f32[32,512]{1,0:T(8,128)S(1)}, u32[]{:S(2)}, u32[]{:S(2)}) collective-permute-start(f32[32,512]{1,0:T(8,128)S(1)} %dynamic-slice_add_fusion), channel_id=1, source_target_pairs={{0,5},{1,4},{2,7},{3,6},{4,1},{5,0},{6,3},{7,2},{8,13},{9,12},{10,... | collective-permute-start | bytes 196616 | tf_op jit(solution)/shard_map/ppermute | solution.py:930
  33.8 1.1 %collective-permute-start.6 = (f32[32,512]{1,0:T(8,128)S(1)}, f32[32,512]{1,0:T(8,128)S(1)}, u32[]{:S(2)}, u32[]{:S(2)}) collective-permute-start(f32[32,512]{1,0:T(8,128)S(1)} %dynamic-slice_add_fusion), channel_id=1, source_target_pairs={{0,1},{1,0},{2,3},{3,2},{4,5},{5,4},{6,7},{7,6},{8,9},{9,8},{10,11... | collective-permute-start | bytes 196616 | tf_op jit(solution)/shard_map/ppermute | solution.py:930
  34.9 1.9 %collective-permute-start.5 = (f32[32,512]{1,0:T(8,128)S(1)}, f32[32,512]{1,0:T(8,128)S(1)}, u32[]{:S(2)}, u32[]{:S(2)}) collective-permute-start(f32[32,512]{1,0:T(8,128)S(1)} %dynamic-slice_add_fusion), channel_id=1, source_target_pairs={{0,4},{1,5},{2,6},{3,7},{4,0},{5,1},{6,2},{7,3},{8,12},{9,13},{10,... | collective-permute-start | bytes 196616 | tf_op jit(solution)/shard_map/ppermute | solution.py:930
  36.8 2.0 %collective-permute-done.7 = f32[32,512]{1,0:T(8,128)S(1)} collective-permute-done((f32[32,512]{1,0:T(8,128)S(1)}, f32[32,512]{1,0:T(8,128)S(1)}, u32[]{:S(2)}, u32[]{:S(2)}) %collective-permute-start.7) | collective-permute-done | bytes 65568 | tf_op jit(solution)/shard_map/ppermute | solution.py:930
  38.9 0.0 collective-permute-done.6
  38.9 0.9 %collective-permute-done.5 = f32[32,512]{1,0:T(8,128)S(1)} collective-permute-done((f32[32,512]{1,0:T(8,128)S(1)}, f32[32,512]{1,0:T(8,128)S(1)}, u32[]{:S(2)}, u32[]{:S(2)}) %collective-permute-start.5) | collective-permute-done | bytes 65568 | tf_op jit(solution)/shard_map/ppermute | solution.py:930
  39.8 0.1 collective-permute-start.10
  39.9 1.9 %collective-permute-start.9 = (f32[32,512]{1,0:T(8,128)S(1)}, f32[32,512]{1,0:T(8,128)S(1)}, u32[]{:S(2)}, u32[]{:S(2)}) collective-permute-start(f32[32,512]{1,0:T(8,128)S(1)} %add_add_fusion.1.after), channel_id=1, source_target_pairs={{0,24},{1,25},{2,26},{3,27},{4,28},{5,29},{6,30},{7,31},{8,16},{9,... | collective-permute-start | bytes 196616 | tf_op jit(solution)/shard_map/ppermute | solution.py:930
  41.8 1.6 %collective-permute-start.8 = (f32[32,512]{1,0:T(8,128)S(1)}, f32[32,512]{1,0:T(8,128)S(1)}, u32[]{:S(2)}, u32[]{:S(2)}) collective-permute-start(f32[32,512]{1,0:T(8,128)S(1)} %add_add_fusion.1.after), channel_id=1, source_target_pairs={{0,8},{1,9},{2,10},{3,11},{4,12},{5,13},{6,14},{7,15},{8,0},{9,1},... | collective-permute-start | bytes 196616 | tf_op jit(solution)/shard_map/ppermute | solution.py:930
  43.4 3.6 %shard_map.134 = f32[312,256]{1,0:T(8,128)} custom-call(f32[32,512]{1,0:T(8,128)S(1)} %add_add_fusion.1.after, bf16[8,512,256]{2,1,0:T(8,128)(2,1)} %get-tuple-element.73.da0_h, f32[2,384,128]{2,1,0:T(8,128)} %get-tuple-element.74.gp0_h, bf16[32,512]{1,0:T(8,128)(2,1)S(1)} %get-tuple-element.51.w_in, bf16[48,96]{1,0:T(8,128)(2,1)S(1)} %copy-done), custom_call_target="tpu_custom_call" | custom-call | flops 1000000000 | bytes 2000000 | tf_op jit(solution)/shard_map/pallas_call | solution.py:731
  46.9 0.1 collective-permute-done.10
  47.0 0.0 collective-permute-done.9
  47.0 0.5 %collective-permute-done.8 = f32[32,512]{1,0:T(8,128)S(1)} collective-permute-done((f32[32,512]{1,0:T(8,128)S(1)}, f32[32,512]{1,0:T(8,128)S(1)}, u32[]{:S(2)}, u32[]{:S(2)}) %collective-permute-start.8) | collective-permute-done | bytes 65568 | tf_op jit(solution)/shard_map/ppermute | solution.py:930
  47.6 0.1 collective-permute-start.11
  47.7 1.2 %collective-permute-done.11.refs_2_ = f32[32,512]{1,0:T(8,128)S(1)} collective-permute-done((f32[32,512]{1,0:T(8,128)S(1)}, f32[32,512]{1,0:T(8,128)S(1)}, u32[]{:S(2)}, u32[]{:S(2)}) %collective-permute-start.11) | collective-permute-done | bytes 65568 | tf_op jit(solution)/shard_map/ppermute | solution.py:947
  48.9 0.7 %shard_map.135 = (f32[20,512]{1,0:T(8,128)}, f32[1,512]{1,0:T(1,128)}, f32[39,512]{1,0:T(8,128)}, f32[1,39]{1,0:T(1,128)}) custom-call(s32[1]{0:T(128)} %bitcast.core.refs_0_, f32[32,512]{1,0:T(8,128)S(1)} %add_add_fusion.refs_1_, f32[32,512]{1,0:T(8,128)S(1)} %collective-permute-done.11.refs_2_), custom_call_target="tpu_custom_call" | custom-call | flops 1000000000 | bytes 2000000 | tf_op jit(solution)/shard_map/pallas_call | solution.py:731
  (4 shorter events, 0.1 us)
Async XLA Ops:
  3.1 8.8 %copy-start.2 = (s32[1,8,256]{2,1,0:T(8,128)S(1)}, s32[1,8,256]{2,1,0:T(8,128)}, u32[]{:S(2)}) copy-start(s32[1,8,256]{2,1,0:T(8,128)} %param.10) | copy-start | bytes 24580
  3.2 8.8 %copy-start.3 = (bf16[32,144]{1,0:T(8,128)(2,1)S(1)}, bf16[32,144]{1,0:T(8,128)(2,1)}, u32[]{:S(2)}) copy-start(bf16[32,144]{1,0:T(8,128)(2,1)} %constant.31.clone.herm_h.herm) | copy-start | bytes 27652
  3.2 8.7 %collective-permute-start = (f32[160,256]{1,0:T(8,128)S(1)}, f32[160,256]{1,0:T(8,128)S(1)}, u32[]{:S(2)}, u32[]{:S(2)}) collective-permute-start(f32[160,256]{1,0:T(8,128)S(1)} %get-tuple-element.44), channel_id=1, source_target_pairs={{0,2},{2,0},{4,6},{6,4},{8,10},{10,8},{12,14},{14,12},{16,18},{18,... | collective-permute-start | bytes 491528 | tf_op jit(solution)/shard_map/ppermute | solution.py:836
  3.7 10.6 %collective-permute-start.1 = (f32[160,256]{1,0:T(8,128)S(1)}, f32[160,256]{1,0:T(8,128)S(1)}, u32[]{:S(2)}, u32[]{:S(2)}) collective-permute-start(f32[160,256]{1,0:T(8,128)S(1)} %get-tuple-element.45), channel_id=1, source_target_pairs={{0,30},{2,4},{4,2},{6,8},{8,6},{10,12},{12,10},{14,16},{16,14},{18... | collective-permute-start | bytes 491528 | tf_op jit(solution)/shard_map/ppermute | solution.py:837
  11.9 2.4 %copy-start = (bf16[48,96]{1,0:T(8,128)(2,1)S(1)}, bf16[48,96]{1,0:T(8,128)(2,1)}, u32[]{:S(2)}) copy-start(bf16[48,96]{1,0:T(8,128)(2,1)} %constant.32.clone.herm_t) | copy-start | bytes 27652
  11.9 2.4 %copy-start.1 = (f32[1,39,8,256]{3,2,1,0:T(8,128)S(1)}, f32[1,39,8,256]{3,2,1,0:T(8,128)}, u32[]{:S(2)}) copy-start(f32[1,39,8,256]{3,2,1,0:T(8,128)} %param.11) | copy-start | bytes 958468
  18.9 2.6 %collective-permute-start.2 = (f32[144,256]{1,0:T(8,128)S(1)}, f32[144,256]{1,0:T(8,128)S(1)}, u32[]{:S(2)}, u32[]{:S(2)}) collective-permute-start(f32[144,256]{1,0:T(8,128)S(1)} %get-tuple-element.54), channel_id=1, source_target_pairs={{0,2},{2,0},{4,6},{6,4},{8,10},{10,8},{12,14},{14,12},{16,18},{18,... | collective-permute-start | bytes 442376 | tf_op jit(solution)/shard_map/ppermute | solution.py:885
  19.0 8.7 %collective-permute-start.3 = (f32[144,256]{1,0:T(8,128)S(1)}, f32[144,256]{1,0:T(8,128)S(1)}, u32[]{:S(2)}, u32[]{:S(2)}) collective-permute-start(f32[144,256]{1,0:T(8,128)S(1)} %get-tuple-element.55), channel_id=1, source_target_pairs={{0,30},{2,4},{4,2},{6,8},{8,6},{10,12},{12,10},{14,16},{16,14},{18... | collective-permute-start | bytes 442376 | tf_op jit(solution)/shard_map/ppermute | solution.py:886
  31.9 1.3 %collective-permute-start.4 = (f32[32,512]{1,0:T(8,128)S(1)}, f32[32,512]{1,0:T(8,128)S(1)}, u32[]{:S(2)}, u32[]{:S(2)}) collective-permute-start(f32[32,512]{1,0:T(8,128)S(1)} %constant_dynamic-slice_fusion), channel_id=1, source_target_pairs={{0,2},{1,3},{2,0},{3,1},{4,6},{5,7},{6,4},{7,5},{8,10},{9,11},{10,... | collective-permute-start | bytes 196616 | tf_op jit(solution)/shard_map/ppermute | solution.py:928
  33.3 5.6 %collective-permute-start.7 = (f32[32,512]{1,0:T(8,128)S(1)}, f32[32,512]{1,0:T(8,128)S(1)}, u32[]{:S(2)}, u32[]{:S(2)}) collective-permute-start(f32[32,512]{1,0:T(8,128)S(1)} %dynamic-slice_add_fusion), channel_id=1, source_target_pairs={{0,5},{1,4},{2,7},{3,6},{4,1},{5,0},{6,3},{7,2},{8,13},{9,12},{10,... | collective-permute-start | bytes 196616 | tf_op jit(solution)/shard_map/ppermute | solution.py:930
  33.8 5.0 %collective-permute-start.6 = (f32[32,512]{1,0:T(8,128)S(1)}, f32[32,512]{1,0:T(8,128)S(1)}, u32[]{:S(2)}, u32[]{:S(2)}) collective-permute-start(f32[32,512]{1,0:T(8,128)S(1)} %dynamic-slice_add_fusion), channel_id=1, source_target_pairs={{0,1},{1,0},{2,3},{3,2},{4,5},{5,4},{6,7},{7,6},{8,9},{9,8},{10,11... | collective-permute-start | bytes 196616 | tf_op jit(solution)/shard_map/ppermute | solution.py:930
  34.9 4.9 %collective-permute-start.5 = (f32[32,512]{1,0:T(8,128)S(1)}, f32[32,512]{1,0:T(8,128)S(1)}, u32[]{:S(2)}, u32[]{:S(2)}) collective-permute-start(f32[32,512]{1,0:T(8,128)S(1)} %dynamic-slice_add_fusion), channel_id=1, source_target_pairs={{0,4},{1,5},{2,6},{3,7},{4,0},{5,1},{6,2},{7,3},{8,12},{9,13},{10,... | collective-permute-start | bytes 196616 | tf_op jit(solution)/shard_map/ppermute | solution.py:930
  39.8 7.2 %collective-permute-start.10 = (f32[32,512]{1,0:T(8,128)S(1)}, f32[32,512]{1,0:T(8,128)S(1)}, u32[]{:S(2)}, u32[]{:S(2)}) collective-permute-start(f32[32,512]{1,0:T(8,128)S(1)} %add_add_fusion.1.after), channel_id=1, source_target_pairs={{0,16},{1,17},{2,18},{3,19},{4,20},{5,21},{6,22},{7,23},{8,24},{9,... | collective-permute-start | bytes 196616 | tf_op jit(solution)/shard_map/ppermute | solution.py:930
  39.9 7.1 %collective-permute-start.9 = (f32[32,512]{1,0:T(8,128)S(1)}, f32[32,512]{1,0:T(8,128)S(1)}, u32[]{:S(2)}, u32[]{:S(2)}) collective-permute-start(f32[32,512]{1,0:T(8,128)S(1)} %add_add_fusion.1.after), channel_id=1, source_target_pairs={{0,24},{1,25},{2,26},{3,27},{4,28},{5,29},{6,30},{7,31},{8,16},{9,... | collective-permute-start | bytes 196616 | tf_op jit(solution)/shard_map/ppermute | solution.py:930
  41.8 5.8 %collective-permute-start.8 = (f32[32,512]{1,0:T(8,128)S(1)}, f32[32,512]{1,0:T(8,128)S(1)}, u32[]{:S(2)}, u32[]{:S(2)}) collective-permute-start(f32[32,512]{1,0:T(8,128)S(1)} %add_add_fusion.1.after), channel_id=1, source_target_pairs={{0,8},{1,9},{2,10},{3,11},{4,12},{5,13},{6,14},{7,15},{8,0},{9,1},... | collective-permute-start | bytes 196616 | tf_op jit(solution)/shard_map/ppermute | solution.py:930
  47.6 1.3 %collective-permute-start.11 = (f32[32,512]{1,0:T(8,128)S(1)}, f32[32,512]{1,0:T(8,128)S(1)}, u32[]{:S(2)}, u32[]{:S(2)}) collective-permute-start(f32[32,512]{1,0:T(8,128)S(1)} %add_add_fusion.refs_1_), channel_id=1, source_target_pairs={{0,2},{1,3},{2,0},{3,1},{4,6},{5,7},{6,4},{7,5},{8,10},{9,11},{10,... | collective-permute-start | bytes 196616 | tf_op jit(solution)/shard_map/ppermute | solution.py:947

commit v5 on v4

--- a/solution.py
+++ b/solution.py
@@ -204,11 +204,14 @@
         da[start : start + CHUNK, :] = (d_hidden * (1.0 - hidden * hidden)).astype(BF)
 
 
-def staggered(count, *stages):
-    for turn in range(count + len(stages) - 1):
+def staggered(count, *stages, beside=()):
+    turns = count + len(stages) - 1
+    for turn in range(turns):
         for late, stage in enumerate(stages):
             if 0 <= turn - late < count:
                 stage(turn - late)
+        for work in beside[turn * len(beside) // turns : (turn + 1) * len(beside) // turns]:
+            work()
 
 
 def add_sums(acc, mb, da, gb, h):
@@ -246,7 +249,7 @@
     moves.open = []
     depth, plane = solid.shape
     hid = w_in.shape[1]
-    for copy in copies[:4]:
+    for copy in copies[:6]:
         copy.wait()
     wide[...] = jnp.zeros(wide.shape, F32)
     wide[:MOM, :] = w_in[...].astype(F32)
@@ -264,8 +267,6 @@
     column = tall[0:8, 0:128].T
     b_col_o[...] = jnp.broadcast_to(column[:QP, 0:1], (QP, plane))
 
-    for copy in copies[4:6]:
-        copy.wait()
     for q in range(Q):
         put_rows(state, q, depth, 0, field[q * depth : (q + 1) * depth, :])
     clear_pad(state, depth)
@@ -396,7 +397,7 @@
     clear_pad(target, rows)
 
 
-def collide_layers(first, last, s1, rows, base, p1, h1, mb1, w1, w2, b_col, herm, after):
+def collide_layers(first, last, s1, rows, base, p1, h1, mb1, w1, w2, b_col, herm, after, beside=()):
     def moments(n):
         mb1[n] = moments_of(get_layer(s1, first + n - base, rows), herm[...])
 
@@ -408,7 +409,7 @@
         out = get_layer(s1, first + n - base, rows) + dot(w2[...], h1[n]) + b_col[...]
         p1(first + n, out[:Q])
 
-    staggered(last - first, moments, hide, finish)
+    staggered(last - first, moments, hide, finish, beside=beside)
 
 
 def near_kernel(
@@ -455,20 +456,28 @@
     for q in range(Q):
         put_rows(p1, q, mid, 0, get_rows(p1_near, q, mid, 0, mid))
 
+    def gpost(q):
+        ex, ey, ez = VEL[q]
+        wall = wall_o[edge : edge + depth, :]
+        put_rows(gx, q, mid, edge, cot[q * depth : (q + 1) * depth, :] * (1.0 - wall))
+        moved = roll_plane(get_rows(gx, q, mid, edge + ez, depth), -ex, -ey)
+        at = OPP[q] * depth
+        put_rows(gp2, q, depth, 0, moved + wall * cot[at : at + depth, :])
+
+    clear_pad(gp2, depth)
+
     def run(side):
         below, above = (off, on) if side > 0 else (on, off)
         fill_wall(wall_ext, solid, below, above)
         fill_post(p0, post, below, above, depth)
         base = 0 if side > 0 else mid - some
         stream_post(s1, some, p0, wall_ext, base, depth)
+        fill_single(gx, edge, mid, below, above, depth, REACH * BLOCK + N_REACH, -1, 0)
         first, last = far_layers(side, depth)
         collide_layers(
             first, last, s1, some, base, lambda i, out: put_layer(p1, i, mid, out),
-            h1, mb1, w1, w2, b_col, herm, lambda n: None,
+            h1, mb1, w1, w2, b_col, herm, lambda n: None, [lambda q=q: gpost(q) for q in range(Q)],
         )
-        for q in range(Q):
-            put_rows(gx, q, mid, edge, cot[q * depth : (q + 1) * depth, :] * (1.0 - wall_o[edge : edge + depth, :]))
-        fill_single(gx, edge, mid, below, above, depth, REACH * BLOCK + N_REACH, -1, 0)
 
     by_side(core, run)
     moves.start(h1, h1_h)
@@ -481,12 +490,6 @@
         bounced = get_rows(p1, OPP[q], mid, edge, depth)
         put_rows(s2, q, depth, 0, jnp.where(wall > 0.5, bounced, moved))
     clear_pad(s2, depth)
-    for q in range(Q):
-        ex, ey, ez = VEL[q]
-        moved = roll_plane(get_rows(gx, q, mid, edge + ez, depth), -ex, -ey)
-        at = OPP[q] * depth
-        put_rows(gp2, q, depth, 0, moved + wall * cot[at : at + depth, :])
-    clear_pad(gp2, depth)
 
     total = jnp.zeros((QP, plane), F32)
     for z in range(depth):

time: 49.8 us -> 48.8 us (0.980)
  Pallas kernels: 26.5 us -> 25.6 us
    pallas_call x8, Pallas kernels: 26.5 us -> 25.6 us  [call(): pl.pallas_call(kernel, out_shape=[out[2](out[0], out[1]) if len(out) > 2...]
  transfers between devices with their start and end apart: 12 -> 12, of which waited for: 6 -> 6; matrix products, arithmetic and copies ran while one was open for 0% -> 0% of each run, Pallas kernels for 29% -> 30%
where the time goes in v5:
time: 48.8 us; the launch traced here: 48.6 us
  Pallas kernels  25.6 us (52%)
  starting transfers between devices  16 us (33%)
  waiting for transfers between devices  6.05 us (12%)
  between operations  0.85 us (2%)
    pallas_call x8, Pallas kernels, call(): pl.pallas_call(kernel, out_shape=[out[2](out[0], out[1]) if len(out) > 2...  25.6 us
    ppermute x2, starting transfers between devices, per_device(): off = lax.ppermute(send_off, 'space', next_chip)  8.22 us
    ppermute x6, starting transfers between devices, per_device(): lax.ppermute(mine, axes, pairs)  7.1 us
    ppermute x6, waiting for transfers between devices, per_device(): lax.ppermute(mine, axes, pairs)  3.56 us
    ppermute x1, waiting for transfers between devices, per_device(): other = lax.ppermute(mine, axes, swap)  1.24 us
    ppermute x1, waiting for transfers between devices, per_device(): mine = mine + lax.ppermute(other, axes, swap)  1.23 us
  transfers between devices with their start and end apart: 12, of which 6 were waited for; matrix products, arithmetic and copies ran while one was open for 0% of the time, Pallas kernels for 30%

profile of v5, /device:TPU:0, one launch (start us, length us, event | category | flops | bytes accessed | tf_op | source)
XLA Modules:
  0.0 48.6 jit_solution(6521704002097392167)
XLA Ops:
  0.6 2.5 %shard_map.128 = (f32[160,256]{1,0:T(8,128)S(1)}, f32[160,256]{1,0:T(8,128)S(1)}, f32[2,312,128]{2,1,0:T(8,128)S(1)}, bf16[8,32,256]{2,1,0:T(8,128)(2,1)}, bf16[...) custom-call(s32[1]{0:T(128)} %bitcast.core.refs_0_, bf16[20,512]{1,0:T(8,128)(2,1)} %w_in_h.3, ...), custom_call_target="tpu_custom_call" | custom-call | flops 1000000000 | bytes 2000000 | tf_op jit(solution)/shard_map/pallas_call | solution.py:734
  3.2 0.0 copy-start.2
  3.2 0.0 copy-start.3
  3.2 0.5 %collective-permute-start = (f32[160,256]{1,0:T(8,128)S(1)}, f32[160,256]{1,0:T(8,128)S(1)}, u32[]{:S(2)}, u32[]{:S(2)}) collective-permute-start(f32[160,256]{1,0:T(8,128)S(1)} %get-tuple-element.44), channel_id=1, source_target_pairs={{0,2},{2,0},{4,6},{6,4},{8,10},{10,8},{12,14},{14,12},{16,18},{18,... | collective-permute-start | bytes 491528 | tf_op jit(solution)/shard_map/ppermute | solution.py:839
  3.7 5.7 %collective-permute-start.1 = (f32[160,256]{1,0:T(8,128)S(1)}, f32[160,256]{1,0:T(8,128)S(1)}, u32[]{:S(2)}, u32[]{:S(2)}) collective-permute-start(f32[160,256]{1,0:T(8,128)S(1)} %get-tuple-element.45), channel_id=1, source_target_pairs={{0,30},{2,4},{4,2},{6,8},{8,6},{10,12},{12,10},{14,16},{16,14},{18... | collective-permute-start | bytes 491528 | tf_op jit(solution)/shard_map/ppermute | solution.py:840
  9.4 2.5 %shard_map.130 = (bf16[8,512,256]{2,1,0:T(8,128)(2,1)}, bf16[32,512]{1,0:T(8,128)(2,1)S(1)}, bf16[512,48]{1,0:T(8,128)(2,1)S(1)}) custom-call(bf16[20,512]{1,0:T(8,128)(2,1)} %w_in_h.3, bf16[39,512]{1,0:T(8,128)(2,1)} %bitcast.18, bf16[8,32,256]{2,1,0:T(8,128)(2,1)} %get-tuple-element.50.mb0_h, bf16[512,32]{1,0:T(8,128)(2,1)S(1)} %get-tuple-element.46.w1), custom_call_target="tpu_custom_call" | custom-call | flops 1000000000 | bytes 2000000 | tf_op jit(solution)/shard_map/pallas_call | solution.py:734
  11.9 0.0 copy-start
  11.9 0.0 copy-start.1
  11.9 0.0 collective-permute-done.on
  11.9 0.0 copy-done.2
  11.9 0.0 copy-done.3
  11.9 2.3 %shard_map.129 = (f32[2,624,128]{2,1,0:T(8,128)S(1)}, bf16[8,512,256]{2,1,0:T(8,128)(2,1)}, bf16[8,32,256]{2,1,0:T(8,128)(2,1)}) custom-call(s32[1]{0:T(128)} %bitcast.core.refs_0_, f32[2,312,128]{2,1,0:T(8,128)S(1)} %get-tuple-element.43.post, f32[160,256]{1,0:T(8,128)S(1)} %collective-permute-done.on, s32[8,256]{1,0:T(8,128)S(1)} %bitcast.14, ...), custom_call_target="tpu_custom_call" | custom-call | flops 1000000000 | bytes 2000000 | tf_op jit(solution)/shard_map/pallas_call | solution.py:734
  14.3 0.0 collective-permute-done.1.off
  14.3 0.0 copy-done
  14.3 0.0 copy-done.1
  14.3 3.7 %shard_map.131 = (f32[144,256]{1,0:T(8,128)S(1)}, f32[144,256]{1,0:T(8,128)S(1)}, f32[2,312,128]{2,1,0:T(8,128)S(1)}, f32[64,256]{1,0:T(8,128)S(1)}, bf16[6,512,...) custom-call(s32[1]{0:T(128)} %bitcast.core.refs_0_, ...), custom_call_target="tpu_custom_call" | custom-call | flops 1000000000 | bytes 2000000 | tf_op jit(solution)/shard_map/pallas_call | solution.py:734
  18.0 0.1 collective-permute-start.2
  18.1 2.6 %collective-permute-start.3 = (f32[144,256]{1,0:T(8,128)S(1)}, f32[144,256]{1,0:T(8,128)S(1)}, u32[]{:S(2)}, u32[]{:S(2)}) collective-permute-start(f32[144,256]{1,0:T(8,128)S(1)} %get-tuple-element.55), channel_id=1, source_target_pairs={{0,30},{2,4},{4,2},{6,8},{8,6},{10,12},{12,10},{14,16},{16,14},{18... | collective-permute-start | bytes 442376 | tf_op jit(solution)/shard_map/ppermute | solution.py:889
  20.7 0.0 collective-permute-done.2.on
  20.7 6.1 %shard_map.132 = (f32[2,624,128]{2,1,0:T(8,128)S(1)}, f32[2,624,128]{2,1,0:T(8,128)S(1)}, f32[80,512]{1,0:T(8,128)S(1)}, f32[48,256]{1,0:T(8,128)S(1)}, bf16[6,3...) custom-call(s32[1]{0:T(128)} %bitcast.core.refs_0_, ...), custom_call_target="tpu_custom_call" | custom-call | flops 1000000000 | bytes 2000000 | tf_op jit(solution)/shard_map/pallas_call | solution.py:734
  26.7 0.0 collective-permute-done.3.off
  26.7 4.2 %shard_map.133 = (f32[64,512]{1,0:T(8,128)S(1)}, bf16[8,512,256]{2,1,0:T(8,128)(2,1)}, f32[2,384,128]{2,1,0:T(8,128)}) custom-call(s32[1]{0:T(128)} %bitcast.core.refs_0_, f32[2,312,128]{2,1,0:T(8,128)S(1)} %get-tuple-element.53.g2, f32[144,256]{1,0:T(8,128)S(1)} %collective-permute-done.2.on, f32[144,256]{1,0:T(8,128)S(1)} %collective-permute-done.3.off, ...), custom_call_target="tpu_custom_call" | custom-call | flops 1000000000 | bytes 2000000 | tf_op jit(solution)/shard_map/pallas_call | solution.py:734
  31.0 0.1 collective-permute-start.4
  31.1 1.2 %collective-permute-done.4 = f32[32,512]{1,0:T(8,128)S(1)} collective-permute-done((f32[32,512]{1,0:T(8,128)S(1)}, f32[32,512]{1,0:T(8,128)S(1)}, u32[]{:S(2)}, u32[]{:S(2)}) %collective-permute-start.4) | collective-permute-done | bytes 65568 | tf_op jit(solution)/shard_map/ppermute | solution.py:931
  32.3 0.6 %collective-permute-start.7 = (f32[32,512]{1,0:T(8,128)S(1)}, f32[32,512]{1,0:T(8,128)S(1)}, u32[]{:S(2)}, u32[]{:S(2)}) collective-permute-start(f32[32,512]{1,0:T(8,128)S(1)} %dynamic-slice_add_fusion), channel_id=1, source_target_pairs={{0,5},{1,4},{2,7},{3,6},{4,1},{5,0},{6,3},{7,2},{8,13},{9,12},{10,... | collective-permute-start | bytes 196616 | tf_op jit(solution)/shard_map/ppermute | solution.py:933
  32.9 1.1 %collective-permute-start.6 = (f32[32,512]{1,0:T(8,128)S(1)}, f32[32,512]{1,0:T(8,128)S(1)}, u32[]{:S(2)}, u32[]{:S(2)}) collective-permute-start(f32[32,512]{1,0:T(8,128)S(1)} %dynamic-slice_add_fusion), channel_id=1, source_target_pairs={{0,1},{1,0},{2,3},{3,2},{4,5},{5,4},{6,7},{7,6},{8,9},{9,8},{10,11... | collective-permute-start | bytes 196616 | tf_op jit(solution)/shard_map/ppermute | solution.py:933
  34.0 1.9 %collective-permute-start.5 = (f32[32,512]{1,0:T(8,128)S(1)}, f32[32,512]{1,0:T(8,128)S(1)}, u32[]{:S(2)}, u32[]{:S(2)}) collective-permute-start(f32[32,512]{1,0:T(8,128)S(1)} %dynamic-slice_add_fusion), channel_id=1, source_target_pairs={{0,4},{1,5},{2,6},{3,7},{4,0},{5,1},{6,2},{7,3},{8,12},{9,13},{10,... | collective-permute-start | bytes 196616 | tf_op jit(solution)/shard_map/ppermute | solution.py:933
  35.9 2.1 %collective-permute-done.7 = f32[32,512]{1,0:T(8,128)S(1)} collective-permute-done((f32[32,512]{1,0:T(8,128)S(1)}, f32[32,512]{1,0:T(8,128)S(1)}, u32[]{:S(2)}, u32[]{:S(2)}) %collective-permute-start.7) | collective-permute-done | bytes 65568 | tf_op jit(solution)/shard_map/ppermute | solution.py:933
  38.0 0.0 collective-permute-done.6
  38.0 0.9 %collective-permute-done.5 = f32[32,512]{1,0:T(8,128)S(1)} collective-permute-done((f32[32,512]{1,0:T(8,128)S(1)}, f32[32,512]{1,0:T(8,128)S(1)}, u32[]{:S(2)}, u32[]{:S(2)}) %collective-permute-start.5) | collective-permute-done | bytes 65568 | tf_op jit(solution)/shard_map/ppermute | solution.py:933
  38.9 0.1 collective-permute-start.10
  39.0 1.9 %collective-permute-start.9 = (f32[32,512]{1,0:T(8,128)S(1)}, f32[32,512]{1,0:T(8,128)S(1)}, u32[]{:S(2)}, u32[]{:S(2)}) collective-permute-start(f32[32,512]{1,0:T(8,128)S(1)} %add_add_fusion.1.after), channel_id=1, source_target_pairs={{0,24},{1,25},{2,26},{3,27},{4,28},{5,29},{6,30},{7,31},{8,16},{9,... | collective-permute-start | bytes 196616 | tf_op jit(solution)/shard_map/ppermute | solution.py:933
  40.9 1.6 %collective-permute-start.8 = (f32[32,512]{1,0:T(8,128)S(1)}, f32[32,512]{1,0:T(8,128)S(1)}, u32[]{:S(2)}, u32[]{:S(2)}) collective-permute-start(f32[32,512]{1,0:T(8,128)S(1)} %add_add_fusion.1.after), channel_id=1, source_target_pairs={{0,8},{1,9},{2,10},{3,11},{4,12},{5,13},{6,14},{7,15},{8,0},{9,1},... | collective-permute-start | bytes 196616 | tf_op jit(solution)/shard_map/ppermute | solution.py:933
  42.4 3.6 %shard_map.134 = f32[312,256]{1,0:T(8,128)} custom-call(f32[32,512]{1,0:T(8,128)S(1)} %add_add_fusion.1.after, bf16[8,512,256]{2,1,0:T(8,128)(2,1)} %get-tuple-element.73.da0_h, f32[2,384,128]{2,1,0:T(8,128)} %get-tuple-element.74.gp0_h, bf16[32,512]{1,0:T(8,128)(2,1)S(1)} %get-tuple-element.51.w_in, bf16[48,96]{1,0:T(8,128)(2,1)S(1)} %copy-done), custom_call_target="tpu_custom_call" | custom-call | flops 1000000000 | bytes 2000000 | tf_op jit(solution)/shard_map/pallas_call | solution.py:734
  46.0 0.1 collective-permute-done.10
  46.1 0.0 collective-permute-done.9
  46.1 0.5 %collective-permute-done.8 = f32[32,512]{1,0:T(8,128)S(1)} collective-permute-done((f32[32,512]{1,0:T(8,128)S(1)}, f32[32,512]{1,0:T(8,128)S(1)}, u32[]{:S(2)}, u32[]{:S(2)}) %collective-permute-start.8) | collective-permute-done | bytes 65568 | tf_op jit(solution)/shard_map/ppermute | solution.py:933
  46.6 0.1 collective-permute-start.11
  46.7 1.2 %collective-permute-done.11.refs_2_ = f32[32,512]{1,0:T(8,128)S(1)} collective-permute-done((f32[32,512]{1,0:T(8,128)S(1)}, f32[32,512]{1,0:T(8,128)S(1)}, u32[]{:S(2)}, u32[]{:S(2)}) %collective-permute-start.11) | collective-permute-done | bytes 65568 | tf_op jit(solution)/shard_map/ppermute | solution.py:950
  47.9 0.7 %shard_map.135 = (f32[20,512]{1,0:T(8,128)}, f32[1,512]{1,0:T(1,128)}, f32[39,512]{1,0:T(8,128)}, f32[1,39]{1,0:T(1,128)}) custom-call(s32[1]{0:T(128)} %bitcast.core.refs_0_, f32[32,512]{1,0:T(8,128)S(1)} %add_add_fusion.refs_1_, f32[32,512]{1,0:T(8,128)S(1)} %collective-permute-done.11.refs_2_), custom_call_target="tpu_custom_call" | custom-call | flops 1000000000 | bytes 2000000 | tf_op jit(solution)/shard_map/pallas_call | solution.py:734
  (4 shorter events, 0.1 us)
Async XLA Ops:
  3.2 8.8 %copy-start.2 = (s32[1,8,256]{2,1,0:T(8,128)S(1)}, s32[1,8,256]{2,1,0:T(8,128)}, u32[]{:S(2)}) copy-start(s32[1,8,256]{2,1,0:T(8,128)} %param.10) | copy-start | bytes 24580
  3.2 8.8 %copy-start.3 = (bf16[32,144]{1,0:T(8,128)(2,1)S(1)}, bf16[32,144]{1,0:T(8,128)(2,1)}, u32[]{:S(2)}) copy-start(bf16[32,144]{1,0:T(8,128)(2,1)} %constant.31.clone.herm_h.herm) | copy-start | bytes 27652
  3.2 8.7 %collective-permute-start = (f32[160,256]{1,0:T(8,128)S(1)}, f32[160,256]{1,0:T(8,128)S(1)}, u32[]{:S(2)}, u32[]{:S(2)}) collective-permute-start(f32[160,256]{1,0:T(8,128)S(1)} %get-tuple-element.44), channel_id=1, source_target_pairs={{0,2},{2,0},{4,6},{6,4},{8,10},{10,8},{12,14},{14,12},{16,18},{18,... | collective-permute-start | bytes 491528 | tf_op jit(solution)/shard_map/ppermute | solution.py:839
  3.7 10.6 %collective-permute-start.1 = (f32[160,256]{1,0:T(8,128)S(1)}, f32[160,256]{1,0:T(8,128)S(1)}, u32[]{:S(2)}, u32[]{:S(2)}) collective-permute-start(f32[160,256]{1,0:T(8,128)S(1)} %get-tuple-element.45), channel_id=1, source_target_pairs={{0,30},{2,4},{4,2},{6,8},{8,6},{10,12},{12,10},{14,16},{16,14},{18... | collective-permute-start | bytes 491528 | tf_op jit(solution)/shard_map/ppermute | solution.py:840
  11.9 2.4 %copy-start = (bf16[48,96]{1,0:T(8,128)(2,1)S(1)}, bf16[48,96]{1,0:T(8,128)(2,1)}, u32[]{:S(2)}) copy-start(bf16[48,96]{1,0:T(8,128)(2,1)} %constant.32.clone.herm_t) | copy-start | bytes 27652
  11.9 2.4 %copy-start.1 = (f32[1,39,8,256]{3,2,1,0:T(8,128)S(1)}, f32[1,39,8,256]{3,2,1,0:T(8,128)}, u32[]{:S(2)}) copy-start(f32[1,39,8,256]{3,2,1,0:T(8,128)} %param.11) | copy-start | bytes 958468
  18.0 2.6 %collective-permute-start.2 = (f32[144,256]{1,0:T(8,128)S(1)}, f32[144,256]{1,0:T(8,128)S(1)}, u32[]{:S(2)}, u32[]{:S(2)}) collective-permute-start(f32[144,256]{1,0:T(8,128)S(1)} %get-tuple-element.54), channel_id=1, source_target_pairs={{0,2},{2,0},{4,6},{6,4},{8,10},{10,8},{12,14},{14,12},{16,18},{18,... | collective-permute-start | bytes 442376 | tf_op jit(solution)/shard_map/ppermute | solution.py:888
  18.1 8.6 %collective-permute-start.3 = (f32[144,256]{1,0:T(8,128)S(1)}, f32[144,256]{1,0:T(8,128)S(1)}, u32[]{:S(2)}, u32[]{:S(2)}) collective-permute-start(f32[144,256]{1,0:T(8,128)S(1)} %get-tuple-element.55), channel_id=1, source_target_pairs={{0,30},{2,4},{4,2},{6,8},{8,6},{10,12},{12,10},{14,16},{16,14},{18... | collective-permute-start | bytes 442376 | tf_op jit(solution)/shard_map/ppermute | solution.py:889
  31.0 1.3 %collective-permute-start.4 = (f32[32,512]{1,0:T(8,128)S(1)}, f32[32,512]{1,0:T(8,128)S(1)}, u32[]{:S(2)}, u32[]{:S(2)}) collective-permute-start(f32[32,512]{1,0:T(8,128)S(1)} %constant_dynamic-slice_fusion), channel_id=1, source_target_pairs={{0,2},{1,3},{2,0},{3,1},{4,6},{5,7},{6,4},{7,5},{8,10},{9,11},{10,... | collective-permute-start | bytes 196616 | tf_op jit(solution)/shard_map/ppermute | solution.py:931
  32.3 5.6 %collective-permute-start.7 = (f32[32,512]{1,0:T(8,128)S(1)}, f32[32,512]{1,0:T(8,128)S(1)}, u32[]{:S(2)}, u32[]{:S(2)}) collective-permute-start(f32[32,512]{1,0:T(8,128)S(1)} %dynamic-slice_add_fusion), channel_id=1, source_target_pairs={{0,5},{1,4},{2,7},{3,6},{4,1},{5,0},{6,3},{7,2},{8,13},{9,12},{10,... | collective-permute-start | bytes 196616 | tf_op jit(solution)/shard_map/ppermute | solution.py:933
  32.9 5.1 %collective-permute-start.6 = (f32[32,512]{1,0:T(8,128)S(1)}, f32[32,512]{1,0:T(8,128)S(1)}, u32[]{:S(2)}, u32[]{:S(2)}) collective-permute-start(f32[32,512]{1,0:T(8,128)S(1)} %dynamic-slice_add_fusion), channel_id=1, source_target_pairs={{0,1},{1,0},{2,3},{3,2},{4,5},{5,4},{6,7},{7,6},{8,9},{9,8},{10,11... | collective-permute-start | bytes 196616 | tf_op jit(solution)/shard_map/ppermute | solution.py:933
  34.0 4.9 %collective-permute-start.5 = (f32[32,512]{1,0:T(8,128)S(1)}, f32[32,512]{1,0:T(8,128)S(1)}, u32[]{:S(2)}, u32[]{:S(2)}) collective-permute-start(f32[32,512]{1,0:T(8,128)S(1)} %dynamic-slice_add_fusion), channel_id=1, source_target_pairs={{0,4},{1,5},{2,6},{3,7},{4,0},{5,1},{6,2},{7,3},{8,12},{9,13},{10,... | collective-permute-start | bytes 196616 | tf_op jit(solution)/shard_map/ppermute | solution.py:933
  38.9 7.2 %collective-permute-start.10 = (f32[32,512]{1,0:T(8,128)S(1)}, f32[32,512]{1,0:T(8,128)S(1)}, u32[]{:S(2)}, u32[]{:S(2)}) collective-permute-start(f32[32,512]{1,0:T(8,128)S(1)} %add_add_fusion.1.after), channel_id=1, source_target_pairs={{0,16},{1,17},{2,18},{3,19},{4,20},{5,21},{6,22},{7,23},{8,24},{9,... | collective-permute-start | bytes 196616 | tf_op jit(solution)/shard_map/ppermute | solution.py:933
  39.0 7.1 %collective-permute-start.9 = (f32[32,512]{1,0:T(8,128)S(1)}, f32[32,512]{1,0:T(8,128)S(1)}, u32[]{:S(2)}, u32[]{:S(2)}) collective-permute-start(f32[32,512]{1,0:T(8,128)S(1)} %add_add_fusion.1.after), channel_id=1, source_target_pairs={{0,24},{1,25},{2,26},{3,27},{4,28},{5,29},{6,30},{7,31},{8,16},{9,... | collective-permute-start | bytes 196616 | tf_op jit(solution)/shard_map/ppermute | solution.py:933
  40.9 5.7 %collective-permute-start.8 = (f32[32,512]{1,0:T(8,128)S(1)}, f32[32,512]{1,0:T(8,128)S(1)}, u32[]{:S(2)}, u32[]{:S(2)}) collective-permute-start(f32[32,512]{1,0:T(8,128)S(1)} %add_add_fusion.1.after), channel_id=1, source_target_pairs={{0,8},{1,9},{2,10},{3,11},{4,12},{5,13},{6,14},{7,15},{8,0},{9,1},... | collective-permute-start | bytes 196616 | tf_op jit(solution)/shard_map/ppermute | solution.py:933
  46.6 1.3 %collective-permute-start.11 = (f32[32,512]{1,0:T(8,128)S(1)}, f32[32,512]{1,0:T(8,128)S(1)}, u32[]{:S(2)}, u32[]{:S(2)}) collective-permute-start(f32[32,512]{1,0:T(8,128)S(1)} %add_add_fusion.refs_1_), channel_id=1, source_target_pairs={{0,2},{1,3},{2,0},{3,1},{4,6},{5,7},{6,4},{7,5},{8,10},{9,11},{10,... | collective-permute-start | bytes 196616 | tf_op jit(solution)/shard_map/ppermute | solution.py:950

commit v6 on v5

--- a/solution.py
+++ b/solution.py
@@ -576,7 +576,7 @@
         if edge <= first + n < edge + depth:
             add_sums(acc, mb[n], da.at[n], gb[n], h.at[n])
 
-    staggered(last - first, act, back, finish, add)
+    staggered(last - first, act, lambda n: None, back, finish, add)
 
 
 def third_near_kernel(
@@ -592,7 +592,7 @@
     sources = (mb2_h, gb2_h, mb_near_h, h_near_h, mb_far_h, h_far_h, mb0_h, h0_h)
     targets = (mb2, gb2, mb_near, h_near, mb_far, h_far, mb0, h0)
     pairs = list(zip(sources, targets))
-    copies = [moves.start(source, target) for source, target in pairs[:2]]
+    copies = [moves.start(source, target) for source, target in pairs[:4]]
     acc[...] = jnp.zeros(acc.shape, F32)
 
     def stream(side):
@@ -603,7 +603,7 @@
     by_side(core, stream)
     for copy in copies[:2]:
         copy.wait()
-    copies += [moves.start(source, target) for source, target in pairs[2:4]]
+    copies += [moves.start(source, target) for source, target in pairs[4:]]
 
     def hide(z):
         hidden_into(h2.at[z], w1, mb2[z])
@@ -617,7 +617,6 @@
     staggered(depth, hide, act, add)
     for copy in copies[2:4]:
         copy.wait()
-    copies += [moves.start(source, target) for source, target in pairs[4:]]
 
     def run(side):
         first, last = near_layers(side, depth)

time: 48.8 us -> 48.7 us (level)
  no operation moved by 1% of the time
where the time goes in v6:
time: 48.7 us; the launch traced here: 48.5 us
  Pallas kernels  25.5 us (52%)
  starting transfers between devices  16.1 us (33%)
  waiting for transfers between devices  5.99 us (12%)
  between operations  0.85 us (2%)
    pallas_call x8, Pallas kernels, call(): pl.pallas_call(kernel, out_shape=[out[2](out[0], out[1]) if len(out) > 2...  25.5 us
    ppermute x2, starting transfers between devices, per_device(): off = lax.ppermute(send_off, 'space', next_chip)  8.22 us
    ppermute x6, starting transfers between devices, per_device(): lax.ppermute(mine, axes, pairs)  7.1 us
    ppermute x6, waiting for transfers between devices, per_device(): lax.ppermute(mine, axes, pairs)  3.51 us
    ppermute x1, waiting for transfers between devices, per_device(): other = lax.ppermute(mine, axes, swap)  1.24 us
    ppermute x1, waiting for transfers between devices, per_device(): mine = mine + lax.ppermute(other, axes, swap)  1.23 us
  transfers between devices with their start and end apart: 12, of which 6 were waited for; matrix products, arithmetic and copies ran while one was open for 0% of the time, Pallas kernels for 30%

profile of v6, /device:TPU:0, one launch (start us, length us, event | category | flops | bytes accessed | tf_op | source)
XLA Modules:
  0.0 48.5 jit_solution(11941251616130944299)
XLA Ops:
  0.6 2.5 %shard_map.128 = (f32[160,256]{1,0:T(8,128)S(1)}, f32[160,256]{1,0:T(8,128)S(1)}, f32[2,312,128]{2,1,0:T(8,128)S(1)}, bf16[8,32,256]{2,1,0:T(8,128)(2,1)}, bf16[...) custom-call(s32[1]{0:T(128)} %bitcast.core.refs_0_, bf16[20,512]{1,0:T(8,128)(2,1)} %w_in_h.3, ...), custom_call_target="tpu_custom_call" | custom-call | flops 1000000000 | bytes 2000000 | tf_op jit(solution)/shard_map/pallas_call | solution.py:733
  3.2 0.0 copy-start.2
  3.2 0.0 copy-start.3
  3.2 0.5 %collective-permute-start = (f32[160,256]{1,0:T(8,128)S(1)}, f32[160,256]{1,0:T(8,128)S(1)}, u32[]{:S(2)}, u32[]{:S(2)}) collective-permute-start(f32[160,256]{1,0:T(8,128)S(1)} %get-tuple-element.44), channel_id=1, source_target_pairs={{0,2},{2,0},{4,6},{6,4},{8,10},{10,8},{12,14},{14,12},{16,18},{18,... | collective-permute-start | bytes 491528 | tf_op jit(solution)/shard_map/ppermute | solution.py:838
  3.7 5.7 %collective-permute-start.1 = (f32[160,256]{1,0:T(8,128)S(1)}, f32[160,256]{1,0:T(8,128)S(1)}, u32[]{:S(2)}, u32[]{:S(2)}) collective-permute-start(f32[160,256]{1,0:T(8,128)S(1)} %get-tuple-element.45), channel_id=1, source_target_pairs={{0,30},{2,4},{4,2},{6,8},{8,6},{10,12},{12,10},{14,16},{16,14},{18... | collective-permute-start | bytes 491528 | tf_op jit(solution)/shard_map/ppermute | solution.py:839
  9.4 2.5 %shard_map.130 = (bf16[8,512,256]{2,1,0:T(8,128)(2,1)}, bf16[32,512]{1,0:T(8,128)(2,1)S(1)}, bf16[512,48]{1,0:T(8,128)(2,1)S(1)}) custom-call(bf16[20,512]{1,0:T(8,128)(2,1)} %w_in_h.3, bf16[39,512]{1,0:T(8,128)(2,1)} %bitcast.18, bf16[8,32,256]{2,1,0:T(8,128)(2,1)} %get-tuple-element.50.mb0_h, bf16[512,32]{1,0:T(8,128)(2,1)S(1)} %get-tuple-element.46.w1), custom_call_target="tpu_custom_call" | custom-call | flops 1000000000 | bytes 2000000 | tf_op jit(solution)/shard_map/pallas_call | solution.py:733
  11.9 0.0 copy-start
  11.9 0.0 copy-start.1
  11.9 0.0 collective-permute-done.on
  11.9 0.0 copy-done.2
  11.9 0.0 copy-done.3
  11.9 2.3 %shard_map.129 = (f32[2,624,128]{2,1,0:T(8,128)S(1)}, bf16[8,512,256]{2,1,0:T(8,128)(2,1)}, bf16[8,32,256]{2,1,0:T(8,128)(2,1)}) custom-call(s32[1]{0:T(128)} %bitcast.core.refs_0_, f32[2,312,128]{2,1,0:T(8,128)S(1)} %get-tuple-element.43.post, f32[160,256]{1,0:T(8,128)S(1)} %collective-permute-done.on, s32[8,256]{1,0:T(8,128)S(1)} %bitcast.14, ...), custom_call_target="tpu_custom_call" | custom-call | flops 1000000000 | bytes 2000000 | tf_op jit(solution)/shard_map/pallas_call | solution.py:733
  14.3 0.0 collective-permute-done.1.off
  14.3 0.0 copy-done
  14.3 0.0 copy-done.1
  14.3 3.7 %shard_map.131 = (f32[144,256]{1,0:T(8,128)S(1)}, f32[144,256]{1,0:T(8,128)S(1)}, f32[2,312,128]{2,1,0:T(8,128)S(1)}, f32[64,256]{1,0:T(8,128)S(1)}, bf16[6,512,...) custom-call(s32[1]{0:T(128)} %bitcast.core.refs_0_, ...), custom_call_target="tpu_custom_call" | custom-call | flops 1000000000 | bytes 2000000 | tf_op jit(solution)/shard_map/pallas_call | solution.py:733
  18.0 0.1 collective-permute-start.2
  18.1 2.6 %collective-permute-start.3 = (f32[144,256]{1,0:T(8,128)S(1)}, f32[144,256]{1,0:T(8,128)S(1)}, u32[]{:S(2)}, u32[]{:S(2)}) collective-permute-start(f32[144,256]{1,0:T(8,128)S(1)} %get-tuple-element.55), channel_id=1, source_target_pairs={{0,30},{2,4},{4,2},{6,8},{8,6},{10,12},{12,10},{14,16},{16,14},{18... | collective-permute-start | bytes 442376 | tf_op jit(solution)/shard_map/ppermute | solution.py:888
  20.7 0.0 collective-permute-done.2.on
  20.7 6.0 %shard_map.132 = (f32[2,624,128]{2,1,0:T(8,128)S(1)}, f32[2,624,128]{2,1,0:T(8,128)S(1)}, f32[80,512]{1,0:T(8,128)S(1)}, f32[48,256]{1,0:T(8,128)S(1)}, bf16[6,3...) custom-call(s32[1]{0:T(128)} %bitcast.core.refs_0_, ...), custom_call_target="tpu_custom_call" | custom-call | flops 1000000000 | bytes 2000000 | tf_op jit(solution)/shard_map/pallas_call | solution.py:733
  26.6 0.0 collective-permute-done.3.off
  26.7 4.2 %shard_map.133 = (f32[64,512]{1,0:T(8,128)S(1)}, bf16[8,512,256]{2,1,0:T(8,128)(2,1)}, f32[2,384,128]{2,1,0:T(8,128)}) custom-call(s32[1]{0:T(128)} %bitcast.core.refs_0_, f32[2,312,128]{2,1,0:T(8,128)S(1)} %get-tuple-element.53.g2, f32[144,256]{1,0:T(8,128)S(1)} %collective-permute-done.2.on, f32[144,256]{1,0:T(8,128)S(1)} %collective-permute-done.3.off, ...), custom_call_target="tpu_custom_call" | custom-call | flops 1000000000 | bytes 2000000 | tf_op jit(solution)/shard_map/pallas_call | solution.py:733
  30.9 0.1 collective-permute-start.4
  31.0 1.2 %collective-permute-done.4 = f32[32,512]{1,0:T(8,128)S(1)} collective-permute-done((f32[32,512]{1,0:T(8,128)S(1)}, f32[32,512]{1,0:T(8,128)S(1)}, u32[]{:S(2)}, u32[]{:S(2)}) %collective-permute-start.4) | collective-permute-done | bytes 65568 | tf_op jit(solution)/shard_map/ppermute | solution.py:930
  32.3 0.6 %collective-permute-start.7 = (f32[32,512]{1,0:T(8,128)S(1)}, f32[32,512]{1,0:T(8,128)S(1)}, u32[]{:S(2)}, u32[]{:S(2)}) collective-permute-start(f32[32,512]{1,0:T(8,128)S(1)} %dynamic-slice_add_fusion), channel_id=1, source_target_pairs={{0,5},{1,4},{2,7},{3,6},{4,1},{5,0},{6,3},{7,2},{8,13},{9,12},{10,... | collective-permute-start | bytes 196616 | tf_op jit(solution)/shard_map/ppermute | solution.py:932
  32.8 1.1 %collective-permute-start.6 = (f32[32,512]{1,0:T(8,128)S(1)}, f32[32,512]{1,0:T(8,128)S(1)}, u32[]{:S(2)}, u32[]{:S(2)}) collective-permute-start(f32[32,512]{1,0:T(8,128)S(1)} %dynamic-slice_add_fusion), channel_id=1, source_target_pairs={{0,1},{1,0},{2,3},{3,2},{4,5},{5,4},{6,7},{7,6},{8,9},{9,8},{10,11... | collective-permute-start | bytes 196616 | tf_op jit(solution)/shard_map/ppermute | solution.py:932
  33.9 1.9 %collective-permute-start.5 = (f32[32,512]{1,0:T(8,128)S(1)}, f32[32,512]{1,0:T(8,128)S(1)}, u32[]{:S(2)}, u32[]{:S(2)}) collective-permute-start(f32[32,512]{1,0:T(8,128)S(1)} %dynamic-slice_add_fusion), channel_id=1, source_target_pairs={{0,4},{1,5},{2,6},{3,7},{4,0},{5,1},{6,2},{7,3},{8,12},{9,13},{10,... | collective-permute-start | bytes 196616 | tf_op jit(solution)/shard_map/ppermute | solution.py:932
  35.8 2.1 %collective-permute-done.7 = f32[32,512]{1,0:T(8,128)S(1)} collective-permute-done((f32[32,512]{1,0:T(8,128)S(1)}, f32[32,512]{1,0:T(8,128)S(1)}, u32[]{:S(2)}, u32[]{:S(2)}) %collective-permute-start.7) | collective-permute-done | bytes 65568 | tf_op jit(solution)/shard_map/ppermute | solution.py:932
  37.9 0.0 collective-permute-done.6
  37.9 0.9 %collective-permute-done.5 = f32[32,512]{1,0:T(8,128)S(1)} collective-permute-done((f32[32,512]{1,0:T(8,128)S(1)}, f32[32,512]{1,0:T(8,128)S(1)}, u32[]{:S(2)}, u32[]{:S(2)}) %collective-permute-start.5) | collective-permute-done | bytes 65568 | tf_op jit(solution)/shard_map/ppermute | solution.py:932
  38.8 0.1 collective-permute-start.10
  38.9 1.9 %collective-permute-start.9 = (f32[32,512]{1,0:T(8,128)S(1)}, f32[32,512]{1,0:T(8,128)S(1)}, u32[]{:S(2)}, u32[]{:S(2)}) collective-permute-start(f32[32,512]{1,0:T(8,128)S(1)} %add_add_fusion.1.after), channel_id=1, source_target_pairs={{0,24},{1,25},{2,26},{3,27},{4,28},{5,29},{6,30},{7,31},{8,16},{9,... | collective-permute-start | bytes 196616 | tf_op jit(solution)/shard_map/ppermute | solution.py:932
  40.8 1.5 %collective-permute-start.8 = (f32[32,512]{1,0:T(8,128)S(1)}, f32[32,512]{1,0:T(8,128)S(1)}, u32[]{:S(2)}, u32[]{:S(2)}) collective-permute-start(f32[32,512]{1,0:T(8,128)S(1)} %add_add_fusion.1.after), channel_id=1, source_target_pairs={{0,8},{1,9},{2,10},{3,11},{4,12},{5,13},{6,14},{7,15},{8,0},{9,1},... | collective-permute-start | bytes 196616 | tf_op jit(solution)/shard_map/ppermute | solution.py:932
  42.4 3.6 %shard_map.134 = f32[312,256]{1,0:T(8,128)} custom-call(f32[32,512]{1,0:T(8,128)S(1)} %add_add_fusion.1.after, bf16[8,512,256]{2,1,0:T(8,128)(2,1)} %get-tuple-element.73.da0_h, f32[2,384,128]{2,1,0:T(8,128)} %get-tuple-element.74.gp0_h, bf16[32,512]{1,0:T(8,128)(2,1)S(1)} %get-tuple-element.51.w_in, bf16[48,96]{1,0:T(8,128)(2,1)S(1)} %copy-done), custom_call_target="tpu_custom_call" | custom-call | flops 1000000000 | bytes 2000000 | tf_op jit(solution)/shard_map/pallas_call | solution.py:733
  45.9 0.1 collective-permute-done.10
  46.0 0.0 collective-permute-done.9
  46.0 0.5 collective-permute-done.8
  46.5 0.1 collective-permute-start.11
  46.6 1.2 %collective-permute-done.11.refs_2_ = f32[32,512]{1,0:T(8,128)S(1)} collective-permute-done((f32[32,512]{1,0:T(8,128)S(1)}, f32[32,512]{1,0:T(8,128)S(1)}, u32[]{:S(2)}, u32[]{:S(2)}) %collective-permute-start.11) | collective-permute-done | bytes 65568 | tf_op jit(solution)/shard_map/ppermute | solution.py:949
  47.8 0.7 %shard_map.135 = (f32[20,512]{1,0:T(8,128)}, f32[1,512]{1,0:T(1,128)}, f32[39,512]{1,0:T(8,128)}, f32[1,39]{1,0:T(1,128)}) custom-call(s32[1]{0:T(128)} %bitcast.core.refs_0_, f32[32,512]{1,0:T(8,128)S(1)} %add_add_fusion.refs_1_, f32[32,512]{1,0:T(8,128)S(1)} %collective-permute-done.11.refs_2_), custom_call_target="tpu_custom_call" | custom-call | flops 1000000000 | bytes 2000000 | tf_op jit(solution)/shard_map/pallas_call | solution.py:733
  (4 shorter events, 0.1 us)
Async XLA Ops:
  3.2 8.8 %copy-start.2 = (s32[1,8,256]{2,1,0:T(8,128)S(1)}, s32[1,8,256]{2,1,0:T(8,128)}, u32[]{:S(2)}) copy-start(s32[1,8,256]{2,1,0:T(8,128)} %param.10) | copy-start | bytes 24580
  3.2 8.8 %copy-start.3 = (bf16[32,144]{1,0:T(8,128)(2,1)S(1)}, bf16[32,144]{1,0:T(8,128)(2,1)}, u32[]{:S(2)}) copy-start(bf16[32,144]{1,0:T(8,128)(2,1)} %constant.31.clone.herm_h.herm) | copy-start | bytes 27652
  3.2 8.7 %collective-permute-start = (f32[160,256]{1,0:T(8,128)S(1)}, f32[160,256]{1,0:T(8,128)S(1)}, u32[]{:S(2)}, u32[]{:S(2)}) collective-permute-start(f32[160,256]{1,0:T(8,128)S(1)} %get-tuple-element.44), channel_id=1, source_target_pairs={{0,2},{2,0},{4,6},{6,4},{8,10},{10,8},{12,14},{14,12},{16,18},{18,... | collective-permute-start | bytes 491528 | tf_op jit(solution)/shard_map/ppermute | solution.py:838
  3.7 10.6 %collective-permute-start.1 = (f32[160,256]{1,0:T(8,128)S(1)}, f32[160,256]{1,0:T(8,128)S(1)}, u32[]{:S(2)}, u32[]{:S(2)}) collective-permute-start(f32[160,256]{1,0:T(8,128)S(1)} %get-tuple-element.45), channel_id=1, source_target_pairs={{0,30},{2,4},{4,2},{6,8},{8,6},{10,12},{12,10},{14,16},{16,14},{18... | collective-permute-start | bytes 491528 | tf_op jit(solution)/shard_map/ppermute | solution.py:839
  11.9 2.4 %copy-start = (bf16[48,96]{1,0:T(8,128)(2,1)S(1)}, bf16[48,96]{1,0:T(8,128)(2,1)}, u32[]{:S(2)}) copy-start(bf16[48,96]{1,0:T(8,128)(2,1)} %constant.32.clone.herm_t) | copy-start | bytes 27652
  11.9 2.4 %copy-start.1 = (f32[1,39,8,256]{3,2,1,0:T(8,128)S(1)}, f32[1,39,8,256]{3,2,1,0:T(8,128)}, u32[]{:S(2)}) copy-start(f32[1,39,8,256]{3,2,1,0:T(8,128)} %param.11) | copy-start | bytes 958468
  18.0 2.6 %collective-permute-start.2 = (f32[144,256]{1,0:T(8,128)S(1)}, f32[144,256]{1,0:T(8,128)S(1)}, u32[]{:S(2)}, u32[]{:S(2)}) collective-permute-start(f32[144,256]{1,0:T(8,128)S(1)} %get-tuple-element.54), channel_id=1, source_target_pairs={{0,2},{2,0},{4,6},{6,4},{8,10},{10,8},{12,14},{14,12},{16,18},{18,... | collective-permute-start | bytes 442376 | tf_op jit(solution)/shard_map/ppermute | solution.py:887
  18.1 8.5 %collective-permute-start.3 = (f32[144,256]{1,0:T(8,128)S(1)}, f32[144,256]{1,0:T(8,128)S(1)}, u32[]{:S(2)}, u32[]{:S(2)}) collective-permute-start(f32[144,256]{1,0:T(8,128)S(1)} %get-tuple-element.55), channel_id=1, source_target_pairs={{0,30},{2,4},{4,2},{6,8},{8,6},{10,12},{12,10},{14,16},{16,14},{18... | collective-permute-start | bytes 442376 | tf_op jit(solution)/shard_map/ppermute | solution.py:888
  30.9 1.3 %collective-permute-start.4 = (f32[32,512]{1,0:T(8,128)S(1)}, f32[32,512]{1,0:T(8,128)S(1)}, u32[]{:S(2)}, u32[]{:S(2)}) collective-permute-start(f32[32,512]{1,0:T(8,128)S(1)} %constant_dynamic-slice_fusion), channel_id=1, source_target_pairs={{0,2},{1,3},{2,0},{3,1},{4,6},{5,7},{6,4},{7,5},{8,10},{9,11},{10,... | collective-permute-start | bytes 196616 | tf_op jit(solution)/shard_map/ppermute | solution.py:930
  32.3 5.6 %collective-permute-start.7 = (f32[32,512]{1,0:T(8,128)S(1)}, f32[32,512]{1,0:T(8,128)S(1)}, u32[]{:S(2)}, u32[]{:S(2)}) collective-permute-start(f32[32,512]{1,0:T(8,128)S(1)} %dynamic-slice_add_fusion), channel_id=1, source_target_pairs={{0,5},{1,4},{2,7},{3,6},{4,1},{5,0},{6,3},{7,2},{8,13},{9,12},{10,... | collective-permute-start | bytes 196616 | tf_op jit(solution)/shard_map/ppermute | solution.py:932
  32.8 5.1 %collective-permute-start.6 = (f32[32,512]{1,0:T(8,128)S(1)}, f32[32,512]{1,0:T(8,128)S(1)}, u32[]{:S(2)}, u32[]{:S(2)}) collective-permute-start(f32[32,512]{1,0:T(8,128)S(1)} %dynamic-slice_add_fusion), channel_id=1, source_target_pairs={{0,1},{1,0},{2,3},{3,2},{4,5},{5,4},{6,7},{7,6},{8,9},{9,8},{10,11... | collective-permute-start | bytes 196616 | tf_op jit(solution)/shard_map/ppermute | solution.py:932
  33.9 4.9 %collective-permute-start.5 = (f32[32,512]{1,0:T(8,128)S(1)}, f32[32,512]{1,0:T(8,128)S(1)}, u32[]{:S(2)}, u32[]{:S(2)}) collective-permute-start(f32[32,512]{1,0:T(8,128)S(1)} %dynamic-slice_add_fusion), channel_id=1, source_target_pairs={{0,4},{1,5},{2,6},{3,7},{4,0},{5,1},{6,2},{7,3},{8,12},{9,13},{10,... | collective-permute-start | bytes 196616 | tf_op jit(solution)/shard_map/ppermute | solution.py:932
  38.8 7.2 %collective-permute-start.10 = (f32[32,512]{1,0:T(8,128)S(1)}, f32[32,512]{1,0:T(8,128)S(1)}, u32[]{:S(2)}, u32[]{:S(2)}) collective-permute-start(f32[32,512]{1,0:T(8,128)S(1)} %add_add_fusion.1.after), channel_id=1, source_target_pairs={{0,16},{1,17},{2,18},{3,19},{4,20},{5,21},{6,22},{7,23},{8,24},{9,... | collective-permute-start | bytes 196616 | tf_op jit(solution)/shard_map/ppermute | solution.py:932
  38.9 7.1 %collective-permute-start.9 = (f32[32,512]{1,0:T(8,128)S(1)}, f32[32,512]{1,0:T(8,128)S(1)}, u32[]{:S(2)}, u32[]{:S(2)}) collective-permute-start(f32[32,512]{1,0:T(8,128)S(1)} %add_add_fusion.1.after), channel_id=1, source_target_pairs={{0,24},{1,25},{2,26},{3,27},{4,28},{5,29},{6,30},{7,31},{8,16},{9,... | collective-permute-start | bytes 196616 | tf_op jit(solution)/shard_map/ppermute | solution.py:932
  40.8 5.6 %collective-permute-start.8 = (f32[32,512]{1,0:T(8,128)S(1)}, f32[32,512]{1,0:T(8,128)S(1)}, u32[]{:S(2)}, u32[]{:S(2)}) collective-permute-start(f32[32,512]{1,0:T(8,128)S(1)} %add_add_fusion.1.after), channel_id=1, source_target_pairs={{0,8},{1,9},{2,10},{3,11},{4,12},{5,13},{6,14},{7,15},{8,0},{9,1},... | collective-permute-start | bytes 196616 | tf_op jit(solution)/shard_map/ppermute | solution.py:932
  46.5 1.3 %collective-permute-start.11 = (f32[32,512]{1,0:T(8,128)S(1)}, f32[32,512]{1,0:T(8,128)S(1)}, u32[]{:S(2)}, u32[]{:S(2)}) collective-permute-start(f32[32,512]{1,0:T(8,128)S(1)} %add_add_fusion.refs_1_), channel_id=1, source_target_pairs={{0,2},{1,3},{2,0},{3,1},{4,6},{5,7},{6,4},{7,5},{8,10},{9,11},{10,... | collective-permute-start | bytes 196616 | tf_op jit(solution)/shard_map/ppermute | solution.py:949
